TPU v7x, 512 devices: a whole 4x4x16 slice. The times are simulated.
512 devices in a mesh: regime: 8 (over y, core), obj: 64 (over x, z).
Axes of the slice: x: 4, y: 4, z: 16, core: 2. Of those that a mesh axis runs over, the one named last changes fastest.
Arguments:
- local_jac: bfloat16 [7, 245760], P(None, ('regime', 'obj')), may hold values from -6 to 6
- global_jac: bfloat16 [245760, 512], P(('regime', 'obj')), may hold values from -0.1331338 to 0.1331338
- coeff_index: int32 [4, 245760], P(None, ('regime', 'obj')), may hold values from 0 to 511
- coeff_weight: bfloat16 [4, 245760], P(None, ('regime', 'obj')), may hold values from -2.065591 to 2.065591
- residual: float32 [245760], P(('regime', 'obj')), may hold values from -10 to 10
- obs_weight: float32 [245760], P(('regime', 'obj')), may hold values from 0.3 to 3
- obs_count: int32 [4096], P(('regime', 'obj')), may hold values from 1 to 60
- local_prior: float32 [7, 4096], P(None, ('regime', 'obj')), may hold values from 0.3 to 3
- regional_prior: float32 [8, 512], P('regime'), may hold values from 0.1 to 1
- global_prior: float32 [512], replicated, may hold values from 0.3 to 3
Outputs:
- local_step: float32 [7, 4096], P(None, ('regime', 'obj'))
- regional_step: float32 [8, 512], P('regime')
- global_step: float32 [512], replicated
All inputs are finite; a program needn't handle non-finite values.
Results may differ from a plain program's by a relative error of at most 0.0005.
The roundings to bfloat16 on the way count: a program that leaves them out, or rounds other values in their place, can miss the bound.
Values sent between devices are 32-bit elements; how exact they have to be, the bound alone decides.
No kernel may reach another device: no remote copies, remote signals or barrier semaphores. Data moves between devices by JAX's collectives and lax.ppermute only.
A program may use at most 64 MiB of HBM per device.

v0:
```python
import jax
import jax.numpy as jnp
from jax import lax
from jax.sharding import PartitionSpec as P


def live_weight(obs_weight, obs_count, observed):
    objects = obs_count.shape[0]
    position = jnp.arange(observed, dtype=jnp.int32)
    present = (position[None, :] < obs_count[:, None]).reshape(objects * observed)
    return (jnp.where(present, obs_weight, jnp.float32(0.0)), present)


def jacobian(coeff_index, coeff_weight, global_jac, regional_width):
    columns = jnp.arange(regional_width, dtype=jnp.int32)
    regional = jnp.zeros((coeff_index.shape[1], regional_width), jnp.float32)
    for k in range(coeff_index.shape[0]):
        regional = regional + jnp.where(
            coeff_index[k][:, None] == columns[None, :],
            coeff_weight[k][:, None].astype(jnp.float32),
            jnp.float32(0.0),
        )
    return jnp.concatenate([regional.astype(jnp.bfloat16), global_jac], axis=1)


def cholesky_small(entries):
    order = len(entries)
    factor = [[None] * order for i in range(order)]
    for j in range(order):
        diagonal = entries[j][j]
        for k in range(j):
            diagonal = diagonal - factor[j][k] * factor[j][k]
        factor[j][j] = jnp.sqrt(diagonal)
        for i in range(j + 1, order):
            current = entries[i][j]
            for k in range(j):
                current = current - factor[i][k] * factor[j][k]
            factor[i][j] = current / factor[j][j]
    return factor


def broaden(entry, like):
    return entry.reshape(entry.shape + (1,) * (like.ndim - 1))


def forward_small(factor, target):
    result = []
    for a in range(len(target)):
        current = target[a]
        for k in range(a):
            current = current - broaden(factor[a][k], current) * result[k]
        result.append(current / broaden(factor[a][a], current))
    return result


def backward_small(factor, target):
    order = len(target)
    result = [None] * order
    for a in reversed(range(order)):
        current = target[a]
        for k in range(a + 1, order):
            current = current - broaden(factor[k][a], current) * result[k]
        result[a] = current / broaden(factor[a][a], current)
    return result


def cho_apply(factor, target):
    return jax.scipy.linalg.cho_solve((factor, True), target)


def body(
    local_jac,
    global_jac,
    coeff_index,
    coeff_weight,
    residual,
    obs_weight,
    obs_count,
    local_prior,
    regional_prior,
    global_prior,
):
    objects = obs_count.shape[0]
    observed = local_jac.shape[1] // objects
    nparams = local_jac.shape[0]
    regional_width = regional_prior.shape[1]
    weight, present = live_weight(obs_weight, obs_count, observed)
    misfit, counted = lax.psum(
        (jnp.sum(weight * residual * residual), jnp.sum(present.astype(jnp.float32))),
        ("regime", "obj"),
    )
    damping = misfit / counted
    joined = jacobian(coeff_index, coeff_weight, global_jac, regional_width)
    scaled = (joined.astype(jnp.float32) * weight[:, None]).astype(jnp.bfloat16)
    normal = jnp.dot(scaled.T, joined, preferred_element_type=jnp.float32)
    gradient = jnp.dot(residual, scaled.astype(jnp.float32), precision=lax.Precision.HIGHEST)
    local_rows = local_jac.astype(jnp.float32).reshape(nparams, objects, observed)
    weighted_local = local_rows * weight.reshape(objects, observed)[None]
    small_normal = jnp.einsum(
        "anp,bnp->abn", weighted_local, local_rows, precision=lax.Precision.HIGHEST
    )
    entries = [
        [small_normal[a, b] + (local_prior[a] if a == b else 0.0) for b in range(nparams)]
        for a in range(nparams)
    ]
    factor = cholesky_small(entries)
    coupling = jnp.einsum(
        "anp,npc->anc",
        weighted_local,
        joined.reshape(objects, observed, -1).astype(jnp.float32),
        precision=lax.Precision.HIGHEST,
    )
    local_gradient = jnp.sum(weighted_local * residual.reshape(objects, observed)[None], axis=2)
    reduced = forward_small(factor, [coupling[a] for a in range(nparams)])
    reduced_gradient = forward_small(factor, [local_gradient[a] for a in range(nparams)])
    stacked = jnp.concatenate(reduced, axis=0)
    vector = jnp.concatenate(reduced_gradient, axis=0)
    schur = normal - jnp.dot(stacked.T, stacked, precision=lax.Precision.HIGHEST)
    rhs = gradient - jnp.dot(vector, stacked, precision=lax.Precision.HIGHEST)
    regional_block, block, global_block, rhs_regional, rhs_global = lax.psum(
        (
            schur[:regional_width, :regional_width],
            schur[:regional_width, regional_width:],
            schur[regional_width:, regional_width:],
            rhs[:regional_width],
            rhs[regional_width:],
        ),
        "obj",
    )
    regional_factor = jnp.linalg.cholesky(regional_block + damping * jnp.diag(regional_prior[0]))
    coupled = cho_apply(regional_factor, block)
    shifted = cho_apply(regional_factor, rhs_regional)
    group_matrix = global_block - jnp.dot(block.T, coupled, precision=lax.Precision.HIGHEST)
    group_vector = rhs_global - jnp.dot(shifted, block, precision=lax.Precision.HIGHEST)
    global_matrix, global_vector = lax.psum((group_matrix, group_vector), "regime")
    global_factor = jnp.linalg.cholesky(global_matrix + damping * jnp.diag(global_prior))
    global_step = cho_apply(global_factor, global_vector)
    regional_step = cho_apply(
        regional_factor, rhs_regional - jnp.dot(block, global_step, precision=lax.Precision.HIGHEST)
    )
    update = jnp.concatenate([regional_step, global_step], axis=0)
    moved = jnp.dot(joined.astype(jnp.float32), update, precision=lax.Precision.HIGHEST)
    target = jnp.sum(weighted_local * (residual - moved).reshape(objects, observed)[None], axis=2)
    solved = backward_small(factor, forward_small(factor, [target[a] for a in range(nparams)]))
    local_step = jnp.stack(solved, axis=0)
    return (local_step, regional_step[None, :], global_step)


def solution(mesh):
    return jax.shard_map(
        body,
        mesh=mesh,
        in_specs=(
            P(None, ("regime", "obj")),
            P(("regime", "obj"), None),
            P(None, ("regime", "obj")),
            P(None, ("regime", "obj")),
            P(("regime", "obj")),
            P(("regime", "obj")),
            P(("regime", "obj")),
            P(None, ("regime", "obj")),
            P("regime", None),
            P(),
        ),
        out_specs=(P(None, ("regime", "obj")), P("regime", None), P()),
        check_vma=False,
    )
```

profile of v0, /device:TPU:1, one launch (start us, length us, event | category | flops | bytes accessed | tf_op | source)
XLA Modules:
  0.0 742.4 jit_solution(18203108806637925098)
XLA Ops:
  8.0 1.3 fusion.163
  15.2 1.1 pad_maximum_fusion
  18.4 3.5 fusion.289
  21.9 1.4 convolution_subtract_fusion
  23.3 1.8 fusion.283
  26.5 112.3 %all-reduce.1 = (f32[]{:T(128)}, f32[]{:T(128)}) all-reduce(f32[]{:T(128)} %get-tuple-element.214, f32[]{:T(128)} %convert_reduce_fusion), channel_id=1, replica_groups=mesh['regime'=8,'obj'=64] {'regime','obj'}, use_global_device_ids=true, to_apply=%region_2.3 | all-reduce | flops 2 | bytes 16 | tf_op jit(solution)/shard_map/psum | solution.py:88
  146.3 111.7 %all-reduce.2 = (f32[512]{0:T(512)S(1)}, f32[512]{0:T(512)S(1)}) all-reduce(f32[512]{0:T(512)S(1)} %get-tuple-element.333, f32[512]{0:T(512)S(1)} %get-tuple-element.332), channel_id=1, replica_groups=mesh['regime'=8,'obj'=64] {'obj'}, use_global_device_ids=true, to_apply=%region_18.20 | all-reduce | flops 1024 | bytes 8192 | tf_op jit(solution)/shard_map/psum | solution.py:120
  258.9 48.3 %all-reduce.9.cloned.1.call-done = (f32[512,512]{0,1:T(8,128)}, f32[512,512]{0,1:T(8,128)}, f32[512,512]{0,1:T(8,128)}) async-done(((f32[512,512]{0,1:T(8,128)}, f32[512,512]{0,1:T(8,128)}, f32[512,512]{0,1:T(8,128)}), (f32[512,512]{0,1:T(8,128)}, f32[512,512]{0,1:T(8,128)}, f32[512,512]{0,1:T(8,128)})) %all-reduce.9.cloned.1.call-update) | async-done | bytes 3145744 | tf_op jit(solution)/shard_map/psum | solution.py:120
  307.2 2.4 multiply_add_fusion.1
  309.6 1.6 copy.200
  312.4 11.7 %cholesky.286 = f32[128,128]{1,0:T(8,128)S(1)} custom-call(f32[128,128]{1,0:T(8,128)S(1)} %cholesky.426), custom_call_target="Cholesky" | custom-call | tf_op jit(solution)/shard_map/jit(cholesky)/cholesky | solution.py:130
  324.2 9.8 %custom-call.38 = f32[1,128,128]{1,2,0:T(8,128)S(1)} custom-call(f32[1,128,128]{2,1,0:T(8,128)S(1)} %get-tuple-element.288), custom_call_target="InvertDiagBlocksLowerTriangular" | custom-call | tf_op jit(solution)/shard_map/jit(cholesky)/cholesky | solution.py:130
  334.0 1.2 fusion.74
  335.2 1.3 convolution_subtract_fusion.9
  336.5 11.7 %cholesky.305 = f32[128,128]{1,0:T(8,128)S(1)} custom-call(f32[128,128]{1,0:T(8,128)S(1)} %cholesky.430), custom_call_target="Cholesky" | custom-call | tf_op jit(solution)/shard_map/jit(cholesky)/cholesky | solution.py:130
  348.6 10.2 %custom-call.39 = f32[1,128,128]{1,2,0:T(8,128)S(1)} custom-call(f32[1,128,128]{2,1,0:T(8,128)S(1)} %get-tuple-element.286), custom_call_target="InvertDiagBlocksLowerTriangular" | custom-call | tf_op jit(solution)/shard_map/jit(cholesky)/cholesky | solution.py:130
  359.3 1.5 convolution_subtract_fusion.11
  360.8 11.7 %cholesky.326 = f32[128,128]{1,0:T(8,128)S(1)} custom-call(f32[128,128]{1,0:T(8,128)S(1)} %cholesky.435), custom_call_target="Cholesky" | custom-call | tf_op jit(solution)/shard_map/jit(cholesky)/cholesky | solution.py:130
  372.6 9.8 %custom-call.40 = f32[1,128,128]{1,2,0:T(8,128)S(1)} custom-call(f32[1,128,128]{2,1,0:T(8,128)S(1)} %get-tuple-element.284), custom_call_target="InvertDiagBlocksLowerTriangular" | custom-call | tf_op jit(solution)/shard_map/jit(cholesky)/cholesky | solution.py:130
  382.7 1.3 convolution_subtract_fusion.13
  384.1 11.9 %cholesky.343 = f32[128,128]{1,0:T(8,128)S(1)} custom-call(f32[128,128]{1,0:T(8,128)S(1)} %convolution_subtract_fusion.13), custom_call_target="Cholesky" | custom-call | tf_op jit(solution)/shard_map/jit(cholesky)/cholesky | solution.py:130
  401.1 1.4 select_select_fusion.1
  402.6 8.3 %while.8 = (s32[]{:T(128)}, f32[512,512]{0,1:T(8,128)S(1)}, s32[4,2]{0,1:T(2,128)S(1)}, f32[4,128,128]{2,1,0:T(8,128)S(1)}, s32[]{:T(128)}) while((s32[]{:T(128)}, f32[512,512]{0,1:T(8,128)S(1)}, s32[4,2]{0,1:T(2,128)S(1)}, f32[4,128,128]{2,1,0:T(8,128)S(1)}, s32[]{:T(128)}) %tuple.279), condition=%wide.while_cond.clone.1, body=%wide.while_body.clone.1.sunk | while | flops 2 | bytes 393321 | solution.py:68
  403.3 1.3 dynamic-slice.20
  405.3 1.3 dynamic-slice.20
  407.4 1.3 dynamic-slice.20
  409.5 1.3 dynamic-slice.20
  411.7 40.1 %custom-call.46 = f32[4,128,128]{1,2,0:T(8,128)S(1)} custom-call(f32[4,128,128]{2,1,0:T(8,128)} %copy-done.6), custom_call_target="InvertDiagBlocksLowerTriangular" | custom-call | tf_op jit(solution)/shard_map/jit(_cho_solve)/triangular_solve | solution.py:68
  454.7 1.5 convolution_subtract_fusion.7
  459.5 3.0 convolution_subtract_fusion.1
  466.5 22.1 %psum.71 = f32[512]{0:T(512)} all-reduce(f32[512]{0:T(512)S(1)} %sub.2291), channel_id=1, replica_groups=mesh['regime'=8,'obj'=64] {'regime'}, use_global_device_ids=true, to_apply=%region_19.22 | all-reduce | flops 512 | bytes 4096 | tf_op jit(solution)/shard_map/psum | solution.py:135
  488.6 54.5 %all-reduce.7.cloned.1.call-done = f32[512,512]{0,1:T(8,128)} async-done(((f32[512,512]{0,1:T(8,128)}), f32[512,512]{0,1:T(8,128)}) %all-reduce.7.cloned.1.call-update) | async-done | bytes 1048592 | tf_op jit(solution)/shard_map/psum | solution.py:135
  543.1 2.3 multiply_add_fusion
  545.4 2.6 copy.214
  548.0 1.8 fusion.44
  550.8 11.7 %cholesky.358 = f32[128,128]{1,0:T(8,128)S(1)} custom-call(f32[128,128]{1,0:T(8,128)S(1)} %cholesky.439), custom_call_target="Cholesky" | custom-call | tf_op jit(solution)/shard_map/jit(cholesky)/cholesky | solution.py:136
  563.1 1.2 cholesky.384
  564.3 9.8 %custom-call.41 = f32[1,128,128]{1,2,0:T(8,128)S(1)} custom-call(f32[1,128,128]{2,1,0:T(8,128)S(1)} %get-tuple-element.282), custom_call_target="InvertDiagBlocksLowerTriangular" | custom-call | tf_op jit(solution)/shard_map/jit(cholesky)/cholesky | solution.py:136
  574.1 2.0 constant_dynamic-update-slice_fusion.9
  576.1 1.2 convolution_subtract_fusion.8
  577.9 13.2 %cholesky.377 = f32[128,128]{1,0:T(8,128)} custom-call(f32[128,128]{1,0:T(8,128)} %cholesky.443), custom_call_target="Cholesky" | custom-call | tf_op jit(solution)/shard_map/jit(cholesky)/cholesky | solution.py:136
  591.1 1.5 select_reduce_fusion.2
  593.3 1.4 compare_reduce_fusion.3
  594.7 11.4 %custom-call.42 = f32[1,128,128]{1,2,0:T(8,128)} custom-call(f32[1,128,128]{2,1,0:T(8,128)} %get-tuple-element.279), custom_call_target="InvertDiagBlocksLowerTriangular" | custom-call | tf_op jit(solution)/shard_map/jit(cholesky)/cholesky | solution.py:136
  606.1 1.8 convolution_dynamic-update-slice_fusion
  607.9 1.4 convolution_subtract_fusion.10
  609.9 13.2 %cholesky.398 = f32[128,128]{1,0:T(8,128)} custom-call(f32[128,128]{1,0:T(8,128)} %cholesky.448), custom_call_target="Cholesky" | custom-call | tf_op jit(solution)/shard_map/jit(cholesky)/cholesky | solution.py:136
  623.1 1.5 select_reduce_fusion.1
  625.3 11.3 %custom-call.43 = f32[1,128,128]{1,2,0:T(8,128)} custom-call(f32[1,128,128]{2,1,0:T(8,128)} %get-tuple-element.276), custom_call_target="InvertDiagBlocksLowerTriangular" | custom-call | tf_op jit(solution)/shard_map/jit(cholesky)/cholesky | solution.py:136
  636.6 1.7 convolution_dynamic-update-slice_fusion.2
  638.2 1.4 convolution_subtract_fusion.12
  639.7 11.9 %cholesky.415 = f32[128,128]{1,0:T(8,128)S(1)} custom-call(f32[128,128]{1,0:T(8,128)S(1)} %convolution_subtract_fusion.12), custom_call_target="Cholesky" | custom-call | tf_op jit(solution)/shard_map/jit(cholesky)/cholesky | solution.py:136
  655.4 2.4 select_select_fusion
  658.5 13.9 %while.7 = (s32[]{:T(128)}, f32[512,512]{1,0:T(8,128)}, s32[4,2]{0,1:T(2,128)S(1)}, f32[4,128,128]{2,1,0:T(8,128)}, s32[]{:T(128)}) while((s32[]{:T(128)}, f32[512,512]{1,0:T(8,128)}, s32[4,2]{0,1:T(2,128)S(1)}, f32[4,128,128]{2,1,0:T(8,128)}, s32[]{:T(128)}) %tuple.290), condition=%wide.while_cond.clone, body=%wide.while_body.clone.sunk | while | flops 2 | bytes 132705 | solution.py:68
  659.1 2.9 bitcast_dynamic-update-slice_fusion.4
  662.6 2.9 bitcast_dynamic-update-slice_fusion.4
  666.1 2.9 bitcast_dynamic-update-slice_fusion.4
  669.6 2.8 bitcast_dynamic-update-slice_fusion.4
  672.5 40.7 %custom-call.45 = f32[4,128,128]{1,2,0:T(8,128)} custom-call(f32[4,128,128]{2,1,0:T(8,128)} %get-tuple-element.34), custom_call_target="InvertDiagBlocksLowerTriangular" | custom-call | tf_op jit(solution)/shard_map/jit(_cho_solve)/triangular_solve | solution.py:68
  716.3 1.1 fusion.21
  718.4 1.2 fusion.32
  719.6 1.1 convolution_bitcast_fusion.17
  723.8 1.1 fusion.22
  726.2 1.2 fusion.30
  (290 shorter events, 60.5 us)
Async XLA Ops:
  7.2 300.0 %all-reduce.9.cloned.1.call-start = ((), (), s32[]{:S(2)}) async-start(), calls=%async_computation.1 | async-start | bytes 6291456 | tf_op jit(solution)/shard_map/psum | solution.py:120
  9.4 7.2 copy-start.7
  16.4 0.9 copy-start.51
  25.1 0.7 copy-start.55
  25.1 120.5 %copy-start.14 = (f32[480]{0:T(512)S(1)}, f32[480]{0:T(512)}, u32[]{:S(2)}) copy-start(f32[480]{0:T(512)} %param.17) | copy-start | bytes 5764
  25.1 282.0 %copy-start.53 = (f32[1,512]{1,0:T(1,128)S(1)}, f32[1,512]{1,0:T(1,128)}, u32[]{:S(2)}) copy-start(f32[1,512]{1,0:T(1,128)} %param.21) | copy-start | bytes 6148
  25.2 517.9 %all-reduce.7.cloned.1.call-start = ((), (), s32[]{:S(2)}) async-start(), calls=%async_computation | async-start | bytes 2097152 | tf_op jit(solution)/shard_map/psum | solution.py:135
  258.0 205.4 %copy-start.11 = (f32[512]{0:T(512)}, f32[512]{0:T(512)S(1)}, u32[]{:S(2)}) copy-start(f32[512]{0:T(512)S(1)} %get-tuple-element.159) | copy-start | bytes 6148
  307.2 4.0 copy-start.2
  311.4 1.0 copy-start.4
  398.7 1.9 copy-start.1
  401.1 50.6 %copy-start = (f32[512,512]{0,1:T(8,128)S(1)}, f32[512,512]{0,1:T(8,128)}, u32[]{:S(2)}) copy-start(f32[512,512]{0,1:T(8,128)} %get-tuple-element.161) | copy-start | bytes 3145732
  410.9 0.7 copy-start.6
  411.6 44.5 %copy-start.9 = (s32[4,2]{0,1:T(2,128)}, s32[4,2]{0,1:T(2,128)S(1)}, u32[]{:S(2)}) copy-start(s32[4,2]{0,1:T(2,128)S(1)} %get-tuple-element.491) | copy-start | bytes 100
  457.7 1.8 copy-start.5
  462.5 80.6 %copy-start.54 = (f32[512]{0:T(512)S(1)}, f32[512]{0:T(512)}, u32[]{:S(2)}) copy-start(f32[512]{0:T(512)} %param.22) | copy-start | bytes 6148
  549.8 1.0 copy-start.3
  607.9 50.6 %copy-start.10 = (s32[4,2]{0,1:T(2,128)S(1)}, s32[4,2]{0,1:T(2,128)}, u32[]{:S(2)}) copy-start(s32[4,2]{0,1:T(2,128)} %copy-done.9) | copy-start | bytes 100
  624.6 88.6 %copy-start.13 = (f32[512]{0:T(512)S(1)}, f32[512]{0:T(512)}, u32[]{:S(2)}) copy-start(f32[512]{0:T(512)} %psum.71) | copy-start | bytes 6148
  657.8 71.4 %copy-start.12 = (f32[512]{0:T(512)S(1)}, f32[512]{0:T(512)}, u32[]{:S(2)}) copy-start(f32[512]{0:T(512)} %copy-done.11) | copy-start | bytes 6148
  722.7 10.9 %copy-start.15 = (f32[480]{0:T(512)S(1)}, f32[480]{0:T(512)}, u32[]{:S(2)}) copy-start(f32[480]{0:T(512)} %param.17) | copy-start | bytes 5764
  723.8 10.0 %copy-start.8 = (f32[8,60]{1,0:T(8,128)S(1)}, f32[8,60]{1,0:T(8,128)}, u32[]{:S(2)}) copy-start(f32[8,60]{1,0:T(8,128)} %copy-done.7) | copy-start | bytes 5764
  724.9 8.9 %copy-start.16 = (f32[1,1,8]{1,0,2:T(1,128)S(1)}, f32[1,1,8]{1,0,2:T(1,128)}, u32[]{:S(2)}) copy-start(f32[1,1,8]{1,0,2:T(1,128)} %get-tuple-element.296) | copy-start | bytes 100
  724.9 9.0 %copy-start.17 = (f32[1,1,8]{1,0,2:T(1,128)S(1)}, f32[1,1,8]{1,0,2:T(1,128)}, u32[]{:S(2)}) copy-start(f32[1,1,8]{1,0,2:T(1,128)} %get-tuple-element.297) | copy-start | bytes 100
  724.9 9.0 %copy-start.18 = (f32[1,1,8]{1,0,2:T(1,128)S(1)}, f32[1,1,8]{1,0,2:T(1,128)}, u32[]{:S(2)}) copy-start(f32[1,1,8]{1,0,2:T(1,128)} %get-tuple-element.298) | copy-start | bytes 100
  724.9 9.0 %copy-start.19 = (f32[1,1,8]{1,0,2:T(1,128)S(1)}, f32[1,1,8]{1,0,2:T(1,128)}, u32[]{:S(2)}) copy-start(f32[1,1,8]{1,0,2:T(1,128)} %get-tuple-element.299) | copy-start | bytes 100
  724.9 9.0 %copy-start.20 = (f32[1,1,8]{1,0,2:T(1,128)S(1)}, f32[1,1,8]{1,0,2:T(1,128)}, u32[]{:S(2)}) copy-start(f32[1,1,8]{1,0,2:T(1,128)} %get-tuple-element.300) | copy-start | bytes 100
  725.0 9.0 %copy-start.21 = (f32[1,1,8]{1,0,2:T(1,128)S(1)}, f32[1,1,8]{1,0,2:T(1,128)}, u32[]{:S(2)}) copy-start(f32[1,1,8]{1,0,2:T(1,128)} %get-tuple-element.301) | copy-start | bytes 100
  725.0 9.0 %copy-start.22 = (f32[1,1,8]{1,0,2:T(1,128)S(1)}, f32[1,1,8]{1,0,2:T(1,128)}, u32[]{:S(2)}) copy-start(f32[1,1,8]{1,0,2:T(1,128)} %get-tuple-element.302) | copy-start | bytes 100
  725.0 9.0 %copy-start.23 = (f32[1,1,8]{1,0,2:T(1,128)S(1)}, f32[1,1,8]{1,0,2:T(1,128)}, u32[]{:S(2)}) copy-start(f32[1,1,8]{1,0,2:T(1,128)} %get-tuple-element.303) | copy-start | bytes 100
  725.0 9.0 %copy-start.24 = (f32[1,1,8]{1,0,2:T(1,128)S(1)}, f32[1,1,8]{1,0,2:T(1,128)}, u32[]{:S(2)}) copy-start(f32[1,1,8]{1,0,2:T(1,128)} %get-tuple-element.304) | copy-start | bytes 100
  725.0 9.0 %copy-start.25 = (f32[1,1,8]{1,0,2:T(1,128)S(1)}, f32[1,1,8]{1,0,2:T(1,128)}, u32[]{:S(2)}) copy-start(f32[1,1,8]{1,0,2:T(1,128)} %get-tuple-element.305) | copy-start | bytes 100
  725.0 9.0 %copy-start.26 = (f32[1,1,8]{1,0,2:T(1,128)S(1)}, f32[1,1,8]{1,0,2:T(1,128)}, u32[]{:S(2)}) copy-start(f32[1,1,8]{1,0,2:T(1,128)} %get-tuple-element.306) | copy-start | bytes 100
  725.0 9.0 %copy-start.27 = (f32[1,1,8]{1,0,2:T(1,128)S(1)}, f32[1,1,8]{1,0,2:T(1,128)}, u32[]{:S(2)}) copy-start(f32[1,1,8]{1,0,2:T(1,128)} %get-tuple-element.307) | copy-start | bytes 100
  725.0 9.0 %copy-start.28 = (f32[1,1,8]{1,0,2:T(1,128)S(1)}, f32[1,1,8]{1,0,2:T(1,128)}, u32[]{:S(2)}) copy-start(f32[1,1,8]{1,0,2:T(1,128)} %get-tuple-element.308) | copy-start | bytes 100
  725.0 9.0 %copy-start.29 = (f32[1,1,8]{1,0,2:T(1,128)S(1)}, f32[1,1,8]{1,0,2:T(1,128)}, u32[]{:S(2)}) copy-start(f32[1,1,8]{1,0,2:T(1,128)} %get-tuple-element.309) | copy-start | bytes 100
  725.0 9.0 %copy-start.30 = (f32[1,1,8]{1,0,2:T(1,128)S(1)}, f32[1,1,8]{1,0,2:T(1,128)}, u32[]{:S(2)}) copy-start(f32[1,1,8]{1,0,2:T(1,128)} %get-tuple-element.310) | copy-start | bytes 100
  725.1 9.0 %copy-start.31 = (f32[1,1,8]{1,0,2:T(1,128)S(1)}, f32[1,1,8]{1,0,2:T(1,128)}, u32[]{:S(2)}) copy-start(f32[1,1,8]{1,0,2:T(1,128)} %get-tuple-element.311) | copy-start | bytes 100
  725.1 9.0 %copy-start.32 = (f32[1,1,8]{1,0,2:T(1,128)S(1)}, f32[1,1,8]{1,0,2:T(1,128)}, u32[]{:S(2)}) copy-start(f32[1,1,8]{1,0,2:T(1,128)} %get-tuple-element.312) | copy-start | bytes 100
  725.1 9.0 %copy-start.33 = (f32[1,1,8]{1,0,2:T(1,128)S(1)}, f32[1,1,8]{1,0,2:T(1,128)}, u32[]{:S(2)}) copy-start(f32[1,1,8]{1,0,2:T(1,128)} %get-tuple-element.313) | copy-start | bytes 100
  725.1 9.0 %copy-start.34 = (f32[1,1,8]{1,0,2:T(1,128)S(1)}, f32[1,1,8]{1,0,2:T(1,128)}, u32[]{:S(2)}) copy-start(f32[1,1,8]{1,0,2:T(1,128)} %get-tuple-element.314) | copy-start | bytes 100
  725.1 9.0 %copy-start.35 = (f32[1,1,8]{1,0,2:T(1,128)S(1)}, f32[1,1,8]{1,0,2:T(1,128)}, u32[]{:S(2)}) copy-start(f32[1,1,8]{1,0,2:T(1,128)} %get-tuple-element.315) | copy-start | bytes 100
  725.1 9.0 %copy-start.36 = (f32[1,1,8]{1,0,2:T(1,128)S(1)}, f32[1,1,8]{1,0,2:T(1,128)}, u32[]{:S(2)}) copy-start(f32[1,1,8]{1,0,2:T(1,128)} %slice.477) | copy-start | bytes 100
  725.1 9.0 %copy-start.37 = (f32[1,8]{0,1:T(8,128)S(1)}, f32[1,8]{0,1:T(8,128)}, u32[]{:S(2)}) copy-start(f32[1,8]{0,1:T(8,128)} %copy.256) | copy-start | bytes 100
  725.1 9.0 %copy-start.38 = (f32[1,8]{0,1:T(8,128)S(1)}, f32[1,8]{0,1:T(8,128)}, u32[]{:S(2)}) copy-start(f32[1,8]{0,1:T(8,128)} %copy.258) | copy-start | bytes 100
  725.1 9.0 %copy-start.39 = (f32[1,8]{0,1:T(8,128)S(1)}, f32[1,8]{0,1:T(8,128)}, u32[]{:S(2)}) copy-start(f32[1,8]{0,1:T(8,128)} %copy.260) | copy-start | bytes 100
  725.1 9.0 %copy-start.40 = (f32[1,8]{0,1:T(8,128)S(1)}, f32[1,8]{0,1:T(8,128)}, u32[]{:S(2)}) copy-start(f32[1,8]{0,1:T(8,128)} %copy.262) | copy-start | bytes 100
  725.2 9.0 %copy-start.41 = (f32[1,8]{0,1:T(8,128)S(1)}, f32[1,8]{0,1:T(8,128)}, u32[]{:S(2)}) copy-start(f32[1,8]{0,1:T(8,128)} %copy.264) | copy-start | bytes 100
  725.2 9.0 %copy-start.42 = (f32[1,8]{0,1:T(8,128)S(1)}, f32[1,8]{0,1:T(8,128)}, u32[]{:S(2)}) copy-start(f32[1,8]{0,1:T(8,128)} %copy.266) | copy-start | bytes 100
  727.4 6.9 copy-start.44
  727.4 6.9 copy-start.45
  727.4 6.9 copy-start.46
  727.4 6.9 copy-start.47
  727.4 6.9 copy-start.48
  727.4 6.9 copy-start.49
  728.5 5.9 copy-start.43
  728.5 5.9 copy-start.50
  732.8 2.5 copy-start.52
Sparse Core Ops, SparseCore 0:
  25.3 281.8 all-reduce.8
  462.7 80.3 all-reduce.6
where the time goes:
time: 752 us; the launch traced here: 742 us
  other arithmetic  269 us (36%)
  blocking collectives  246 us (33%)
  waiting for transfers between devices  103 us (14%)
  matrix products  55.8 us (7%)
  local copies, waits for them, and re-layouts  46.9 us (6%)
  between operations  21.9 us (3%)
    psum x1, blocking collectives, body(): lax.psum((jnp.sum(weight * residual * residual), jnp.sum(present.astype(j...  112 us
    psum x1, blocking collectives, body(): lax.psum((schur[:regional_width, :regional_width], schur[:regional_width,...  112 us
    another operation x15, other arithmetic, body(): jnp.linalg.cholesky(global_matrix + damping * jnp.diag(global_prior))  90.1 us
    another operation x7, other arithmetic, cho_apply(): return jax.scipy.linalg.cho_solve((factor, True), target)  84.7 us
    another operation x15, other arithmetic, body(): jnp.linalg.cholesky(regional_block + damping * jnp.diag(regional_prior[0]))  79.5 us
    psum x1, waiting for transfers between devices, body(): lax.psum((group_matrix, group_vector), 'regime')  54.5 us
    psum x1, waiting for transfers between devices, body(): lax.psum((schur[:regional_width, :regional_width], schur[:regional_width,...  48.3 us
    another operation x56, matrix products, cho_apply(): return jax.scipy.linalg.cho_solve((factor, True), target)  28.3 us
  transfers between devices with their start and end apart: 2, of which 2 were waited for; matrix products, arithmetic and copies ran while one was open for 2% of the time, Pallas kernels for 0%

commit v1 on v0

v1 whole, which is shorter than its diff:
```python
import jax
import jax.numpy as jnp
from jax import lax
from jax.experimental import pallas as pl
from jax.experimental.pallas import tpu as pltpu
from jax.sharding import Mesh, PartitionSpec as P

f32 = jnp.float32
bf16 = jnp.bfloat16
HIGHEST = lax.Precision.HIGHEST

NB = 128
NBLK = 4
PAIRS = [(i, j) for i in range(NBLK) for j in range(i, NBLK)]
SLOT = {pair: at for at, pair in enumerate(PAIRS)}
TRI = len(PAIRS) * NB
REG_PARTS = 8
PART = TRI // REG_PARTS
PART_ROWS = PART + 8
MAIN_ROWS = 1536
SUM_AT = TRI + 8
CHUNK = 48
RPAD = 64

LAYERS = ("x", "z")
GROUPS = ("y", "core")


def tn(a, b, precision=None):
    return lax.dot_general(
        a, b, (((0,), (0,)), ((), ())), precision=precision, preferred_element_type=f32
    )


def nt(a, b, precision=None):
    return lax.dot_general(
        a, b, (((1,), (1,)), ((), ())), precision=precision, preferred_element_type=f32
    )


def nn(a, b, precision=None):
    return jnp.dot(a, b, precision=precision, preferred_element_type=f32)


def pieces(value):
    first = value.astype(bf16)
    rest = value - first.astype(f32)
    second = rest.astype(bf16)
    third = (rest - second.astype(f32)).astype(bf16)
    return first, second, third


def cholesky_small(entries):
    order = len(entries)
    factor = [[None] * order for i in range(order)]
    for j in range(order):
        diagonal = entries[j][j]
        for k in range(j):
            diagonal = diagonal - factor[j][k] * factor[j][k]
        factor[j][j] = jnp.sqrt(diagonal)
        for i in range(j + 1, order):
            current = entries[i][j]
            for k in range(j):
                current = current - factor[i][k] * factor[j][k]
            factor[i][j] = current / factor[j][j]
    return factor


def forward_small(factor, target):
    result = []
    for a in range(len(target)):
        current = target[a]
        for k in range(a):
            current = current - factor[a][k] * result[k]
        result.append(current / factor[a][a])
    return result


def backward_small(factor, target):
    order = len(target)
    result = [None] * order
    for a in reversed(range(order)):
        current = target[a]
        for k in range(a + 1, order):
            current = current - factor[k][a] * result[k]
        result[a] = current / factor[a][a]
    return result


def store_split(ref, slot, block):
    done = 0
    while done < NB:
        flat = slot * NB + done
        part, off = flat // PART, flat % PART
        take = min(NB - done, PART - off)
        start = part * PART_ROWS + off
        ref[start : start + take, :] = block[done : done + take]
        done += take


def assemble_kernel(
    lj_ref, gj_ref, ci_ref, cw_ref, res_ref, ow_ref, cnt_ref, lp_ref,
    gg_ref, main_ref, rg_ref, red_ref, aux_ref,
    left, right, padded,
):
    rows = gj_ref.shape[0]
    nparams = lj_ref.shape[0]
    objects = 8
    observed = rows // objects
    width = gj_ref.shape[1]
    res = res_ref[...]
    position = lax.broadcasted_iota(jnp.int32, (objects, rows), 1)
    owner = lax.broadcasted_iota(jnp.int32, (objects, rows), 0)
    count = jnp.zeros((objects, rows), jnp.int32)
    for n in range(objects):
        count = jnp.where(owner == n, cnt_ref[n], count)
    local = position - owner * observed
    present = (local >= 0) & (local < observed) & (local < count)
    live = jnp.where(present, jnp.broadcast_to(ow_ref[...], (objects, rows)), 0.0)
    weight = jnp.sum(live, axis=0, keepdims=True)
    misfit = jnp.sum(weight * res * res, axis=1, keepdims=True)
    counted = jnp.sum(
        jnp.sum(jnp.where(present, 1.0, 0.0), axis=0, keepdims=True), axis=1, keepdims=True
    )

    padded[...] = jnp.zeros_like(padded)
    padded[0:1, :rows] = weight
    padded[1:5, :rows] = ci_ref[...].astype(f32)
    padded[5:9, :rows] = cw_ref[...].astype(f32)
    for block in range(padded.shape[1] // NB):
        columns = padded[:, block * NB : (block + 1) * NB].T
        low = block * NB
        while low < min((block + 1) * NB, rows):
            high = min(low + 32, rows)
            here = columns[low - block * NB : high - block * NB]
            weights = here[:, 0:1]
            lanes = lax.broadcasted_iota(jnp.int32, (high - low, width), 1).astype(f32)
            total = jnp.zeros((high - low, width), f32)
            for k in range(4):
                total = total + jnp.where(here[:, 1 + k : 2 + k] == lanes, here[:, 5 + k : 6 + k], 0.0)
            joined = total.astype(bf16)
            for at, value in ((0, joined), (width, gj_ref[low:high, :])):
                scaled = (value.astype(f32) * weights).astype(bf16)
                right[low:high, at : at + width] = value
                right[rows + low : rows + high, at : at + width] = scaled
                left[low:high, at : at + width] = (scaled.astype(f32) * 0.5).astype(bf16)
                left[rows + low : rows + high, at : at + width] = (value.astype(f32) * 0.5).astype(bf16)
            low = high

    jac = lj_ref[...].astype(f32)
    weighted = [jac[a : a + 1, :] * live for a in range(nparams)]
    entries = [[None] * nparams for a in range(nparams)]
    owner8 = lax.broadcasted_iota(jnp.int32, (objects, objects), 0)
    lane8 = lax.broadcasted_iota(jnp.int32, (objects, objects), 1)
    for a in range(nparams):
        for b in range(a + 1):
            value = jnp.sum(weighted[a] * jac[b : b + 1, :], axis=1, keepdims=True)
            if a == b:
                prior = jnp.broadcast_to(lp_ref[a : a + 1, :], (objects, objects))
                value = value + jnp.sum(jnp.where(owner8 == lane8, prior, 0.0), axis=1, keepdims=True)
            entries[a][b] = value
    factor = cholesky_small(entries)
    local_gradient = [jnp.sum(weighted[a] * res, axis=1, keepdims=True) for a in range(nparams)]
    reduced_gradient = forward_small(factor, local_gradient)

    blank = jnp.zeros((8, rows), f32)
    stacked = jnp.concatenate(weighted + [blank], axis=0)
    everything = right[0:rows, :]
    coupling = None
    for piece in pieces(stacked):
        term = nn(piece, everything)
        coupling = term if coupling is None else coupling + term
    reduced = forward_small(factor, [coupling[8 * a : 8 * a + 8] for a in range(nparams)])
    joint = jnp.concatenate(reduced + [jnp.zeros((8, 2 * width), f32)], axis=0)
    red_ref[...] = joint
    r0, r1, r2 = pieces(joint)
    base = 2 * rows
    for at, (one, two) in enumerate(((r0, r0), (r0, r1), (r1, r0), (r1, r1), (r0, r2), (r2, r0))):
        left[base + at * RPAD : base + (at + 1) * RPAD, :] = -one
        right[base + at * RPAD : base + (at + 1) * RPAD, :] = two

    lane = lax.broadcasted_iota(jnp.int32, (objects, NB), 1)
    aux = jnp.zeros((objects, NB), f32)
    at = 0
    for a in range(nparams):
        for b in range(a + 1):
            aux = jnp.where(lane == at, factor[a][b], aux)
            at += 1
    for a in range(nparams):
        aux = jnp.where(lane == at, reduced_gradient[a], aux)
        at += 1
    aux_ref[...] = aux

    first, second, third = pieces(res)
    lhs = jnp.concatenate(
        [first.astype(f32), second.astype(f32), third.astype(f32), jnp.zeros((13, rows), f32)], axis=0
    ).astype(bf16)
    gradient = jnp.sum(nn(lhs, right[rows : 2 * rows, :]), axis=0, keepdims=True)
    for a in range(nparams):
        gradient = gradient - jnp.sum(reduced_gradient[a] * reduced[a], axis=0, keepdims=True)
    for at in range(8):
        main_ref[TRI + at : TRI + at + 1, :] = gradient[:, at * NB : (at + 1) * NB]

    row_lane = lax.broadcasted_iota(jnp.int32, (8, NB), 1)
    scalars = jnp.where(row_lane == 0, misfit, jnp.where(row_lane == 1, counted, 0.0))
    for part in range(REG_PARTS):
        gg_ref[part * PART_ROWS + PART : (part + 1) * PART_ROWS, :] = scalars
    for i in range(NBLK):
        for half in range(2):
            at = half * width
            value = tn(left[:, at + i * NB : at + (i + 1) * NB], right[:, at + i * NB : at + width])
            for j in range(i, NBLK):
                block = value[:, (j - i) * NB : (j - i + 1) * NB]
                slot = SLOT[i, j]
                if half == 0:
                    main_ref[slot * NB : (slot + 1) * NB, :] = block
                else:
                    store_split(gg_ref, slot, block)
        value = 2.0 * tn(left[0:rows, i * NB : (i + 1) * NB], right[0:rows, width:]) + tn(
            left[base:, i * NB : (i + 1) * NB], right[base:, width:]
        )
        for c in range(NBLK):
            rg_ref[c * width + i * NB : c * width + (i + 1) * NB, :] = value[:, c * NB : (c + 1) * NB]


def lane_take(value, at):
    return jnp.take_along_axis(value, jnp.full(value.shape, at, jnp.int32), axis=1)


def spread(value, at):
    return jnp.broadcast_to(value[at : at + 1], (8, NB))


def tree(terms):
    terms = list(terms)
    while len(terms) > 1:
        paired = [terms[a] + terms[a + 1] for a in range(0, len(terms) - 1, 2)]
        terms = paired + ([terms[-1]] if len(terms) % 2 else [])
    return terms[0]


def reciprocal(value):
    guess = pltpu.reciprocal(value, approx=True)
    guess = guess * (2.0 - value * guess)
    return guess * (2.0 - value * guess)


def invert_block(ref):
    lane = lax.broadcasted_iota(jnp.int32, (8, NB), 1)
    sub = lax.broadcasted_iota(jnp.int32, (8, NB), 0)

    def group(g, carry):
        base = pl.multiple_of(8 * g, 8)
        panel = ref[pl.ds(base, 8), :]
        columns = [lane_take(panel, base + i) for i in range(8)]
        e = [[None] * 8 for i in range(8)]
        for i in range(8):
            for j in range(i, 8):
                e[i][j] = spread(columns[j], i)

        def get(i, j):
            return e[min(i, j)][max(i, j)]

        for k in range(0, 8, 2):
            a, b, c = e[k][k], e[k][k + 1], e[k + 1][k + 1]
            q = reciprocal(a * c - b * b)
            pa, pb, pc = c * q, -(b * q), a * q
            others = [i for i in range(8) if i not in (k, k + 1)]
            c0 = {i: get(i, k) for i in others}
            c1 = {i: get(i, k + 1) for i in others}
            s0 = {i: c0[i] * pa + c1[i] * pb for i in others}
            s1 = {i: c0[i] * pb + c1[i] * pc for i in others}
            for at, i in enumerate(others):
                for j in others[at:]:
                    e[i][j] = e[i][j] - s0[i] * c0[j] - s1[i] * c1[j]
            for i in others:
                e[min(i, k)][max(i, k)] = s0[i]
                e[min(i, k + 1)][max(i, k + 1)] = s1[i]
            e[k][k], e[k][k + 1], e[k + 1][k + 1] = -pa, -pb, -pc

        inside = (lane >= base) & (lane < base + 8)
        source = [
            jnp.where(inside, jnp.where(lane == base + i, 1.0, 0.0), spread(panel, i)) for i in range(8)
        ]
        rows = [tree([get(i, j) * source[j] for j in range(8)]) for i in range(8)]
        for t in range(NB // 8):
            tile = ref[8 * t : 8 * t + 8, :]
            terms = [jnp.where(inside, 0.0, tile)]
            terms = terms + [lane_take(tile, base + i) * rows[i] for i in range(8)]
            ref[8 * t : 8 * t + 8, :] = tree(terms)
        last = rows[7]
        for i in range(7):
            last = jnp.where(sub == i, rows[i], last)
        ref[pl.ds(base, 8), :] = -last
        return carry

    lax.fori_loop(0, NB // 8, group, 0)


def damped(block, damping, profile):
    row = lax.broadcasted_iota(jnp.int32, (NB, NB), 0)
    col = lax.broadcasted_iota(jnp.int32, (NB, NB), 1)
    return block + jnp.where(row == col, damping * profile, 0.0)


def factor_steps(tri, inv, ratio, vec, solved):
    for p in range(NBLK):
        slot = SLOT[p, p]
        inv[...] = tri[slot * NB : (slot + 1) * NB, :]
        invert_block(inv)
        pivot = inv[...]
        tri[slot * NB : (slot + 1) * NB, :] = pivot
        solved[p] = nn(vec[p], pivot, HIGHEST)
        if p + 1 < NBLK:
            others = range(p + 1, NBLK)
            block = jnp.concatenate([tri[SLOT[p, j] * NB : (SLOT[p, j] + 1) * NB, :] for j in others], axis=1)
            scaled = nn(pivot, block, HIGHEST)
            for j in others:
                at = SLOT[p, j] * NB
                ratio[at : at + NB, :] = scaled[:, (j - p - 1) * NB : (j - p) * NB]
            step = nn(solved[p], block, HIGHEST)
            for i in others:
                off = (i - p - 1) * NB
                change = tn(block[:, off : off + NB], scaled[:, off:], HIGHEST)
                for j in range(i, NBLK):
                    at = SLOT[i, j] * NB
                    tri[at : at + NB, :] = tri[at : at + NB, :] - change[:, (j - i) * NB : (j - i + 1) * NB]
                vec[i] = vec[i] - step[:, off : off + NB]


def regional_kernel(main_ref, prior_ref, tri_ref, ratio_ref, solved_ref, inv, vec):
    scal = main_ref[SUM_AT + PART : SUM_AT + PART + 8, :]
    damping = scal[0:1, 0:1] / scal[0:1, 1:2]
    tri_ref[...] = main_ref[0:TRI, :]
    for p in range(NBLK):
        slot = SLOT[p, p]
        profile = prior_ref[0:1, p * NB : (p + 1) * NB]
        tri_ref[slot * NB : (slot + 1) * NB, :] = damped(
            tri_ref[slot * NB : (slot + 1) * NB, :], damping, profile
        )
        vec[p] = jnp.broadcast_to(main_ref[TRI + p : TRI + p + 1, :], (8, NB))
    ratio_ref[...] = jnp.zeros_like(ratio_ref)
    factor_steps(tri_ref, inv, ratio_ref, vec, solved_ref)


def coupling_kernel(main_ref, rg_ref, tri_ref, ratio_ref, solved_ref, out_ref, gb_ref, b, t, v):
    width = NBLK * NB
    for c in range(NBLK):
        b[:, c * NB : (c + 1) * NB] = rg_ref[c * width : (c + 1) * width, :]
        v[:, c * NB : (c + 1) * NB] = jnp.broadcast_to(
            main_ref[TRI + NBLK + c : TRI + NBLK + c + 1, :], (8, NB)
        )
    t[...] = jnp.zeros_like(t)
    for p in range(NBLK):
        here = b[p * NB : (p + 1) * NB, :]
        slot = SLOT[p, p]
        scaled = nn(tri_ref[slot * NB : (slot + 1) * NB, :], here, HIGHEST)
        gb_ref[p * NB : (p + 1) * NB, :] = scaled
        v[...] = v[...] - nn(solved_ref[p], here, HIGHEST)
        for i in range(p + 1, NBLK):
            at = SLOT[p, i] * NB
            b[i * NB : (i + 1) * NB, :] = b[i * NB : (i + 1) * NB, :] - tn(
                tri_ref[at : at + NB, :], scaled, HIGHEST
            )
        for i in range(NBLK):
            rows = slice(i * NB, (i + 1) * NB)
            t[rows, i * NB :] = t[rows, i * NB :] + tn(here[:, i * NB : (i + 1) * NB], scaled[:, i * NB :], HIGHEST)
    for (i, j), slot in SLOT.items():
        store_split(out_ref, slot, t[i * NB : (i + 1) * NB, j * NB : (j + 1) * NB])
    sub = lax.broadcasted_iota(jnp.int32, (8, NB), 0)
    tail = jnp.zeros((8, NB), f32)
    for c in range(NBLK):
        tail = jnp.where(sub == c, v[:, c * NB : (c + 1) * NB], tail)
    for part in range(REG_PARTS):
        out_ref[part * PART_ROWS + PART : (part + 1) * PART_ROWS, :] = tail


def finish_kernel(
    g_ref, v_ref, main_ref, prior_ref, ratio_ref, solved_ref, gb_ref, red_ref, aux_ref,
    local_ref, regional_ref, global_ref,
    tri, inv, gratio, vec, gsolved,
):
    nparams = local_ref.shape[0]
    width = NBLK * NB
    scal = main_ref[SUM_AT + PART : SUM_AT + PART + 8, :]
    damping = scal[0:1, 0:1] / scal[0:1, 1:2]
    tri[...] = g_ref[...]
    for p in range(NBLK):
        slot = SLOT[p, p]
        profile = prior_ref[0:1, p * NB : (p + 1) * NB]
        tri[slot * NB : (slot + 1) * NB, :] = damped(tri[slot * NB : (slot + 1) * NB, :], damping, profile)
        vec[p] = jnp.broadcast_to(v_ref[p : p + 1, :], (8, NB))
    factor_steps(tri, inv, gratio, vec, gsolved)

    def back(ratio, start):
        found = [None] * NBLK
        for p in reversed(range(NBLK)):
            current = start[p]
            for j in range(p + 1, NBLK):
                at = SLOT[p, j] * NB
                current = current - nt(found[j], ratio[at : at + NB, :], HIGHEST)
            found[p] = current
        return found

    global_step = jnp.concatenate(back(gratio, [gsolved[p] for p in range(NBLK)]), axis=1)
    moved = nt(global_step, gb_ref[...], HIGHEST)
    regional = back(
        ratio_ref, [solved_ref[p] - moved[:, p * NB : (p + 1) * NB] for p in range(NBLK)]
    )
    regional_step = jnp.concatenate(regional, axis=1)
    regional_ref[...] = regional_step[0:1, :]
    global_ref[...] = global_step[0:1, :]

    aux = aux_ref[...]
    at = 0
    factor = [[None] * nparams for a in range(nparams)]
    for a in range(nparams):
        for c in range(a + 1):
            factor[a][c] = aux[:, at : at + 1]
            at += 1
    update = jnp.concatenate([regional_step, global_step], axis=1)
    target = []
    for a in range(nparams):
        target.append(
            aux[:, at : at + 1] - jnp.sum(red_ref[8 * a : 8 * a + 8, :] * update, axis=1, keepdims=True)
        )
        at += 1
    found = backward_small(factor, target)
    sub = lax.broadcasted_iota(jnp.int32, (8, 8), 0)
    lane = lax.broadcasted_iota(jnp.int32, (8, 8), 1)
    for a in range(nparams):
        local_ref[a : a + 1, :] = jnp.sum(jnp.where(sub == lane, found[a], 0.0), axis=0, keepdims=True)


def shape(*dims, dtype=f32):
    return jax.ShapeDtypeStruct(dims, dtype)


VMEM = pl.BlockSpec(memory_space=pltpu.VMEM)
SMEM = pl.BlockSpec(memory_space=pltpu.SMEM)


def call(kernel, out_shape, scratch, specs, flops):
    return pl.pallas_call(
        kernel,
        out_shape=out_shape,
        in_specs=specs,
        out_specs=[VMEM] * len(out_shape),
        scratch_shapes=scratch,
        name=kernel.__name__,
        compiler_params=pltpu.CompilerParams(vmem_limit_bytes=40 * 1024 * 1024),
        cost_estimate=pl.CostEstimate(flops=flops, bytes_accessed=4_000_000, transcendentals=0),
    )


def part_sums(value, axis, parts):
    moved = lax.all_to_all(value, axis, 0, 0, tiled=True)
    return jnp.sum(moved.reshape((parts, value.shape[0] // parts) + value.shape[1:]), axis=0)


def sum_layers(value, nx, nz):
    piece = part_sums(value, "x", nx)
    piece = part_sums(piece, "z", nz)
    copies = jnp.broadcast_to(piece[None], (nz,) + piece.shape).reshape((-1,) + piece.shape[1:])
    whole = lax.all_to_all(copies, "z", 0, 0, tiled=True)
    return lax.all_gather(whole, "x", axis=0, tiled=True)


def body(
    local_jac,
    global_jac,
    coeff_index,
    coeff_weight,
    residual,
    obs_weight,
    obs_count,
    local_prior,
    regional_prior,
    global_prior,
):
    nx, nz = lax.axis_size("x"), lax.axis_size("z")
    rows = residual.shape[0]
    nparams = local_jac.shape[0]
    width = global_jac.shape[1]
    stack = 2 * rows + 6 * RPAD
    gg, main, rg, red, aux = call(
        assemble_kernel,
        [
            shape(REG_PARTS * PART_ROWS, NB),
            shape(SUM_AT, NB),
            shape(NBLK * width, NB),
            shape(RPAD, 2 * width),
            shape(8, NB),
        ],
        [
            pltpu.VMEM((stack, 2 * width), bf16),
            pltpu.VMEM((stack, 2 * width), bf16),
            pltpu.VMEM((NB, 512), f32),
        ],
        [VMEM, VMEM, VMEM, VMEM, VMEM, VMEM, SMEM, VMEM],
        2_000_000_000,
    )(
        local_jac, global_jac, coeff_index, coeff_weight, residual[None], obs_weight[None],
        obs_count, local_prior,
    )
    share = part_sums(gg, GROUPS, REG_PARTS)
    main = jnp.concatenate([main, share, jnp.zeros((MAIN_ROWS - SUM_AT - PART_ROWS, NB), f32)], axis=0)
    main = sum_layers(main, nx, nz)
    rg = sum_layers(rg, nx, nz)
    tri, ratio, solved = call(
        regional_kernel,
        [shape(TRI, NB), shape(TRI, NB), shape(NBLK, 8, NB)],
        [pltpu.VMEM((NB, NB), f32), pltpu.VMEM((NBLK, 8, NB), f32)],
        [VMEM, VMEM],
        20_000_000_000,
    )(main, regional_prior)
    outer, gb = call(
        coupling_kernel,
        [shape(REG_PARTS * PART_ROWS, NB), shape(width, width)],
        [pltpu.VMEM((width, width), f32), pltpu.VMEM((width, width), f32), pltpu.VMEM((8, width), f32)],
        [VMEM] * 5,
        4_000_000_000,
    )(main, rg, tri, ratio, solved)
    outer = part_sums(outer, GROUPS, REG_PARTS)
    mine = main[SUM_AT : SUM_AT + PART] - outer[:PART]
    matrix = lax.all_gather(mine, GROUPS, axis=0, tiled=True)
    local_step, regional_step, global_step = call(
        finish_kernel,
        [shape(nparams, 8), shape(1, width), shape(1, width)],
        [
            pltpu.VMEM((TRI, NB), f32),
            pltpu.VMEM((NB, NB), f32),
            pltpu.VMEM((TRI, NB), f32),
            pltpu.VMEM((NBLK, 8, NB), f32),
            pltpu.VMEM((NBLK, 8, NB), f32),
        ],
        [VMEM] * 9,
        20_000_000_000,
    )(matrix, outer[PART:], main, global_prior[None], ratio, solved, gb, red, aux)
    return local_step, regional_step, global_step[0]


def solution(mesh):
    devices = mesh.devices.reshape(4, 2, 4, 16)
    split = Mesh(devices, ("y", "core", "x", "z"))
    both = GROUPS + LAYERS
    return jax.shard_map(
        body,
        mesh=split,
        in_specs=(
            P(None, both),
            P(both, None),
            P(None, both),
            P(None, both),
            P(both),
            P(both),
            P(both),
            P(None, both),
            P(GROUPS, None),
            P(),
        ),
        out_specs=(P(None, both), P(GROUPS, None), P()),
        check_vma=False,
    )
```

time: 752 us -> 275 us (0.37); the launches traced: 742 us -> 274 us
  other arithmetic: 269 us -> 1.89 us
  blocking collectives: 246 us -> 60.3 us
  Pallas kernels: 0 us -> 78.2 us
  matrix products: 55.8 us -> 0 us
  starting transfers between devices: 0.08 us -> 48.8 us
  waiting for transfers between devices: 103 us -> 61.5 us
  local copies, waits for them, and re-layouts: 46.9 us -> 9.26 us
  between operations: 21.9 us -> 14.2 us
    another operation x37 -> x0, other arithmetic: 254 us -> none  [the longest x15 90.1 us: body(): jnp.linalg.cholesky(global_matrix + damping * jnp.diag(global_prior))]
    psum x3 -> x0, blocking collectives: 246 us -> none  [the longest x1 112 us: body(): lax.psum((jnp.sum(weight * residual * residual), jnp.sum(present.astype(j...]
    psum x2 -> x0, waiting for transfers between devices: 103 us -> none  [the longest x1 54.5 us: body(): lax.psum((group_matrix, group_vector), 'regime')]
    pallas_call x0 -> x4, Pallas kernels: none -> 78.2 us  [the longest x1 36 us: body(): call(finish_kernel, [shape(nparams, 8), shape(1, width), shape(1, width)]...]
    all_to_all x0 -> x6, waiting for transfers between devices: none -> 60.8 us  [the longest x4 48 us: part_sums(): moved = lax.all_to_all(value, axis, 0, 0, tiled=True)]
    all_to_all x0 -> x6, starting transfers between devices: none -> 48.7 us  [the longest x4 32.2 us: part_sums(): moved = lax.all_to_all(value, axis, 0, 0, tiled=True)]
    another operation x68 -> x0, matrix products: 43.8 us -> none  [the longest x56 28.3 us: cho_apply(): return jax.scipy.linalg.cho_solve((factor, True), target)]
    all_to_all x0 -> x2, blocking collectives: none -> 33.8 us  [part_sums(): moved = lax.all_to_all(value, axis, 0, 0, tiled=True)]
  transfers between devices with their start and end apart: 2 -> 7, of which waited for: 2 -> 7; matrix products, arithmetic and copies ran while one was open for 2% -> 1% of each run, Pallas kernels for 0% -> 11%
where the time goes in v1:
time: 275 us; the launch traced here: 274 us
  Pallas kernels  78.2 us (28%)
  waiting for transfers between devices  61.5 us (22%)
  blocking collectives  60.3 us (22%)
  starting transfers between devices  48.8 us (18%)
  between operations  14.2 us (5%)
  local copies, waits for them, and re-layouts  9.26 us (3%)
    all_to_all x4, waiting for transfers between devices, part_sums(): moved = lax.all_to_all(value, axis, 0, 0, tiled=True)  48 us
    pallas_call x1, Pallas kernels, body(): call(finish_kernel, [shape(nparams, 8), shape(1, width), shape(1, width)]...  36 us
    all_to_all x2, blocking collectives, part_sums(): moved = lax.all_to_all(value, axis, 0, 0, tiled=True)  33.8 us
    all_to_all x4, starting transfers between devices, part_sums(): moved = lax.all_to_all(value, axis, 0, 0, tiled=True)  32.2 us
    pallas_call x1, Pallas kernels, body(): call(regional_kernel, [shape(TRI, NB), shape(TRI, NB), shape(NBLK, 8, NB)...  31.4 us
    all_to_all x2, starting transfers between devices, sum_layers(): whole = lax.all_to_all(copies, 'z', 0, 0, tiled=True)  16.6 us
    all_gather x1, blocking collectives, body(): matrix = lax.all_gather(mine, GROUPS, axis=0, tiled=True)  14.2 us
    all_to_all x2, waiting for transfers between devices, sum_layers(): whole = lax.all_to_all(copies, 'z', 0, 0, tiled=True)  12.8 us
  transfers between devices with their start and end apart: 7, of which 7 were waited for; matrix products, arithmetic and copies ran while one was open for 1% of the time, Pallas kernels for 11%

profile of v1, /device:TPU:1, one launch (start us, length us, event | category | flops | bytes accessed | tf_op | source)
XLA Modules:
  0.0 274.1 jit_solution(8590901108224477906)
XLA Ops:
  7.2 0.0 copy-start.6
  7.2 0.0 copy-start.10
  7.2 0.7 copy-done.6
  7.8 0.0 copy-done.10
  7.9 0.0 copy-start.1
  7.9 1.0 copy-done.1
  8.9 0.0 copy-start.2
  8.9 0.7 copy-done.2
  9.6 0.0 copy-start.3
  9.6 0.7 copy-done.3
  10.3 0.0 copy-start.4
  10.3 0.7 copy-done.4
  11.0 0.0 copy-start.5
  11.0 0.7 copy-done.5
  11.7 0.0 copy-start.7
  11.7 0.7 copy-done.7
  12.3 5.9 %assemble_kernel.1 = (f32[1344,128]{1,0:T(8,128)}, f32[1288,128]{1,0:T(8,128)S(1)}, f32[2048,128]{1,0:T(8,128)}, f32[64,1024]{1,0:T(8,128)S(1)}, f32[8,128]{1,0:T(8,128)S(1)}) custom-call(bf16[7,480]{1,0:T(8,128)(2,1)S(1)} %copy-done.2, bf16[480,512]{1,0:T(8,128)(2,1)S(1)} %copy-done.1, s32[4,480]{1,0:T(4,128)S(1)} %copy-done.3, ...), custom_call_target="tpu_custom_call" | custom-call | flops 2000000000 | bytes 4000000 | tf_op jit(solution)/shard_map/assemble_kernel/pallas_call | solution.py:486
  18.2 10.3 %all-to-all-start = ((f32[8,168,128]{2,1,0:T(8,128)}), f32[8,168,128]{2,1,0:T(8,128)S(1)}, u32[]{:S(2)}, u32[]{:S(2)}) async-start(f32[8,168,128]{2,1,0:T(8,128)} %bitcast.2), calls=%async_computation | async-start | bytes 1376256 | tf_op jit(solution)/shard_map/all_to_all | solution.py:457
  28.6 0.1 pad.2.clone
  28.6 11.2 %all-to-all-done = f32[8,168,128]{2,1,0:T(8,128)S(1)} async-done(((f32[8,168,128]{2,1,0:T(8,128)}), f32[8,168,128]{2,1,0:T(8,128)S(1)}, u32[]{:S(2)}, u32[]{:S(2)}) %all-to-all-start) | async-done | bytes 688160 | tf_op jit(solution)/shard_map/all_to_all | solution.py:457
  39.9 0.3 maximum_maximum_fusion
  40.1 13.8 %all_to_all.72 = f32[4,384,128]{2,1,0:T(8,128)S(1)} all-to-all(f32[4,384,128]{2,1,0:T(8,128)S(1)} %bitcast.16), channel_id=1, replica_groups=mesh['y'=4,'core'=2,'x'=4,'z'=16] {'x'}, dimensions={0} | all-to-all | bytes 1572864 | tf_op jit(solution)/shard_map/all_to_all | solution.py:457
  54.0 3.5 %all-to-all-start.4 = ((f32[4,512,128]{2,1,0:T(8,128)}), f32[4,512,128]{2,1,0:T(8,128)S(1)}, u32[]{:S(2)}, u32[]{:S(2)}) async-start(f32[4,512,128]{2,1,0:T(8,128)} %bitcast.6), calls=%async_computation.4 | async-start | bytes 2097152 | tf_op jit(solution)/shard_map/all_to_all | solution.py:457
  57.5 0.7 reduce_sum.55
  58.2 12.5 %all-to-all-done.4 = f32[4,512,128]{2,1,0:T(8,128)S(1)} async-done(((f32[4,512,128]{2,1,0:T(8,128)}), f32[4,512,128]{2,1,0:T(8,128)S(1)}, u32[]{:S(2)}, u32[]{:S(2)}) %all-to-all-start.4) | async-done | bytes 1048608 | tf_op jit(solution)/shard_map/all_to_all | solution.py:457
  70.7 11.5 %all-to-all-start.2 = ((f32[16,24,128]{2,1,0:T(8,128)}), f32[16,24,128]{2,1,0:T(8,128)S(1)}, u32[]{:S(2)}, u32[]{:S(2)}) async-start(f32[16,24,128]{2,1,0:T(8,128)} %bitcast.4), calls=%async_computation.2 | async-start | bytes 393216 | tf_op jit(solution)/shard_map/all_to_all | solution.py:457
  82.2 0.8 reduce_sum.57
  83.0 11.6 %all-to-all-done.2 = f32[16,24,128]{2,1,0:T(8,128)S(1)} async-done(((f32[16,24,128]{2,1,0:T(8,128)}), f32[16,24,128]{2,1,0:T(8,128)S(1)}, u32[]{:S(2)}, u32[]{:S(2)}) %all-to-all-start.2) | async-done | bytes 196640 | tf_op jit(solution)/shard_map/all_to_all | solution.py:457
  94.5 6.9 %all-to-all-start.5 = ((f32[16,32,128]{2,1,0:T(8,128)}), f32[16,32,128]{2,1,0:T(8,128)S(1)}, u32[]{:S(2)}, u32[]{:S(2)}) async-start(f32[16,32,128]{2,1,0:T(8,128)} %bitcast.7), calls=%async_computation.5 | async-start | bytes 524288 | tf_op jit(solution)/shard_map/all_to_all | solution.py:457
  101.5 12.7 %all-to-all-done.5 = f32[16,32,128]{2,1,0:T(8,128)S(1)} async-done(((f32[16,32,128]{2,1,0:T(8,128)}), f32[16,32,128]{2,1,0:T(8,128)S(1)}, u32[]{:S(2)}, u32[]{:S(2)}) %all-to-all-start.5) | async-done | bytes 262176 | tf_op jit(solution)/shard_map/all_to_all | solution.py:457
  114.2 0.7 broadcast_in_dim.27
  114.9 9.4 %all-to-all-start.3 = ((f32[16,24,128]{2,1,0:T(8,128)}), f32[16,24,128]{2,1,0:T(8,128)S(1)}, u32[]{:S(2)}, u32[]{:S(2)}) async-start(f32[16,24,128]{2,1,0:T(8,128)} %broadcast_in_dim.27), calls=%async_computation.3 | async-start | bytes 393216 | tf_op jit(solution)/shard_map/all_to_all | solution.py:465
  124.3 12.3 %all-to-all-done.3 = f32[16,24,128]{2,1,0:T(8,128)S(1)} async-done(((f32[16,24,128]{2,1,0:T(8,128)}), f32[16,24,128]{2,1,0:T(8,128)S(1)}, u32[]{:S(2)}, u32[]{:S(2)}) %all-to-all-start.3) | async-done | bytes 196640 | tf_op jit(solution)/shard_map/all_to_all | solution.py:465
  136.6 0.7 broadcast_in_dim.28
  137.4 7.2 %all-to-all-start.6 = ((f32[16,32,128]{2,1,0:T(8,128)}), f32[16,32,128]{2,1,0:T(8,128)S(1)}, u32[]{:S(2)}, u32[]{:S(2)}) async-start(f32[16,32,128]{2,1,0:T(8,128)} %broadcast_in_dim.28), calls=%async_computation.6 | async-start | bytes 524288 | tf_op jit(solution)/shard_map/all_to_all | solution.py:465
  144.5 0.0 all-gather.2.cloned.1.call-start
  144.6 12.3 %all_gather.9.main_ref = f32[1536,128]{1,0:T(8,128)S(1)} all-gather(f32[384,128]{1,0:T(8,128)S(1)} %bitcast.18), channel_id=1, replica_groups=mesh['y'=4,'core'=2,'x'=4,'z'=16] {'x'}, dimensions={0}, use_global_device_ids=true | all-gather | bytes 983040 | tf_op jit(solution)/shard_map/all_gather | solution.py:466
  156.9 0.5 all-to-all-done.6
  157.3 0.0 copy-start.11
  157.3 0.0 copy-start.8
  157.3 0.7 copy-done.11
  158.0 0.0 all-gather.2.cloned.1.call-update
  158.1 0.0 copy-done.8
  158.1 31.4 %regional_kernel.1 = (f32[1280,128]{1,0:T(8,128)S(1)}, f32[1280,128]{1,0:T(8,128)S(1)}, f32[4,8,128]{2,1,0:T(8,128)S(1)}) custom-call(f32[1536,128]{1,0:T(8,128)S(1)} %all_gather.9.main_ref, f32[1,512]{1,0:T(1,128)S(1)} %copy-done.8), custom_call_target="tpu_custom_call" | custom-call | flops 20000000000 | bytes 4000000 | tf_op jit(solution)/shard_map/regional_kernel/pallas_call | solution.py:510
  189.5 0.7 all-gather.2.cloned.1.call-done.rg_ref
  190.2 0.0 copy-start
  190.2 1.2 copy-done
  191.4 4.9 %coupling_kernel.1 = (f32[1344,128]{1,0:T(8,128)S(1)}, f32[512,512]{1,0:T(8,128)S(1)}) custom-call(f32[1536,128]{1,0:T(8,128)S(1)} %all_gather.9.main_ref, f32[2048,128]{1,0:T(8,128)S(1)} %copy-done, f32[1280,128]{1,0:T(8,128)S(1)} %get-tuple-element.19.tri_ref, f32[1280,128]{1,0:T(8,128)S(1)} %get-tuple-element.20.ratio_ref, ...), custom_call_target="tpu_custom_call" | custom-call | flops 4000000000 | bytes 4000000 | tf_op jit(solution)/shard_map/coupling_kernel/pallas_call | solution.py:517
  196.3 20.0 %all_to_all.73 = f32[8,168,128]{2,1,0:T(8,128)S(1)} all-to-all(f32[8,168,128]{2,1,0:T(8,128)S(1)} %bitcast.12), channel_id=1, replica_groups=mesh['y'=4,'core'=2,'x'=4,'z'=16] {'y','core'}, dimensions={0} | all-to-all | bytes 1376256 | tf_op jit(solution)/shard_map/all_to_all | solution.py:457
  216.3 14.2 %all_gather.11.g_ref = f32[1280,128]{1,0:T(8,128)S(1)} all-gather(f32[160,128]{1,0:T(8,128)S(1)} %slice_subtract_fusion), channel_id=1, replica_groups=mesh['y'=4,'core'=2,'x'=4,'z'=16] {'y','core'}, dimensions={0}, use_global_device_ids=true | all-gather | bytes 737280 | tf_op jit(solution)/shard_map/all_gather | solution.py:526
  230.5 0.0 copy-start.9
  230.5 0.7 copy-done.9
  231.2 36.0 %finish_kernel.1 = (f32[7,8]{1,0:T(8,128)}, f32[1,512]{1,0:T(1,128)}, f32[1,512]{1,0:T(1,128)}) custom-call(f32[1280,128]{1,0:T(8,128)S(1)} %all_gather.11.g_ref, f32[8,128]{1,0:T(8,128)S(1)} %slice.14.v_ref, f32[1536,128]{1,0:T(8,128)S(1)} %all_gather.9.main_ref, f32[1,512]{1,0:T(1,128)S(1)} %bitcast.15, f32[1280,128]{1,0:T(8,128)S(1)} %get-tuple-element.20.ratio_ref, ...), custom_call_target="tpu_custom_call" | custom-call | flops 20000000000 | bytes 4000000 | tf_op jit(solution)/shard_map/finish_kernel/pallas_call | solution.py:527
  (7 shorter events, 0.1 us)
Async XLA Ops:
  7.2 0.7 copy-start.6
  7.2 0.7 copy-start.10
  7.9 1.0 copy-start.1
  8.9 0.7 copy-start.2
  9.6 0.7 copy-start.3
  10.3 0.7 copy-start.4
  11.0 0.7 copy-start.5
  11.7 0.7 copy-start.7
  18.2 21.6 %all-to-all-start = ((f32[8,168,128]{2,1,0:T(8,128)}), f32[8,168,128]{2,1,0:T(8,128)S(1)}, u32[]{:S(2)}, u32[]{:S(2)}) async-start(f32[8,168,128]{2,1,0:T(8,128)} %bitcast.2), calls=%async_computation | async-start | bytes 1376256 | tf_op jit(solution)/shard_map/all_to_all | solution.py:457
  54.0 16.8 %all-to-all-start.4 = ((f32[4,512,128]{2,1,0:T(8,128)}), f32[4,512,128]{2,1,0:T(8,128)S(1)}, u32[]{:S(2)}, u32[]{:S(2)}) async-start(f32[4,512,128]{2,1,0:T(8,128)} %bitcast.6), calls=%async_computation.4 | async-start | bytes 2097152 | tf_op jit(solution)/shard_map/all_to_all | solution.py:457
  70.7 23.8 %all-to-all-start.2 = ((f32[16,24,128]{2,1,0:T(8,128)}), f32[16,24,128]{2,1,0:T(8,128)S(1)}, u32[]{:S(2)}, u32[]{:S(2)}) async-start(f32[16,24,128]{2,1,0:T(8,128)} %bitcast.4), calls=%async_computation.2 | async-start | bytes 393216 | tf_op jit(solution)/shard_map/all_to_all | solution.py:457
  94.5 19.7 %all-to-all-start.5 = ((f32[16,32,128]{2,1,0:T(8,128)}), f32[16,32,128]{2,1,0:T(8,128)S(1)}, u32[]{:S(2)}, u32[]{:S(2)}) async-start(f32[16,32,128]{2,1,0:T(8,128)} %bitcast.7), calls=%async_computation.5 | async-start | bytes 524288 | tf_op jit(solution)/shard_map/all_to_all | solution.py:457
  114.9 21.7 %all-to-all-start.3 = ((f32[16,24,128]{2,1,0:T(8,128)}), f32[16,24,128]{2,1,0:T(8,128)S(1)}, u32[]{:S(2)}, u32[]{:S(2)}) async-start(f32[16,24,128]{2,1,0:T(8,128)} %broadcast_in_dim.27), calls=%async_computation.3 | async-start | bytes 393216 | tf_op jit(solution)/shard_map/all_to_all | solution.py:465
  137.4 20.0 %all-to-all-start.6 = ((f32[16,32,128]{2,1,0:T(8,128)}), f32[16,32,128]{2,1,0:T(8,128)S(1)}, u32[]{:S(2)}, u32[]{:S(2)}) async-start(f32[16,32,128]{2,1,0:T(8,128)} %broadcast_in_dim.28), calls=%async_computation.6 | async-start | bytes 524288 | tf_op jit(solution)/shard_map/all_to_all | solution.py:465
  144.5 45.6 %all-gather.2.cloned.1.call-start = ((), (), s32[]{:S(2)}) async-start(), calls=%async_computation.8 | async-start | bytes 1310720 | tf_op jit(solution)/shard_map/all_gather | solution.py:466
  157.3 0.7 copy-start.11
  157.3 0.7 copy-start.8
  190.2 1.2 copy-start
  230.5 0.7 copy-start.9
Sparse Core Ops, SparseCore 0:
  158.2 31.9 all-gather.1

commit v2 on v1

--- a/solution.py
+++ b/solution.py
@@ -11,6 +11,7 @@
 
 NB = 128
 NBLK = 4
+PB = 64
 PAIRS = [(i, j) for i in range(NBLK) for j in range(i, NBLK)]
 SLOT = {pair: at for at, pair in enumerate(PAIRS)}
 TRI = len(PAIRS) * NB
@@ -99,8 +100,8 @@
 
 
 def assemble_kernel(
-    lj_ref, gj_ref, ci_ref, cw_ref, res_ref, ow_ref, cnt_ref, lp_ref,
-    gg_ref, main_ref, rg_ref, red_ref, aux_ref,
+    lj_ref, gj_ref, ci_ref, cw_ref, res_ref, ow_ref, cnt_ref, lp_ref, rp_ref, gp_ref,
+    gg_ref, main_ref, rg_ref, red_ref, aux_ref, prior_ref,
     left, right, padded,
 ):
     rows = gj_ref.shape[0]
@@ -109,6 +110,8 @@
     observed = rows // objects
     width = gj_ref.shape[1]
     res = res_ref[...]
+    prior_ref[:, :width] = jnp.broadcast_to(rp_ref[...], (8, width))
+    prior_ref[:, width:] = jnp.broadcast_to(gp_ref[...], (8, width))
     position = lax.broadcasted_iota(jnp.int32, (objects, rows), 1)
     owner = lax.broadcasted_iota(jnp.int32, (objects, rows), 0)
     count = jnp.zeros((objects, rows), jnp.int32)
@@ -223,78 +226,110 @@
             rg_ref[c * width + i * NB : c * width + (i + 1) * NB, :] = value[:, c * NB : (c + 1) * NB]
 
 
-def lane_take(value, at):
-    return jnp.take_along_axis(value, jnp.full(value.shape, at, jnp.int32), axis=1)
-
-
 def spread(value, at):
-    return jnp.broadcast_to(value[at : at + 1], (8, NB))
-
-
-def tree(terms):
-    terms = list(terms)
-    while len(terms) > 1:
-        paired = [terms[a] + terms[a + 1] for a in range(0, len(terms) - 1, 2)]
-        terms = paired + ([terms[-1]] if len(terms) % 2 else [])
-    return terms[0]
+    return jnp.broadcast_to(value[at : at + 1], (8, 128))
 
 
 def reciprocal(value):
     guess = pltpu.reciprocal(value, approx=True)
-    guess = guess * (2.0 - value * guess)
     return guess * (2.0 - value * guess)
 
 
-def invert_block(ref):
-    lane = lax.broadcasted_iota(jnp.int32, (8, NB), 1)
-    sub = lax.broadcasted_iota(jnp.int32, (8, NB), 0)
+def invert_pivot(ref):
+    lane = lax.broadcasted_iota(jnp.int32, (8, 128), 1)
+    sub = lax.broadcasted_iota(jnp.int32, (8, 128), 0)
+    col = lane & (PB - 1)
+    half = lane - col
+    tiles = PB // 16
+
+    def pick(value, index):
+        return jnp.take_along_axis(value, index, axis=1)
 
     def group(g, carry):
-        base = pl.multiple_of(8 * g, 8)
-        panel = ref[pl.ds(base, 8), :]
-        columns = [lane_take(panel, base + i) for i in range(8)]
-        e = [[None] * 8 for i in range(8)]
-        for i in range(8):
-            for j in range(i, 8):
-                e[i][j] = spread(columns[j], i)
-
-        def get(i, j):
-            return e[min(i, j)][max(i, j)]
-
+        at = pl.multiple_of(8 * lax.rem(g, tiles), 8)
+        side = lax.div(g, tiles) * PB
+        base = 8 * g
+        source = ref[pl.ds(at, 8), :]
+        panel = pick(source, col + side)
+        columns = [pick(source, jnp.full((8, 128), side + base + j, jnp.int32)) for j in range(8)]
         for k in range(0, 8, 2):
-            a, b, c = e[k][k], e[k][k + 1], e[k + 1][k + 1]
+            c0, c1 = columns[k], columns[k + 1]
+            a, b, c = spread(c0, k), spread(c1, k), spread(c1, k + 1)
             q = reciprocal(a * c - b * b)
-            pa, pb, pc = c * q, -(b * q), a * q
-            others = [i for i in range(8) if i not in (k, k + 1)]
-            c0 = {i: get(i, k) for i in others}
-            c1 = {i: get(i, k + 1) for i in others}
-            s0 = {i: c0[i] * pa + c1[i] * pb for i in others}
-            s1 = {i: c0[i] * pb + c1[i] * pc for i in others}
-            for at, i in enumerate(others):
-                for j in others[at:]:
-                    e[i][j] = e[i][j] - s0[i] * c0[j] - s1[i] * c1[j]
-            for i in others:
-                e[min(i, k)][max(i, k)] = s0[i]
-                e[min(i, k + 1)][max(i, k + 1)] = s1[i]
-            e[k][k], e[k][k + 1], e[k + 1][k + 1] = -pa, -pb, -pc
-
-        inside = (lane >= base) & (lane < base + 8)
-        source = [
-            jnp.where(inside, jnp.where(lane == base + i, 1.0, 0.0), spread(panel, i)) for i in range(8)
-        ]
-        rows = [tree([get(i, j) * source[j] for j in range(8)]) for i in range(8)]
-        for t in range(NB // 8):
+            pa, pb, pc = c * q, b * q, a * q
+            s0, s1 = sub == k, sub == k + 1
+            m0, m1 = col == base + k, col == base + k + 1
+            r0 = jnp.where(m0, 1.0, jnp.where(m1, 0.0, spread(panel, k)))
+            r1 = jnp.where(m1, 1.0, jnp.where(m0, 0.0, spread(panel, k + 1)))
+            n0 = pa * r0 - pb * r1
+            n1 = pc * r1 - pb * r0
+            rest = jnp.where(m0 | m1, 0.0, panel) - c0 * n0 - c1 * n1
+            panel = jnp.where(s0, n0, jnp.where(s1, n1, rest))
+            for j in range(k + 2, 8):
+                r0, r1 = spread(columns[j], k), spread(columns[j], k + 1)
+                n0 = pa * r0 - pb * r1
+                n1 = pc * r1 - pb * r0
+                columns[j] = jnp.where(s0, n0, jnp.where(s1, n1, columns[j] - c0 * n0 - c1 * n1))
+        rows = [spread(panel, i) for i in range(8)]
+        inside = (col >= base) & (col < base + 8)
+        for t in range(tiles):
             tile = ref[8 * t : 8 * t + 8, :]
-            terms = [jnp.where(inside, 0.0, tile)]
-            terms = terms + [lane_take(tile, base + i) * rows[i] for i in range(8)]
-            ref[8 * t : 8 * t + 8, :] = tree(terms)
-        last = rows[7]
-        for i in range(7):
-            last = jnp.where(sub == i, rows[i], last)
-        ref[pl.ds(base, 8), :] = -last
+            terms = [pick(tile, half + (base + i)) * rows[i] for i in range(8)]
+            kept = jnp.where(inside, 0.0, tile) - terms[0]
+            ref[8 * t : 8 * t + 8, :] = (kept - terms[1] - (terms[2] + terms[3])) - (
+                (terms[4] + terms[5]) + (terms[6] + terms[7])
+            )
+        here = ref[pl.ds(at, 8), :]
+        ref[pl.ds(at, 8), :] = jnp.where(half == side, panel, here)
         return carry
 
-    lax.fori_loop(0, NB // 8, group, 0)
+    lax.fori_loop(0, PB // 8, group, 0)
+
+
+def split_product(a, b):
+    a0, a1, a2 = pieces(a)
+    b0, b1, b2 = pieces(b)
+    left = jnp.concatenate([a0, a0, a1, a1, a0, a2], axis=0)
+    right = jnp.concatenate([b0, b1, b0, b1, b2, b0], axis=0)
+    return tn(left, right)
+
+
+def eliminate(a, packed, lower_ref, pivot_ref):
+    size = NBLK * NB
+    lane = lax.broadcasted_iota(jnp.int32, (PB, size), 1)
+    sub = lax.broadcasted_iota(jnp.int32, (PB, size), 0)
+    lane32 = lax.broadcasted_iota(jnp.int32, (PB // 2, 128), 1)
+    first = lane32 < PB
+    for p in range(size // PB):
+        r0 = PB * p
+        c0 = 128 * (p // 2)
+        odd = p % 2 == 1
+        row = a[r0 : r0 + PB, :]
+        tile = row[:, c0 : c0 + 128]
+        turned = pltpu.roll(tile, PB, 1)
+        one, two = (turned, tile) if odd else (tile, turned)
+        packed[...] = jnp.where(first, one[: PB // 2], two[PB // 2 :])
+        invert_pivot(packed)
+        inverse = packed[...]
+        moved = pltpu.roll(inverse, PB, 1)
+        pivot = jnp.concatenate([jnp.where(first, inverse, 0.0), jnp.where(first, moved, 0.0)], axis=0)
+        if odd:
+            placed = jnp.concatenate([jnp.where(first, 0.0, moved), jnp.where(first, 0.0, inverse)], axis=0)
+        else:
+            placed = pivot
+        pivot_ref[r0 : r0 + PB, :] = placed
+        unit = jnp.where(lane == sub + r0, 1.0, 0.0)
+        lower_ref[r0 : r0 + PB, :] = jnp.where(lane < r0, row, unit)
+        if r0 + PB < size:
+            inside = (lane >= r0) & (lane < r0 + PB)
+            scaled = split_product(pivot[:, :PB], jnp.where(inside, unit, row))
+            c1 = 128 * ((p + 1) // 2)
+            below = jnp.where(lane >= r0 + PB, row, 0.0)[:, c1:]
+            change = split_product(below, scaled)
+            wide = lax.broadcasted_iota(jnp.int32, (size - c1, 128), 1)
+            own = (wide >= r0 - c0) & (wide < r0 - c0 + PB)
+            a[c1:, c0 : c0 + 128] = jnp.where(own, 0.0, a[c1:, c0 : c0 + 128])
+            a[c1:, :] = a[c1:, :] - change
 
 
 def damped(block, damping, profile):
@@ -303,70 +338,54 @@
     return block + jnp.where(row == col, damping * profile, 0.0)
 
 
-def factor_steps(tri, inv, ratio, vec, solved):
-    for p in range(NBLK):
-        slot = SLOT[p, p]
-        inv[...] = tri[slot * NB : (slot + 1) * NB, :]
-        invert_block(inv)
-        pivot = inv[...]
-        tri[slot * NB : (slot + 1) * NB, :] = pivot
-        solved[p] = nn(vec[p], pivot, HIGHEST)
-        if p + 1 < NBLK:
-            others = range(p + 1, NBLK)
-            block = jnp.concatenate([tri[SLOT[p, j] * NB : (SLOT[p, j] + 1) * NB, :] for j in others], axis=1)
-            scaled = nn(pivot, block, HIGHEST)
-            for j in others:
-                at = SLOT[p, j] * NB
-                ratio[at : at + NB, :] = scaled[:, (j - p - 1) * NB : (j - p) * NB]
-            step = nn(solved[p], block, HIGHEST)
-            for i in others:
-                off = (i - p - 1) * NB
-                change = tn(block[:, off : off + NB], scaled[:, off:], HIGHEST)
-                for j in range(i, NBLK):
-                    at = SLOT[i, j] * NB
-                    tri[at : at + NB, :] = tri[at : at + NB, :] - change[:, (j - i) * NB : (j - i + 1) * NB]
-                vec[i] = vec[i] - step[:, off : off + NB]
-
-
-def regional_kernel(main_ref, prior_ref, tri_ref, ratio_ref, solved_ref, inv, vec):
+def unpack(source, a, damping, profile):
+    a[...] = jnp.zeros_like(a)
+    for (i, j), slot in SLOT.items():
+        block = source[slot * NB : (slot + 1) * NB, :]
+        if i == j:
+            block = damped(block, damping, profile[:, i * NB : (i + 1) * NB])
+        a[i * NB : (i + 1) * NB, j * NB : (j + 1) * NB] = block
+
+
+def read_damping(main_ref):
     scal = main_ref[SUM_AT + PART : SUM_AT + PART + 8, :]
-    damping = scal[0:1, 0:1] / scal[0:1, 1:2]
-    tri_ref[...] = main_ref[0:TRI, :]
-    for p in range(NBLK):
-        slot = SLOT[p, p]
-        profile = prior_ref[0:1, p * NB : (p + 1) * NB]
-        tri_ref[slot * NB : (slot + 1) * NB, :] = damped(
-            tri_ref[slot * NB : (slot + 1) * NB, :], damping, profile
-        )
-        vec[p] = jnp.broadcast_to(main_ref[TRI + p : TRI + p + 1, :], (8, NB))
-    ratio_ref[...] = jnp.zeros_like(ratio_ref)
-    factor_steps(tri_ref, inv, ratio_ref, vec, solved_ref)
-
-
-def coupling_kernel(main_ref, rg_ref, tri_ref, ratio_ref, solved_ref, out_ref, gb_ref, b, t, v):
+    return scal[0:1, 0:1] / scal[0:1, 1:2]
+
+
+def pivot_times(pivot_ref, row):
+    return jnp.concatenate(
+        [nn(row[:, i * NB : (i + 1) * NB], pivot_ref[i * NB : (i + 1) * NB, :], HIGHEST) for i in range(NBLK)],
+        axis=1,
+    )
+
+
+def wide_row(ref, at):
+    return jnp.concatenate(
+        [jnp.broadcast_to(ref[at + c : at + c + 1, :], (8, NB)) for c in range(NBLK)], axis=1
+    )
+
+
+def regional_kernel(main_ref, prior_ref, lower_ref, pivot_ref, a, packed):
+    unpack(main_ref, a, read_damping(main_ref), prior_ref[0:1, : NBLK * NB])
+    eliminate(a, packed, lower_ref, pivot_ref)
+
+
+def coupling_kernel(main_ref, rg_ref, lower_ref, pivot_ref, out_ref, scaled_ref, q_ref, b, u):
     width = NBLK * NB
     for c in range(NBLK):
         b[:, c * NB : (c + 1) * NB] = rg_ref[c * width : (c + 1) * width, :]
-        v[:, c * NB : (c + 1) * NB] = jnp.broadcast_to(
-            main_ref[TRI + NBLK + c : TRI + NBLK + c + 1, :], (8, NB)
-        )
-    t[...] = jnp.zeros_like(t)
-    for p in range(NBLK):
-        here = b[p * NB : (p + 1) * NB, :]
-        slot = SLOT[p, p]
-        scaled = nn(tri_ref[slot * NB : (slot + 1) * NB, :], here, HIGHEST)
-        gb_ref[p * NB : (p + 1) * NB, :] = scaled
-        v[...] = v[...] - nn(solved_ref[p], here, HIGHEST)
-        for i in range(p + 1, NBLK):
-            at = SLOT[p, i] * NB
-            b[i * NB : (i + 1) * NB, :] = b[i * NB : (i + 1) * NB, :] - tn(
-                tri_ref[at : at + NB, :], scaled, HIGHEST
-            )
-        for i in range(NBLK):
-            rows = slice(i * NB, (i + 1) * NB)
-            t[rows, i * NB :] = t[rows, i * NB :] + tn(here[:, i * NB : (i + 1) * NB], scaled[:, i * NB :], HIGHEST)
-    for (i, j), slot in SLOT.items():
-        store_split(out_ref, slot, t[i * NB : (i + 1) * NB, j * NB : (j + 1) * NB])
+    for i in range(NBLK):
+        rows = slice(i * NB, (i + 1) * NB)
+        value = nn(lower_ref[rows, : (i + 1) * NB], b[: (i + 1) * NB, :], HIGHEST)
+        u[rows, :] = value
+        scaled_ref[rows, :] = nn(pivot_ref[rows, :], value, HIGHEST)
+    for i in range(NBLK):
+        value = tn(u[:, i * NB : (i + 1) * NB], scaled_ref[:, i * NB :], HIGHEST)
+        for j in range(i, NBLK):
+            store_split(out_ref, SLOT[i, j], value[:, (j - i) * NB : (j - i + 1) * NB])
+    q = pivot_times(pivot_ref, nt(wide_row(main_ref, TRI), lower_ref[...], HIGHEST))
+    q_ref[...] = q
+    v = wide_row(main_ref, TRI + NBLK) - nn(q, u[...], HIGHEST)
     sub = lax.broadcasted_iota(jnp.int32, (8, NB), 0)
     tail = jnp.zeros((8, NB), f32)
     for c in range(NBLK):
@@ -376,60 +395,40 @@
 
 
 def finish_kernel(
-    g_ref, v_ref, main_ref, prior_ref, ratio_ref, solved_ref, gb_ref, red_ref, aux_ref,
+    g_ref, v_ref, main_ref, prior_ref, flower_ref, scaled_ref, q_ref, red_ref, aux_ref,
     local_ref, regional_ref, global_ref,
-    tri, inv, gratio, vec, gsolved,
+    a, packed, lower, pivot,
 ):
     nparams = local_ref.shape[0]
     width = NBLK * NB
-    scal = main_ref[SUM_AT + PART : SUM_AT + PART + 8, :]
-    damping = scal[0:1, 0:1] / scal[0:1, 1:2]
-    tri[...] = g_ref[...]
-    for p in range(NBLK):
-        slot = SLOT[p, p]
-        profile = prior_ref[0:1, p * NB : (p + 1) * NB]
-        tri[slot * NB : (slot + 1) * NB, :] = damped(tri[slot * NB : (slot + 1) * NB, :], damping, profile)
-        vec[p] = jnp.broadcast_to(v_ref[p : p + 1, :], (8, NB))
-    factor_steps(tri, inv, gratio, vec, gsolved)
-
-    def back(ratio, start):
-        found = [None] * NBLK
-        for p in reversed(range(NBLK)):
-            current = start[p]
-            for j in range(p + 1, NBLK):
-                at = SLOT[p, j] * NB
-                current = current - nt(found[j], ratio[at : at + NB, :], HIGHEST)
-            found[p] = current
-        return found
-
-    global_step = jnp.concatenate(back(gratio, [gsolved[p] for p in range(NBLK)]), axis=1)
-    moved = nt(global_step, gb_ref[...], HIGHEST)
-    regional = back(
-        ratio_ref, [solved_ref[p] - moved[:, p * NB : (p + 1) * NB] for p in range(NBLK)]
-    )
-    regional_step = jnp.concatenate(regional, axis=1)
+    unpack(g_ref, a, read_damping(main_ref), prior_ref[0:1, width:])
+    eliminate(a, packed, lower, pivot)
+    whole = lower[...]
+    forward = pivot_times(pivot, nt(wide_row(v_ref, 0), whole, HIGHEST))
+    global_step = nn(forward, whole, HIGHEST)
+    regional_step = nn(q_ref[...] - nt(global_step, scaled_ref[...], HIGHEST), flower_ref[...], HIGHEST)
     regional_ref[...] = regional_step[0:1, :]
     global_ref[...] = global_step[0:1, :]
 
     aux = aux_ref[...]
     at = 0
-    factor = [[None] * nparams for a in range(nparams)]
-    for a in range(nparams):
-        for c in range(a + 1):
-            factor[a][c] = aux[:, at : at + 1]
+    factor = [[None] * nparams for i in range(nparams)]
+    for i in range(nparams):
+        for c in range(i + 1):
+            factor[i][c] = aux[:, at : at + 1]
             at += 1
     update = jnp.concatenate([regional_step, global_step], axis=1)
     target = []
-    for a in range(nparams):
+    for i in range(nparams):
         target.append(
-            aux[:, at : at + 1] - jnp.sum(red_ref[8 * a : 8 * a + 8, :] * update, axis=1, keepdims=True)
+            aux[:, at : at + 1] - jnp.sum(red_ref[8 * i : 8 * i + 8, :] * update, axis=1, keepdims=True)
         )
         at += 1
     found = backward_small(factor, target)
     sub = lax.broadcasted_iota(jnp.int32, (8, 8), 0)
     lane = lax.broadcasted_iota(jnp.int32, (8, 8), 1)
-    for a in range(nparams):
-        local_ref[a : a + 1, :] = jnp.sum(jnp.where(sub == lane, found[a], 0.0), axis=0, keepdims=True)
+    for i in range(nparams):
+        local_ref[i : i + 1, :] = jnp.sum(jnp.where(sub == lane, found[i], 0.0), axis=0, keepdims=True)
 
 
 def shape(*dims, dtype=f32):
@@ -440,9 +439,14 @@
 SMEM = pl.BlockSpec(memory_space=pltpu.SMEM)
 
 
-def call(kernel, out_shape, scratch, specs, flops):
+def whole_block(dims):
+    return pl.BlockSpec(dims, lambda i: (0,) * len(dims))
+
+
+def call(kernel, out_shape, scratch, specs, flops, grid=()):
     return pl.pallas_call(
         kernel,
+        grid=grid,
         out_shape=out_shape,
         in_specs=specs,
         out_specs=[VMEM] * len(out_shape),
@@ -458,12 +462,9 @@
     return jnp.sum(moved.reshape((parts, value.shape[0] // parts) + value.shape[1:]), axis=0)
 
 
-def sum_layers(value, nx, nz):
-    piece = part_sums(value, "x", nx)
-    piece = part_sums(piece, "z", nz)
-    copies = jnp.broadcast_to(piece[None], (nz,) + piece.shape).reshape((-1,) + piece.shape[1:])
-    whole = lax.all_to_all(copies, "z", 0, 0, tiled=True)
-    return lax.all_gather(whole, "x", axis=0, tiled=True)
+def copies_back(piece, axis, parts):
+    copies = jnp.broadcast_to(piece[None], (parts,) + piece.shape).reshape((-1,) + piece.shape[1:])
+    return lax.all_to_all(copies, axis, 0, 0, tiled=True)
 
 
 def body(
@@ -483,7 +484,7 @@
     nparams = local_jac.shape[0]
     width = global_jac.shape[1]
     stack = 2 * rows + 6 * RPAD
-    gg, main, rg, red, aux = call(
+    gg, main, rg, red, aux, prior = call(
         assemble_kernel,
         [
             shape(REG_PARTS * PART_ROWS, NB),
@@ -491,36 +492,47 @@
             shape(NBLK * width, NB),
             shape(RPAD, 2 * width),
             shape(8, NB),
+            shape(8, 2 * width),
         ],
         [
             pltpu.VMEM((stack, 2 * width), bf16),
             pltpu.VMEM((stack, 2 * width), bf16),
             pltpu.VMEM((NB, 512), f32),
         ],
-        [VMEM, VMEM, VMEM, VMEM, VMEM, VMEM, SMEM, VMEM],
+        [
+            whole_block(local_jac.shape), whole_block(global_jac.shape), whole_block(coeff_index.shape),
+            whole_block(coeff_weight.shape), whole_block((1, rows)), whole_block((1, rows)), SMEM,
+            whole_block(local_prior.shape), whole_block((1, width)), whole_block((1, width)),
+        ],
         2_000_000_000,
+        grid=(1,),
     )(
         local_jac, global_jac, coeff_index, coeff_weight, residual[None], obs_weight[None],
-        obs_count, local_prior,
+        obs_count, local_prior, regional_prior, global_prior[None],
     )
     share = part_sums(gg, GROUPS, REG_PARTS)
+    rg = lax.psum_scatter(rg, "x", scatter_dimension=0, tiled=True)
     main = jnp.concatenate([main, share, jnp.zeros((MAIN_ROWS - SUM_AT - PART_ROWS, NB), f32)], axis=0)
-    main = sum_layers(main, nx, nz)
-    rg = sum_layers(rg, nx, nz)
-    tri, ratio, solved = call(
+    main = part_sums(main, "x", nx)
+    both = part_sums(jnp.concatenate([main, rg], axis=0), "z", nz)
+    both = copies_back(both, "z", nz)
+    main = lax.all_gather(both[: MAIN_ROWS // nx], "x", axis=0, tiled=True)
+    main, rg = lax.optimization_barrier((main, both[MAIN_ROWS // nx :]))
+    rg = copies_back(rg, "x", nx)
+    lower, pivot = call(
         regional_kernel,
-        [shape(TRI, NB), shape(TRI, NB), shape(NBLK, 8, NB)],
-        [pltpu.VMEM((NB, NB), f32), pltpu.VMEM((NBLK, 8, NB), f32)],
-        [VMEM, VMEM],
+        [shape(width, width), shape(width, NB)],
+        [pltpu.VMEM((width, width), f32), pltpu.VMEM((PB // 2, 128), f32)],
+        [VMEM] * 2,
         20_000_000_000,
-    )(main, regional_prior)
-    outer, gb = call(
+    )(main, prior)
+    outer, scaled, q = call(
         coupling_kernel,
-        [shape(REG_PARTS * PART_ROWS, NB), shape(width, width)],
-        [pltpu.VMEM((width, width), f32), pltpu.VMEM((width, width), f32), pltpu.VMEM((8, width), f32)],
-        [VMEM] * 5,
+        [shape(REG_PARTS * PART_ROWS, NB), shape(width, width), shape(8, width)],
+        [pltpu.VMEM((width, width), f32), pltpu.VMEM((width, width), f32)],
+        [VMEM] * 4,
         4_000_000_000,
-    )(main, rg, tri, ratio, solved)
+    )(main, rg, lower, pivot)
     outer = part_sums(outer, GROUPS, REG_PARTS)
     mine = main[SUM_AT : SUM_AT + PART] - outer[:PART]
     matrix = lax.all_gather(mine, GROUPS, axis=0, tiled=True)
@@ -528,15 +540,14 @@
         finish_kernel,
         [shape(nparams, 8), shape(1, width), shape(1, width)],
         [
-            pltpu.VMEM((TRI, NB), f32),
-            pltpu.VMEM((NB, NB), f32),
-            pltpu.VMEM((TRI, NB), f32),
-            pltpu.VMEM((NBLK, 8, NB), f32),
-            pltpu.VMEM((NBLK, 8, NB), f32),
+            pltpu.VMEM((width, width), f32),
+            pltpu.VMEM((PB // 2, 128), f32),
+            pltpu.VMEM((width, width), f32),
+            pltpu.VMEM((width, NB), f32),
         ],
         [VMEM] * 9,
         20_000_000_000,
-    )(matrix, outer[PART:], main, global_prior[None], ratio, solved, gb, red, aux)
+    )(matrix, outer[PART:], main, prior, lower, scaled, q, red, aux)
     return local_step, regional_step, global_step[0]
 
 

time: 275 us -> 236 us (0.86)
  blocking collectives: 60.3 us -> 135 us
  waiting for transfers between devices: 61.5 us -> 11.2 us
  starting transfers between devices: 48.8 us -> 14.1 us
  Pallas kernels: 78.2 us -> 49.8 us
    all_to_all x2 -> x3, blocking collectives: 33.8 us -> 77.5 us  [part_sums(): moved = lax.all_to_all(value, axis, 0, 0, tiled=True)]
    all_to_all x4 -> x1, waiting for transfers between devices: 48 us -> 11.2 us  [part_sums(): moved = lax.all_to_all(value, axis, 0, 0, tiled=True)]
    all_to_all x0 -> x1, blocking collectives: none -> 32.3 us  [copies_back(): return lax.all_to_all(copies, axis, 0, 0, tiled=True)]
    all_to_all x4 -> x1, starting transfers between devices: 32.2 us -> 10.3 us  [part_sums(): moved = lax.all_to_all(value, axis, 0, 0, tiled=True)]
    pallas_call x1, Pallas kernels: 36 us -> 21.2 us  [body(): call(finish_kernel, [shape(nparams, 8), shape(1, width), shape(1, width)]...]
    pallas_call x1, Pallas kernels: 31.4 us -> 16.7 us  [body(): call(regional_kernel, [shape(width, width), shape(width, NB)], [pltpu.VME...]
    all_to_all x2 -> x1, starting transfers between devices: 16.6 us -> 3.7 us  [copies_back(): return lax.all_to_all(copies, axis, 0, 0, tiled=True)]
    all_to_all x2 -> x1, waiting for transfers between devices: 12.8 us -> 0.01 us  [copies_back(): return lax.all_to_all(copies, axis, 0, 0, tiled=True)]
  transfers between devices with their start and end apart: 7 -> 3, of which waited for: 7 -> 1; matrix products, arithmetic and copies ran while one was open for 1% -> 0% of each run, Pallas kernels for 11% -> 7%
where the time goes in v2:
time: 236 us; the launch traced here: 235 us
  blocking collectives  135 us (57%)
  Pallas kernels  49.8 us (21%)
  starting transfers between devices  14.1 us (6%)
  between operations  14.1 us (6%)
  waiting for transfers between devices  11.2 us (5%)
  local copies, waits for them, and re-layouts  8.64 us (4%)
  other arithmetic  2.6 us (1%)
    all_to_all x3, blocking collectives, part_sums(): moved = lax.all_to_all(value, axis, 0, 0, tiled=True)  77.5 us
    all_to_all x1, blocking collectives, copies_back(): return lax.all_to_all(copies, axis, 0, 0, tiled=True)  32.3 us
    pallas_call x1, Pallas kernels, body(): call(finish_kernel, [shape(nparams, 8), shape(1, width), shape(1, width)]...  21.2 us
    pallas_call x1, Pallas kernels, body(): call(regional_kernel, [shape(width, width), shape(width, NB)], [pltpu.VME...  16.7 us
    all_gather x1, blocking collectives, body(): matrix = lax.all_gather(mine, GROUPS, axis=0, tiled=True)  14.2 us
    all_to_all x1, waiting for transfers between devices, part_sums(): moved = lax.all_to_all(value, axis, 0, 0, tiled=True)  11.2 us
    all_gather x1, blocking collectives, body(): main = lax.all_gather(both[:MAIN_ROWS // nx], 'x', axis=0, tiled=True)  10.7 us
    all_to_all x1, starting transfers between devices, part_sums(): moved = lax.all_to_all(value, axis, 0, 0, tiled=True)  10.3 us
  transfers between devices with their start and end apart: 3, of which 1 were waited for; matrix products, arithmetic and copies ran while one was open for 0% of the time, Pallas kernels for 7%

profile of v2, /device:TPU:1, one launch (start us, length us, event | category | flops | bytes accessed | tf_op | source)
XLA Modules:
  0.0 235.2 jit_solution(11334458931979967723)
XLA Ops:
  7.2 0.0 copy-start.3
  7.2 0.0 reduce-scatter.2.cloned.1.call-start
  7.2 0.0 copy-start.9
  7.2 0.6 copy-done.3
  7.9 0.0 copy-done.9
  7.9 0.0 copy-start
  7.9 1.0 copy-done
  8.9 0.0 copy-start.1
  8.9 0.7 copy-done.1
  9.6 0.0 copy-start.2
  9.6 0.7 copy-done.2
  10.3 0.0 copy-start.4
  10.3 0.7 copy-done.4
  11.0 0.0 copy-start.5
  11.0 0.7 copy-done.5
  11.7 0.0 copy-start.6
  11.7 0.7 copy-done.6
  12.4 0.0 copy-start.7
  12.4 0.7 copy-done.7
  13.0 0.0 copy-start.8
  13.0 0.7 copy-done.8
  13.7 5.9 %assemble_kernel.1 = (f32[1344,128]{1,0:T(8,128)}, f32[1288,128]{1,0:T(8,128)S(1)}, f32[2048,128]{1,0:T(8,128)}, f32[64,1024]{1,0:T(8,128)S(1)}, f32[8,128]{1,0:T(8,128)S(1)}, /*index=5*/f32[8,1024]{1,0:T(8,128)S(1)}) custom-call(bf16[7,480]{1,0:T(8,128)(2,1)S(1)} %copy-done.1, bf16[480,512]{1,0:T(8,128)(2,1)S(1)} %copy-done, s32[4,480]{1,0:T(4,128)S(1)} %copy-done.2, ...), custom_call_target="tpu_custom_call" | custom-call | flops 2000000000 | bytes 4000000 | tf_op jit(solution)/shard_map/assemble_kernel/pallas_call | solution.py:487
  19.7 0.0 reduce-scatter.2.cloned.1.call-update
  19.7 10.3 %all-to-all-start = ((f32[8,168,128]{2,1,0:T(8,128)}), f32[8,168,128]{2,1,0:T(8,128)S(1)}, u32[]{:S(2)}, u32[]{:S(2)}) async-start(f32[8,168,128]{2,1,0:T(8,128)} %bitcast.3), calls=%async_computation | async-start | bytes 1376256 | tf_op jit(solution)/shard_map/all_to_all | solution.py:461
  30.0 0.1 pad.4.clone
  30.1 11.2 %all-to-all-done = f32[8,168,128]{2,1,0:T(8,128)S(1)} async-done(((f32[8,168,128]{2,1,0:T(8,128)}), f32[8,168,128]{2,1,0:T(8,128)S(1)}, u32[]{:S(2)}, u32[]{:S(2)}) %all-to-all-start) | async-done | bytes 688160 | tf_op jit(solution)/shard_map/all_to_all | solution.py:461
  41.3 0.3 maximum_maximum_fusion
  41.6 19.7 %all_to_all.53 = f32[4,384,128]{2,1,0:T(8,128)S(1)} all-to-all(f32[4,384,128]{2,1,0:T(8,128)S(1)} %bitcast.15), channel_id=1, replica_groups=mesh['y'=4,'core'=2,'x'=4,'z'=16] {'x'}, dimensions={0} | all-to-all | bytes 1572864 | tf_op jit(solution)/shard_map/all_to_all | solution.py:461
  61.3 0.0 reduce-scatter.2.cloned.1.call-done
  61.3 1.0 pad_maximum_fusion
  62.3 32.5 %all_to_all.54 = f32[16,56,128]{2,1,0:T(8,128)S(1)} all-to-all(f32[16,56,128]{2,1,0:T(8,128)S(1)} %bitcast.16), channel_id=1, replica_groups=mesh['y'=4,'core'=2,'x'=4,'z'=16] {'z'}, dimensions={0} | all-to-all | bytes 917504 | tf_op jit(solution)/shard_map/all_to_all | solution.py:461
  94.9 32.3 %all_to_all.55 = f32[16,56,128]{2,1,0:T(8,128)S(1)} all-to-all(f32[16,56,128]{2,1,0:T(8,128)S(1)} %broadcast_in_dim.28), channel_id=1, replica_groups=mesh['y'=4,'core'=2,'x'=4,'z'=16] {'z'}, dimensions={0} | all-to-all | bytes 917504 | tf_op jit(solution)/shard_map/all_to_all | solution.py:467
  127.3 10.7 %all_gather.6.main_ref = f32[1536,128]{1,0:T(8,128)S(1)} all-gather(f32[384,128]{1,0:T(8,128)S(1)} %slice.20), channel_id=1, replica_groups=mesh['y'=4,'core'=2,'x'=4,'z'=16] {'x'}, dimensions={0}, use_global_device_ids=true | all-gather | bytes 983040 | tf_op jit(solution)/shard_map/all_gather | solution.py:519
  138.1 1.0 broadcast_in_dim.29
  139.1 3.7 %all-to-all-start.4 = ((f32[4,512,128]{2,1,0:T(8,128)}), f32[4,512,128]{2,1,0:T(8,128)S(1)}, u32[]{:S(2)}, u32[]{:S(2)}) async-start(f32[4,512,128]{2,1,0:T(8,128)} %broadcast_in_dim.29), calls=%async_computation.5 | async-start | bytes 2097152 | tf_op jit(solution)/shard_map/all_to_all | solution.py:467
  142.8 16.7 %regional_kernel.1 = (f32[512,512]{1,0:T(8,128)S(1)}, f32[512,128]{1,0:T(8,128)S(1)}) custom-call(f32[1536,128]{1,0:T(8,128)S(1)} %all_gather.6.main_ref, f32[8,1024]{1,0:T(8,128)S(1)} %get-tuple-element.24.prior_ref), custom_call_target="tpu_custom_call" | custom-call | flops 20000000000 | bytes 4000000 | tf_op jit(solution)/shard_map/regional_kernel/pallas_call | solution.py:522
  159.4 0.0 all-to-all-done.4
  159.5 6.0 %coupling_kernel.1 = (f32[1344,128]{1,0:T(8,128)S(1)}, f32[512,512]{1,0:T(8,128)S(1)}, f32[8,512]{1,0:T(8,128)S(1)}) custom-call(f32[1536,128]{1,0:T(8,128)S(1)} %all_gather.6.main_ref, f32[2048,128]{1,0:T(8,128)S(1)} %bitcast.10, f32[512,512]{1,0:T(8,128)S(1)} %get-tuple-element.25.lower_ref.flower_ref, f32[512,128]{1,0:T(8,128)S(1)} %get-tuple-element.26.pivot_ref), custom_call_target="tpu_custom_call" | custom-call | flops 4000000000 | bytes 4000000 | tf_op jit(solution)/shard_map/coupling_kernel/pallas_call | solution.py:529
  165.4 0.0 copy-start.10
  165.4 1.0 copy-done.10
  166.4 25.3 %all_to_all.56 = f32[8,168,128]{2,1,0:T(8,128)} all-to-all(f32[8,168,128]{2,1,0:T(8,128)S(1)} %bitcast.11), channel_id=1, replica_groups=mesh['y'=4,'core'=2,'x'=4,'z'=16] {'y','core'}, dimensions={0} | all-to-all | bytes 1376256 | tf_op jit(solution)/shard_map/all_to_all | solution.py:461
  191.7 0.0 copy-start.11
  191.7 1.2 reduce_sum.39
  192.9 14.2 %all_gather.7.g_ref = f32[1280,128]{1,0:T(8,128)S(1)} all-gather(f32[160,128]{1,0:T(8,128)S(1)} %slice_subtract_fusion), channel_id=1, replica_groups=mesh['y'=4,'core'=2,'x'=4,'z'=16] {'y','core'}, dimensions={0}, use_global_device_ids=true | all-gather | bytes 737280 | tf_op jit(solution)/shard_map/all_gather | solution.py:538
  207.2 0.0 copy-done.11
  207.2 21.2 %finish_kernel.1 = (f32[7,8]{1,0:T(8,128)}, f32[1,512]{1,0:T(1,128)}, f32[1,512]{1,0:T(1,128)}) custom-call(f32[1280,128]{1,0:T(8,128)S(1)} %all_gather.7.g_ref, f32[8,128]{1,0:T(8,128)S(1)} %slice.23.v_ref, f32[1536,128]{1,0:T(8,128)S(1)} %all_gather.6.main_ref, f32[8,1024]{1,0:T(8,128)S(1)} %get-tuple-element.24.prior_ref, ...), custom_call_target="tpu_custom_call" | custom-call | flops 20000000000 | bytes 4000000 | tf_op jit(solution)/shard_map/finish_kernel/pallas_call | solution.py:539
  (9 shorter events, 0.2 us)
Async XLA Ops:
  7.2 0.7 copy-start.3
  7.2 54.1 %reduce-scatter.2.cloned.1.call-start = ((), (), s32[]{:S(2)}) async-start(), calls=%async_computation.7 | async-start | bytes 1310720 | tf_op jit(solution)/shard_map/reduce_scatter | solution.py:514
  7.2 0.7 copy-start.9
  7.9 1.0 copy-start
  8.9 0.7 copy-start.1
  9.6 0.7 copy-start.2
  10.3 0.7 copy-start.4
  11.0 0.7 copy-start.5
  11.7 0.7 copy-start.6
  12.4 0.7 copy-start.7
  13.0 0.7 copy-start.8
  19.7 21.6 %all-to-all-start = ((f32[8,168,128]{2,1,0:T(8,128)}), f32[8,168,128]{2,1,0:T(8,128)S(1)}, u32[]{:S(2)}, u32[]{:S(2)}) async-start(f32[8,168,128]{2,1,0:T(8,128)} %bitcast.3), calls=%async_computation | async-start | bytes 1376256 | tf_op jit(solution)/shard_map/all_to_all | solution.py:461
  139.1 20.4 %all-to-all-start.4 = ((f32[4,512,128]{2,1,0:T(8,128)}), f32[4,512,128]{2,1,0:T(8,128)S(1)}, u32[]{:S(2)}, u32[]{:S(2)}) async-start(f32[4,512,128]{2,1,0:T(8,128)} %broadcast_in_dim.29), calls=%async_computation.5 | async-start | bytes 2097152 | tf_op jit(solution)/shard_map/all_to_all | solution.py:467
  165.4 1.0 copy-start.10
  191.7 15.5 %copy-start.11 = (f32[512,512]{1,0:T(8,128)S(1)}, f32[512,512]{1,0:T(8,128)}, u32[]{:S(2)}) copy-start(f32[512,512]{1,0:T(8,128)} %copy-done.10) | copy-start | bytes 3145732
Sparse Core Ops, SparseCore 0:
  19.8 40.3 reduce-scatter.1

commit v3 on v2

--- a/solution.py
+++ b/solution.py
@@ -18,8 +18,9 @@
 REG_PARTS = 8
 PART = TRI // REG_PARTS
 PART_ROWS = PART + 8
-MAIN_ROWS = 1536
-SUM_AT = TRI + 8
+MAIN_PART = TRI // 4
+MAIN_PITCH = 384
+SUM_AT = MAIN_PART + 8
 CHUNK = 48
 RPAD = 64
 
@@ -88,15 +89,41 @@
     return result
 
 
-def store_split(ref, slot, block):
+def spans(slot, part, pitch):
     done = 0
     while done < NB:
         flat = slot * NB + done
-        part, off = flat // PART, flat % PART
-        take = min(NB - done, PART - off)
-        start = part * PART_ROWS + off
+        take = min(NB - done, part - flat % part)
+        yield done, take, flat // part * pitch + flat % part
+        done += take
+
+
+def store_split(ref, slot, block, part=PART, pitch=PART_ROWS):
+    for done, take, start in spans(slot, part, pitch):
         ref[start : start + take, :] = block[done : done + take]
-        done += take
+
+
+def presence(cnt_ref, rows, objects=8):
+    position = lax.broadcasted_iota(jnp.int32, (objects, rows), 1)
+    owner = lax.broadcasted_iota(jnp.int32, (objects, rows), 0)
+    count = jnp.zeros((objects, rows), jnp.int32)
+    for n in range(objects):
+        count = jnp.where(owner == n, cnt_ref[n], count)
+    local = position - owner * (rows // objects)
+    return (local >= 0) & (local < rows // objects) & (local < count)
+
+
+def misfit_kernel(res_ref, ow_ref, cnt_ref, out_ref):
+    rows = res_ref.shape[1]
+    present = presence(cnt_ref, rows)
+    value = jnp.where(present, ow_ref[...] * res_ref[...] * res_ref[...], 0.0)
+    misfit = jnp.sum(jnp.sum(value, axis=0, keepdims=True), axis=1, keepdims=True)
+    counted = jnp.sum(
+        jnp.sum(jnp.where(present, 1.0, 0.0), axis=0, keepdims=True), axis=1, keepdims=True
+    )
+    lane = lax.broadcasted_iota(jnp.int32, out_ref.shape, 1)
+    row = lax.broadcasted_iota(jnp.int32, out_ref.shape, 0) % 8
+    out_ref[...] = jnp.where(row == 0, jnp.where(lane == 0, misfit, jnp.where(lane == 1, counted, 0.0)), 0.0)
 
 
 def assemble_kernel(
@@ -112,19 +139,8 @@
     res = res_ref[...]
     prior_ref[:, :width] = jnp.broadcast_to(rp_ref[...], (8, width))
     prior_ref[:, width:] = jnp.broadcast_to(gp_ref[...], (8, width))
-    position = lax.broadcasted_iota(jnp.int32, (objects, rows), 1)
-    owner = lax.broadcasted_iota(jnp.int32, (objects, rows), 0)
-    count = jnp.zeros((objects, rows), jnp.int32)
-    for n in range(objects):
-        count = jnp.where(owner == n, cnt_ref[n], count)
-    local = position - owner * observed
-    present = (local >= 0) & (local < observed) & (local < count)
-    live = jnp.where(present, jnp.broadcast_to(ow_ref[...], (objects, rows)), 0.0)
+    live = jnp.where(presence(cnt_ref, rows), jnp.broadcast_to(ow_ref[...], (objects, rows)), 0.0)
     weight = jnp.sum(live, axis=0, keepdims=True)
-    misfit = jnp.sum(weight * res * res, axis=1, keepdims=True)
-    counted = jnp.sum(
-        jnp.sum(jnp.where(present, 1.0, 0.0), axis=0, keepdims=True), axis=1, keepdims=True
-    )
 
     padded[...] = jnp.zeros_like(padded)
     padded[0:1, :rows] = weight
@@ -201,13 +217,15 @@
     gradient = jnp.sum(nn(lhs, right[rows : 2 * rows, :]), axis=0, keepdims=True)
     for a in range(nparams):
         gradient = gradient - jnp.sum(reduced_gradient[a] * reduced[a], axis=0, keepdims=True)
-    for at in range(8):
-        main_ref[TRI + at : TRI + at + 1, :] = gradient[:, at * NB : (at + 1) * NB]
-
-    row_lane = lax.broadcasted_iota(jnp.int32, (8, NB), 1)
-    scalars = jnp.where(row_lane == 0, misfit, jnp.where(row_lane == 1, counted, 0.0))
-    for part in range(REG_PARTS):
-        gg_ref[part * PART_ROWS + PART : (part + 1) * PART_ROWS, :] = scalars
+    for part in range(4):
+        main_ref[part * MAIN_PITCH + MAIN_PART : (part + 1) * MAIN_PITCH, :] = jnp.zeros(
+            (MAIN_PITCH - MAIN_PART, NB), f32
+        )
+        for at in range(2):
+            line = 2 * part + at
+            main_ref[part * MAIN_PITCH + MAIN_PART + at : part * MAIN_PITCH + MAIN_PART + at + 1, :] = (
+                gradient[:, line * NB : (line + 1) * NB]
+            )
     for i in range(NBLK):
         for half in range(2):
             at = half * width
@@ -216,9 +234,9 @@
                 block = value[:, (j - i) * NB : (j - i + 1) * NB]
                 slot = SLOT[i, j]
                 if half == 0:
-                    main_ref[slot * NB : (slot + 1) * NB, :] = block
+                    store_split(main_ref, slot, block, MAIN_PART, MAIN_PITCH)
                 else:
-                    store_split(gg_ref, slot, block)
+                    gg_ref[slot * NB : (slot + 1) * NB, :] = block
         value = 2.0 * tn(left[0:rows, i * NB : (i + 1) * NB], right[0:rows, width:]) + tn(
             left[base:, i * NB : (i + 1) * NB], right[base:, width:]
         )
@@ -338,18 +356,23 @@
     return block + jnp.where(row == col, damping * profile, 0.0)
 
 
-def unpack(source, a, damping, profile):
+def unpack(source, a, damping, profile, part=TRI, pitch=TRI):
     a[...] = jnp.zeros_like(a)
     for (i, j), slot in SLOT.items():
-        block = source[slot * NB : (slot + 1) * NB, :]
+        block = jnp.concatenate(
+            [source[start : start + take, :] for done, take, start in spans(slot, part, pitch)], axis=0
+        )
         if i == j:
             block = damped(block, damping, profile[:, i * NB : (i + 1) * NB])
         a[i * NB : (i + 1) * NB, j * NB : (j + 1) * NB] = block
 
 
 def read_damping(main_ref):
-    scal = main_ref[SUM_AT + PART : SUM_AT + PART + 8, :]
-    return scal[0:1, 0:1] / scal[0:1, 1:2]
+    scal = main_ref[SUM_AT : SUM_AT + 1, :]
+    for part in range(1, 4):
+        at = part * MAIN_PITCH + SUM_AT
+        scal = scal + main_ref[at : at + 1, :]
+    return scal[:, 0:1] / scal[:, 1:2]
 
 
 def pivot_times(pivot_ref, row):
@@ -359,21 +382,27 @@
     )
 
 
-def wide_row(ref, at):
-    return jnp.concatenate(
-        [jnp.broadcast_to(ref[at + c : at + c + 1, :], (8, NB)) for c in range(NBLK)], axis=1
-    )
+def wide_row(ref, places):
+    return jnp.concatenate([jnp.broadcast_to(ref[at : at + 1, :], (8, NB)) for at in places], axis=1)
+
+
+def gradient_row(main_ref, half):
+    lines = range(NBLK * half, NBLK * half + NBLK)
+    return wide_row(main_ref, [line // 2 * MAIN_PITCH + MAIN_PART + line % 2 for line in lines])
 
 
 def regional_kernel(main_ref, prior_ref, lower_ref, pivot_ref, a, packed):
-    unpack(main_ref, a, read_damping(main_ref), prior_ref[0:1, : NBLK * NB])
+    unpack(main_ref, a, read_damping(main_ref), prior_ref[0:1, : NBLK * NB], MAIN_PART, MAIN_PITCH)
     eliminate(a, packed, lower_ref, pivot_ref)
 
 
-def coupling_kernel(main_ref, rg_ref, lower_ref, pivot_ref, out_ref, scaled_ref, q_ref, b, u):
+def coupling_kernel(main_ref, rg_ref, lower_ref, pivot_ref, out_ref, scaled_ref, q_ref, share_ref, b, u):
     width = NBLK * NB
     for c in range(NBLK):
-        b[:, c * NB : (c + 1) * NB] = rg_ref[c * width : (c + 1) * width, :]
+        pitch = width + PART
+        b[:, c * NB : (c + 1) * NB] = rg_ref[c * pitch : c * pitch + width, :]
+        part = rg_ref[c * pitch + width : (c + 1) * pitch, :]
+        share_ref[...] = part if c == 0 else share_ref[...] + part
     for i in range(NBLK):
         rows = slice(i * NB, (i + 1) * NB)
         value = nn(lower_ref[rows, : (i + 1) * NB], b[: (i + 1) * NB, :], HIGHEST)
@@ -383,9 +412,9 @@
         value = tn(u[:, i * NB : (i + 1) * NB], scaled_ref[:, i * NB :], HIGHEST)
         for j in range(i, NBLK):
             store_split(out_ref, SLOT[i, j], value[:, (j - i) * NB : (j - i + 1) * NB])
-    q = pivot_times(pivot_ref, nt(wide_row(main_ref, TRI), lower_ref[...], HIGHEST))
+    q = pivot_times(pivot_ref, nt(gradient_row(main_ref, 0), lower_ref[...], HIGHEST))
     q_ref[...] = q
-    v = wide_row(main_ref, TRI + NBLK) - nn(q, u[...], HIGHEST)
+    v = gradient_row(main_ref, 1) - nn(q, u[...], HIGHEST)
     sub = lax.broadcasted_iota(jnp.int32, (8, NB), 0)
     tail = jnp.zeros((8, NB), f32)
     for c in range(NBLK):
@@ -404,7 +433,7 @@
     unpack(g_ref, a, read_damping(main_ref), prior_ref[0:1, width:])
     eliminate(a, packed, lower, pivot)
     whole = lower[...]
-    forward = pivot_times(pivot, nt(wide_row(v_ref, 0), whole, HIGHEST))
+    forward = pivot_times(pivot, nt(wide_row(v_ref, range(NBLK)), whole, HIGHEST))
     global_step = nn(forward, whole, HIGHEST)
     regional_step = nn(q_ref[...] - nt(global_step, scaled_ref[...], HIGHEST), flower_ref[...], HIGHEST)
     regional_ref[...] = regional_step[0:1, :]
@@ -443,7 +472,7 @@
     return pl.BlockSpec(dims, lambda i: (0,) * len(dims))
 
 
-def call(kernel, out_shape, scratch, specs, flops, grid=()):
+def call(kernel, out_shape, scratch, specs, flops, grid=(), limit=40):
     return pl.pallas_call(
         kernel,
         grid=grid,
@@ -452,7 +481,7 @@
         out_specs=[VMEM] * len(out_shape),
         scratch_shapes=scratch,
         name=kernel.__name__,
-        compiler_params=pltpu.CompilerParams(vmem_limit_bytes=40 * 1024 * 1024),
+        compiler_params=pltpu.CompilerParams(vmem_limit_bytes=limit * 1024 * 1024),
         cost_estimate=pl.CostEstimate(flops=flops, bytes_accessed=4_000_000, transcendentals=0),
     )
 
@@ -484,11 +513,21 @@
     nparams = local_jac.shape[0]
     width = global_jac.shape[1]
     stack = 2 * rows + 6 * RPAD
+    sums = call(
+        misfit_kernel,
+        [shape(8 * REG_PARTS, NB)],
+        [],
+        [whole_block((1, rows)), whole_block((1, rows)), SMEM],
+        1_000_000,
+        grid=(1,),
+    )(residual[None], obs_weight[None], obs_count)[0]
+    sums, obs_count = lax.optimization_barrier((sums, obs_count))
+    sums = lax.all_to_all(sums, GROUPS, 0, 0, tiled=True)
     gg, main, rg, red, aux, prior = call(
         assemble_kernel,
         [
-            shape(REG_PARTS * PART_ROWS, NB),
-            shape(SUM_AT, NB),
+            shape(TRI, NB),
+            shape(4 * MAIN_PITCH, NB),
             shape(NBLK * width, NB),
             shape(RPAD, 2 * width),
             shape(8, NB),
@@ -504,21 +543,26 @@
             whole_block(coeff_weight.shape), whole_block((1, rows)), whole_block((1, rows)), SMEM,
             whole_block(local_prior.shape), whole_block((1, width)), whole_block((1, width)),
         ],
-        2_000_000_000,
+        8_000_000_000,
         grid=(1,),
+        limit=60,
     )(
         local_jac, global_jac, coeff_index, coeff_weight, residual[None], obs_weight[None],
         obs_count, local_prior, regional_prior, global_prior[None],
     )
-    share = part_sums(gg, GROUPS, REG_PARTS)
+    sums, gg, main, rg = lax.optimization_barrier((sums, gg, main, rg))
     rg = lax.psum_scatter(rg, "x", scatter_dimension=0, tiled=True)
-    main = jnp.concatenate([main, share, jnp.zeros((MAIN_ROWS - SUM_AT - PART_ROWS, NB), f32)], axis=0)
+    share = lax.psum_scatter(gg, GROUPS, scatter_dimension=0, tiled=True)
     main = part_sums(main, "x", nx)
-    both = part_sums(jnp.concatenate([main, rg], axis=0), "z", nz)
-    both = copies_back(both, "z", nz)
-    main = lax.all_gather(both[: MAIN_ROWS // nx], "x", axis=0, tiled=True)
-    main, rg = lax.optimization_barrier((main, both[MAIN_ROWS // nx :]))
-    rg = copies_back(rg, "x", nx)
+    sums = jnp.sum(sums.reshape(REG_PARTS, 8, NB), axis=0)
+    main = main + jnp.pad(sums, ((SUM_AT, MAIN_PITCH - SUM_AT - 8), (0, 0)))
+    main = copies_back(part_sums(main, "z", nz), "z", nz)
+    rest = jnp.concatenate([rg, share], axis=0)
+    main, rest = lax.optimization_barrier((main, rest))
+    rest = part_sums(rest, "z", nz)
+    main = lax.all_gather(main, "x", axis=0, tiled=True)
+    main, rest = lax.optimization_barrier((main, rest))
+    rest = copies_back(rest, "z", nz)
     lower, pivot = call(
         regional_kernel,
         [shape(width, width), shape(width, NB)],
@@ -526,15 +570,16 @@
         [VMEM] * 2,
         20_000_000_000,
     )(main, prior)
-    outer, scaled, q = call(
+    rg = copies_back(rest, "x", nx)
+    outer, scaled, q, share = call(
         coupling_kernel,
-        [shape(REG_PARTS * PART_ROWS, NB), shape(width, width), shape(8, width)],
+        [shape(REG_PARTS * PART_ROWS, NB), shape(width, width), shape(8, width), shape(PART, NB)],
         [pltpu.VMEM((width, width), f32), pltpu.VMEM((width, width), f32)],
         [VMEM] * 4,
         4_000_000_000,
     )(main, rg, lower, pivot)
     outer = part_sums(outer, GROUPS, REG_PARTS)
-    mine = main[SUM_AT : SUM_AT + PART] - outer[:PART]
+    mine = share - outer[:PART]
     matrix = lax.all_gather(mine, GROUPS, axis=0, tiled=True)
     local_step, regional_step, global_step = call(
         finish_kernel,

time: 236 us -> 254 us (1.076)
  blocking collectives: 135 us -> 100 us
  waiting for transfers between devices: 11.2 us -> 40.3 us
  starting transfers between devices: 14.1 us -> 38.3 us
    all_to_all x3 -> x2, blocking collectives: 77.5 us -> 46.8 us  [part_sums(): moved = lax.all_to_all(value, axis, 0, 0, tiled=True)]
    reduce_scatter x1, waiting for transfers between devices: 0.02 us -> 22.2 us  [body(): rg = lax.psum_scatter(rg, 'x', scatter_dimension=0, tiled=True)]
    all_to_all x0 -> x1, starting transfers between devices: none -> 10.1 us  [body(): sums = lax.all_to_all(sums, GROUPS, 0, 0, tiled=True)]
    all_to_all x1 -> x2, starting transfers between devices: 3.7 us -> 12.7 us  [copies_back(): return lax.all_to_all(copies, axis, 0, 0, tiled=True)]
    all_to_all x1 -> x2, waiting for transfers between devices: 11.2 us -> 17.3 us  [part_sums(): moved = lax.all_to_all(value, axis, 0, 0, tiled=True)]
    all_to_all x1, blocking collectives: 32.3 us -> 27.1 us  [copies_back(): return lax.all_to_all(copies, axis, 0, 0, tiled=True)]
    all_to_all x1 -> x2, starting transfers between devices: 10.3 us -> 15.5 us  [part_sums(): moved = lax.all_to_all(value, axis, 0, 0, tiled=True)]
    unnamed x24 -> x22, local copies, waits for them, and re-layouts: 7.46 us -> 3.61 us
  transfers between devices with their start and end apart: 3 -> 7, of which waited for: 1 -> 3; matrix products, arithmetic and copies ran while one was open for 0% -> 1% of each run, Pallas kernels for 7% -> 9%
where the time goes in v3:
time: 254 us; the launch traced here: 253 us
  blocking collectives  100 us (39%)
  Pallas kernels  51.5 us (20%)
  waiting for transfers between devices  40.3 us (16%)
  starting transfers between devices  38.3 us (15%)
  between operations  14.2 us (6%)
  local copies, waits for them, and re-layouts  6.33 us (2%)
    all_to_all x2, blocking collectives, part_sums(): moved = lax.all_to_all(value, axis, 0, 0, tiled=True)  46.8 us
    all_to_all x1, blocking collectives, copies_back(): return lax.all_to_all(copies, axis, 0, 0, tiled=True)  27.1 us
    reduce_scatter x1, waiting for transfers between devices, body(): rg = lax.psum_scatter(rg, 'x', scatter_dimension=0, tiled=True)  22.2 us
    pallas_call x1, Pallas kernels, body(): call(finish_kernel, [shape(nparams, 8), shape(1, width), shape(1, width)]...  21.2 us
    all_to_all x2, waiting for transfers between devices, part_sums(): moved = lax.all_to_all(value, axis, 0, 0, tiled=True)  17.3 us
    pallas_call x1, Pallas kernels, body(): call(regional_kernel, [shape(width, width), shape(width, NB)], [pltpu.VME...  16.7 us
    all_to_all x2, starting transfers between devices, part_sums(): moved = lax.all_to_all(value, axis, 0, 0, tiled=True)  15.5 us
    all_gather x1, blocking collectives, body(): matrix = lax.all_gather(mine, GROUPS, axis=0, tiled=True)  14.2 us
  transfers between devices with their start and end apart: 7, of which 3 were waited for; matrix products, arithmetic and copies ran while one was open for 1% of the time, Pallas kernels for 9%

profile of v3, /device:TPU:1, one launch (start us, length us, event | category | flops | bytes accessed | tf_op | source)
XLA Modules:
  0.0 253.1 jit_solution(12355712319738469761)
XLA Ops:
  7.2 0.0 copy-start
  7.2 0.7 copy-done
  7.8 0.0 copy-start.1
  7.9 0.7 copy-done.1
  8.5 0.0 copy-start.2
  8.5 0.7 copy-done.2
  9.2 1.2 misfit_kernel.1
  10.4 10.1 %all-to-all-start = ((f32[8,8,128]{2,1,0:T(8,128)}), f32[8,8,128]{2,1,0:T(8,128)S(1)}, u32[]{:S(2)}, u32[]{:S(2)}) async-start(f32[8,8,128]{2,1,0:T(8,128)} %bitcast.2), calls=%async_computation | async-start | bytes 65536 | tf_op jit(solution)/shard_map/all_to_all | solution.py:525
  20.5 0.0 reduce-scatter.5.cloned.1.call-start
  20.5 6.5 %assemble_kernel.1 = (f32[1280,128]{1,0:T(8,128)}, f32[1536,128]{1,0:T(8,128)}, f32[2048,128]{1,0:T(8,128)}, f32[64,1024]{1,0:T(8,128)}, f32[8,128]{1,0:T(8,128)}, /*index=5*/f32[8,1024]{1,0:T(8,128)}) custom-call(bf16[7,480]{1,0:T(8,128)(2,1)} %lj_ref.1, bf16[480,512]{1,0:T(8,128)(2,1)} %gj_ref.1, s32[4,480]{1,0:T(4,128)} %ci_ref.1, bf16[4,480]{1,0:T(4,128)(2,1)} %cw_ref.1, ...), custom_call_target="tpu_custom_call" | custom-call | flops 8000000000 | bytes 4000000 | tf_op jit(solution)/shard_map/assemble_kernel/pallas_call | solution.py:526
  27.1 0.0 all-to-all-done
  27.1 0.0 reduce-scatter.5.cloned.1.call-update
  27.1 3.5 %all-to-all-start.1 = ((f32[4,384,128]{2,1,0:T(8,128)}), f32[4,384,128]{2,1,0:T(8,128)S(1)}, u32[]{:S(2)}, u32[]{:S(2)}) async-start(f32[4,384,128]{2,1,0:T(8,128)} %bitcast.19), calls=%async_computation.1 | async-start | bytes 1572864 | tf_op jit(solution)/shard_map/all_to_all | solution.py:490
  30.6 0.0 reduce-scatter.3.cloned.1.call-start
  30.7 0.7 reduce-scatter.3.cloned.1.call-update
  31.4 11.5 %all-to-all-done.1 = f32[4,384,128]{2,1,0:T(8,128)S(1)} async-done(((f32[4,384,128]{2,1,0:T(8,128)}), f32[4,384,128]{2,1,0:T(8,128)S(1)}, u32[]{:S(2)}, u32[]{:S(2)}) %all-to-all-start.1) | async-done | bytes 786464 | tf_op jit(solution)/shard_map/all_to_all | solution.py:490
  42.9 23.3 %all_to_all.71 = f32[16,24,128]{2,1,0:T(8,128)S(1)} all-to-all(f32[16,24,128]{2,1,0:T(8,128)S(1)} %bitcast.20), channel_id=1, replica_groups=mesh['y'=4,'core'=2,'x'=4,'z'=16] {'z'}, dimensions={0} | all-to-all | bytes 393216 | tf_op jit(solution)/shard_map/all_to_all | solution.py:490
  66.2 0.7 broadcast_in_dim.34
  66.9 8.8 %all-to-all-start.3 = ((f32[16,24,128]{2,1,0:T(8,128)}), f32[16,24,128]{2,1,0:T(8,128)S(1)}, u32[]{:S(2)}, u32[]{:S(2)}) async-start(f32[16,24,128]{2,1,0:T(8,128)} %broadcast_in_dim.34), calls=%async_computation.3 | async-start | bytes 393216 | tf_op jit(solution)/shard_map/all_to_all | solution.py:496
  75.7 0.0 reduce-scatter.5.cloned.1.call-done
  75.8 22.2 %reduce-scatter.3.cloned.1.call-done = f32[512,128]{1,0:T(8,128)} async-done(((f32[2048,128]{1,0:T(8,128)}), f32[512,128]{1,0:T(8,128)}) %reduce-scatter.3.cloned.1.call-update) | async-done | bytes 262160 | tf_op jit(solution)/shard_map/reduce_scatter | solution.py:554
  98.0 1.0 pad_maximum_fusion
  99.0 0.0 all-to-all-done.3
  99.0 0.8 all_to_all.56
  99.8 12.0 %all-to-all-start.4 = ((f32[16,42,128]{2,1,0:T(8,128)}), f32[16,42,128]{2,1,0:T(8,128)S(1)}, u32[]{:S(2)}, u32[]{:S(2)}) async-start(f32[16,42,128]{2,1,0:T(8,128)} %all_to_all.56), calls=%async_computation.6 | async-start | bytes 786432 | tf_op jit(solution)/shard_map/all_to_all | solution.py:490
  111.8 12.0 %all_gather.6.main_ref = f32[1536,128]{1,0:T(8,128)S(1)} all-gather(f32[384,128]{1,0:T(8,128)S(1)} %bitcast.21), channel_id=1, replica_groups=mesh['y'=4,'core'=2,'x'=4,'z'=16] {'x'}, dimensions={0}, use_global_device_ids=true | all-gather | bytes 983040 | tf_op jit(solution)/shard_map/all_gather | solution.py:563
  123.8 5.8 %all-to-all-done.4 = f32[16,42,128]{2,1,0:T(8,128)S(1)} async-done(((f32[16,42,128]{2,1,0:T(8,128)}), f32[16,42,128]{2,1,0:T(8,128)S(1)}, u32[]{:S(2)}, u32[]{:S(2)}) %all-to-all-start.4) | async-done | bytes 344096 | tf_op jit(solution)/shard_map/all_to_all | solution.py:490
  129.7 27.1 %all_to_all.72 = f32[16,42,128]{2,1,0:T(8,128)S(1)} all-to-all(f32[16,42,128]{2,1,0:T(8,128)S(1)} %broadcast_in_dim.35), channel_id=1, replica_groups=mesh['y'=4,'core'=2,'x'=4,'z'=16] {'z'}, dimensions={0} | all-to-all | bytes 688128 | tf_op jit(solution)/shard_map/all_to_all | solution.py:496
  156.8 1.2 broadcast_in_dim.37
  158.0 0.0 copy-start.8
  158.0 3.9 %all-to-all-start.6 = ((f32[4,672,128]{2,1,0:T(8,128)}), f32[4,672,128]{2,1,0:T(8,128)S(1)}, u32[]{:S(2)}, u32[]{:S(2)}) async-start(f32[4,672,128]{2,1,0:T(8,128)} %broadcast_in_dim.37), calls=%async_computation.8 | async-start | bytes 2752512 | tf_op jit(solution)/shard_map/all_to_all | solution.py:496
  161.9 0.0 copy-done.8
  161.9 16.7 %regional_kernel.1 = (f32[512,512]{1,0:T(8,128)S(1)}, f32[512,128]{1,0:T(8,128)S(1)}) custom-call(f32[1536,128]{1,0:T(8,128)S(1)} %all_gather.6.main_ref, f32[8,1024]{1,0:T(8,128)S(1)} %copy-done.8), custom_call_target="tpu_custom_call" | custom-call | flops 20000000000 | bytes 4000000 | tf_op jit(solution)/shard_map/regional_kernel/pallas_call | solution.py:566
  178.6 0.0 all-to-all-done.6
  178.6 5.9 %coupling_kernel.1 = (f32[1344,128]{1,0:T(8,128)S(1)}, f32[512,512]{1,0:T(8,128)S(1)}, f32[8,512]{1,0:T(8,128)S(1)}, f32[160,128]{1,0:T(8,128)S(1)}) custom-call(f32[1536,128]{1,0:T(8,128)S(1)} %all_gather.6.main_ref, f32[2688,128]{1,0:T(8,128)S(1)} %bitcast.13, f32[512,512]{1,0:T(8,128)S(1)} %get-tuple-element.42.lower_ref.flower_ref, ...), custom_call_target="tpu_custom_call" | custom-call | flops 4000000000 | bytes 4000000 | tf_op jit(solution)/shard_map/coupling_kernel/pallas_call | solution.py:574
  184.4 0.0 copy-start.3
  184.4 1.0 copy-done.3
  185.4 0.0 copy-start.6
  185.4 0.6 copy-done.6
  186.0 0.0 copy-start.4
  186.0 0.0 copy-start.5
  186.0 0.0 copy-start.7
  186.0 0.0 copy-start.9
  186.0 0.0 copy-start.10
  186.0 23.5 %all_to_all.73 = f32[8,168,128]{2,1,0:T(8,128)} all-to-all(f32[8,168,128]{2,1,0:T(8,128)S(1)} %bitcast.14), channel_id=1, replica_groups=mesh['y'=4,'core'=2,'x'=4,'z'=16] {'y','core'}, dimensions={0} | all-to-all | bytes 1376256 | tf_op jit(solution)/shard_map/all_to_all | solution.py:490
  209.6 1.1 reduce_sum.49
  210.8 14.2 %all_gather.7.g_ref = f32[1280,128]{1,0:T(8,128)S(1)} all-gather(f32[160,128]{1,0:T(8,128)S(1)} %slice_subtract_fusion), channel_id=1, replica_groups=mesh['y'=4,'core'=2,'x'=4,'z'=16] {'y','core'}, dimensions={0}, use_global_device_ids=true | all-gather | bytes 737280 | tf_op jit(solution)/shard_map/all_gather | solution.py:583
  225.0 0.0 copy-done.4
  225.0 0.0 copy-done.5
  225.0 0.0 copy-done.7
  225.0 0.0 copy-done.9
  225.0 0.0 copy-done.10
  225.0 21.2 %finish_kernel.1 = (f32[7,8]{1,0:T(8,128)}, f32[1,512]{1,0:T(1,128)}, f32[1,512]{1,0:T(1,128)}) custom-call(f32[1280,128]{1,0:T(8,128)S(1)} %all_gather.7.g_ref, f32[8,128]{1,0:T(8,128)S(1)} %slice.9.v_ref, f32[1536,128]{1,0:T(8,128)S(1)} %all_gather.6.main_ref, f32[8,1024]{1,0:T(8,128)S(1)} %copy-done.9, ...), custom_call_target="tpu_custom_call" | custom-call | flops 20000000000 | bytes 4000000 | tf_op jit(solution)/shard_map/finish_kernel/pallas_call | solution.py:584
  (9 shorter events, 0.2 us)
Async XLA Ops:
  7.2 0.7 copy-start
  7.8 0.7 copy-start.1
  8.5 0.7 copy-start.2
  10.4 16.6 %all-to-all-start = ((f32[8,8,128]{2,1,0:T(8,128)}), f32[8,8,128]{2,1,0:T(8,128)S(1)}, u32[]{:S(2)}, u32[]{:S(2)}) async-start(f32[8,8,128]{2,1,0:T(8,128)} %bitcast.2), calls=%async_computation | async-start | bytes 65536 | tf_op jit(solution)/shard_map/all_to_all | solution.py:525
  20.5 55.2 %reduce-scatter.5.cloned.1.call-start = ((), (), s32[]{:S(2)}) async-start(), calls=%async_computation.11 | async-start | bytes 737280 | tf_op jit(solution)/shard_map/reduce_scatter | solution.py:555
  27.1 15.8 %all-to-all-start.1 = ((f32[4,384,128]{2,1,0:T(8,128)}), f32[4,384,128]{2,1,0:T(8,128)S(1)}, u32[]{:S(2)}, u32[]{:S(2)}) async-start(f32[4,384,128]{2,1,0:T(8,128)} %bitcast.19), calls=%async_computation.1 | async-start | bytes 1572864 | tf_op jit(solution)/shard_map/all_to_all | solution.py:490
  30.6 67.4 %reduce-scatter.3.cloned.1.call-start = ((), (), s32[]{:S(2)}) async-start(), calls=%async_computation.10 | async-start | bytes 1310720 | tf_op jit(solution)/shard_map/reduce_scatter | solution.py:554
  66.9 32.1 %all-to-all-start.3 = ((f32[16,24,128]{2,1,0:T(8,128)}), f32[16,24,128]{2,1,0:T(8,128)S(1)}, u32[]{:S(2)}, u32[]{:S(2)}) async-start(f32[16,24,128]{2,1,0:T(8,128)} %broadcast_in_dim.34), calls=%async_computation.3 | async-start | bytes 393216 | tf_op jit(solution)/shard_map/all_to_all | solution.py:496
  99.8 29.9 %all-to-all-start.4 = ((f32[16,42,128]{2,1,0:T(8,128)}), f32[16,42,128]{2,1,0:T(8,128)S(1)}, u32[]{:S(2)}, u32[]{:S(2)}) async-start(f32[16,42,128]{2,1,0:T(8,128)} %all_to_all.56), calls=%async_computation.6 | async-start | bytes 786432 | tf_op jit(solution)/shard_map/all_to_all | solution.py:490
  158.0 3.9 %copy-start.8 = (f32[8,1024]{1,0:T(8,128)S(1)}, f32[8,1024]{1,0:T(8,128)}, u32[]{:S(2)}) copy-start(f32[8,1024]{1,0:T(8,128)} %get-tuple-element.41.prior_ref) | copy-start | bytes 98308
  158.0 20.5 %all-to-all-start.6 = ((f32[4,672,128]{2,1,0:T(8,128)}), f32[4,672,128]{2,1,0:T(8,128)S(1)}, u32[]{:S(2)}, u32[]{:S(2)}) async-start(f32[4,672,128]{2,1,0:T(8,128)} %broadcast_in_dim.37), calls=%async_computation.8 | async-start | bytes 2752512 | tf_op jit(solution)/shard_map/all_to_all | solution.py:496
  184.4 1.0 copy-start.3
  185.4 0.6 copy-start.6
  186.0 39.0 %copy-start.4 = (f32[512,512]{1,0:T(8,128)S(1)}, f32[512,512]{1,0:T(8,128)}, u32[]{:S(2)}) copy-start(f32[512,512]{1,0:T(8,128)} %copy-done.3) | copy-start | bytes 3145732
  186.0 39.0 %copy-start.5 = (f32[64,1024]{1,0:T(8,128)S(1)}, f32[64,1024]{1,0:T(8,128)}, u32[]{:S(2)}) copy-start(f32[64,1024]{1,0:T(8,128)} %get-tuple-element.48.red_ref) | copy-start | bytes 786436
  186.0 39.0 %copy-start.7 = (f32[8,512]{1,0:T(8,128)S(1)}, f32[8,512]{1,0:T(8,128)}, u32[]{:S(2)}) copy-start(f32[8,512]{1,0:T(8,128)} %copy-done.6) | copy-start | bytes 49156
  186.0 39.0 %copy-start.9 = (f32[8,1024]{1,0:T(8,128)S(1)}, f32[8,1024]{1,0:T(8,128)}, u32[]{:S(2)}) copy-start(f32[8,1024]{1,0:T(8,128)} %get-tuple-element.41.prior_ref) | copy-start | bytes 98308
  186.0 39.0 %copy-start.10 = (f32[8,128]{1,0:T(8,128)S(1)}, f32[8,128]{1,0:T(8,128)}, u32[]{:S(2)}) copy-start(f32[8,128]{1,0:T(8,128)} %get-tuple-element.49.aux_ref) | copy-start | bytes 12292
Sparse Core Ops, SparseCore 0:
  27.2 37.2 reduce-scatter.4
  67.3 30.6 reduce-scatter.2

commit v4 on v2

--- a/solution.py
+++ b/solution.py
@@ -230,11 +230,6 @@
     return jnp.broadcast_to(value[at : at + 1], (8, 128))
 
 
-def reciprocal(value):
-    guess = pltpu.reciprocal(value, approx=True)
-    return guess * (2.0 - value * guess)
-
-
 def invert_pivot(ref):
     lane = lax.broadcasted_iota(jnp.int32, (8, 128), 1)
     sub = lax.broadcasted_iota(jnp.int32, (8, 128), 0)
@@ -255,7 +250,7 @@
         for k in range(0, 8, 2):
             c0, c1 = columns[k], columns[k + 1]
             a, b, c = spread(c0, k), spread(c1, k), spread(c1, k + 1)
-            q = reciprocal(a * c - b * b)
+            q = 1.0 / (a * c - b * b)
             pa, pb, pc = c * q, b * q, a * q
             s0, s1 = sub == k, sub == k + 1
             m0, m1 = col == base + k, col == base + k + 1
@@ -352,17 +347,20 @@
     return scal[0:1, 0:1] / scal[0:1, 1:2]
 
 
-def pivot_times(pivot_ref, row):
-    return jnp.concatenate(
-        [nn(row[:, i * NB : (i + 1) * NB], pivot_ref[i * NB : (i + 1) * NB, :], HIGHEST) for i in range(NBLK)],
-        axis=1,
-    )
+def by_row(matrix, row):
+    return jnp.sum(matrix * row, axis=1, keepdims=True)
+
+
+def by_column(matrix, column):
+    return jnp.sum(matrix * column, axis=0, keepdims=True)
+
+
+def turn(row):
+    return jnp.broadcast_to(row, (8, NB)).T
 
 
 def wide_row(ref, at):
-    return jnp.concatenate(
-        [jnp.broadcast_to(ref[at + c : at + c + 1, :], (8, NB)) for c in range(NBLK)], axis=1
-    )
+    return jnp.concatenate([ref[at + c : at + c + 1, :] for c in range(NBLK)], axis=1)
 
 
 def regional_kernel(main_ref, prior_ref, lower_ref, pivot_ref, a, packed):
@@ -370,26 +368,29 @@
     eliminate(a, packed, lower_ref, pivot_ref)
 
 
-def coupling_kernel(main_ref, rg_ref, lower_ref, pivot_ref, out_ref, scaled_ref, q_ref, b, u):
+def coupling_kernel(main_ref, rg_ref, lower_ref, pivot_ref, out_ref, scaled_ref, q_ref, b, u, w):
     width = NBLK * NB
     for c in range(NBLK):
         b[:, c * NB : (c + 1) * NB] = rg_ref[c * width : (c + 1) * width, :]
+    b[:, width:] = jnp.zeros((width, NB), f32)
+    for i in range(NBLK):
+        b[i * NB : (i + 1) * NB, width : width + 8] = turn(main_ref[TRI + i : TRI + i + 1, :])
     for i in range(NBLK):
         rows = slice(i * NB, (i + 1) * NB)
         value = nn(lower_ref[rows, : (i + 1) * NB], b[: (i + 1) * NB, :], HIGHEST)
-        u[rows, :] = value
-        scaled_ref[rows, :] = nn(pivot_ref[rows, :], value, HIGHEST)
+        u[rows, :] = value[:, :width]
+        w[rows, :] = nn(pivot_ref[rows, :], value, HIGHEST)
+    scaled_ref[...] = w[:, :width]
+    q_ref[...] = w[:, width:]
+    sub = lax.broadcasted_iota(jnp.int32, (8, NB), 0)
+    tail = jnp.zeros((8, NB), f32)
     for i in range(NBLK):
-        value = tn(u[:, i * NB : (i + 1) * NB], scaled_ref[:, i * NB :], HIGHEST)
+        value = tn(u[:, i * NB : (i + 1) * NB], w[:, i * NB :], HIGHEST)
         for j in range(i, NBLK):
             store_split(out_ref, SLOT[i, j], value[:, (j - i) * NB : (j - i + 1) * NB])
-    q = pivot_times(pivot_ref, nt(wide_row(main_ref, TRI), lower_ref[...], HIGHEST))
-    q_ref[...] = q
-    v = wide_row(main_ref, TRI + NBLK) - nn(q, u[...], HIGHEST)
-    sub = lax.broadcasted_iota(jnp.int32, (8, NB), 0)
-    tail = jnp.zeros((8, NB), f32)
-    for c in range(NBLK):
-        tail = jnp.where(sub == c, v[:, c * NB : (c + 1) * NB], tail)
+        line = TRI + NBLK + i
+        rest = jnp.broadcast_to(main_ref[line : line + 1, :], (8, NB)) - value[:, width - i * NB :].T[:8]
+        tail = jnp.where(sub == i, jnp.broadcast_to(rest[0:1], (8, NB)), tail)
     for part in range(REG_PARTS):
         out_ref[part * PART_ROWS + PART : (part + 1) * PART_ROWS, :] = tail
 
@@ -404,11 +405,19 @@
     unpack(g_ref, a, read_damping(main_ref), prior_ref[0:1, width:])
     eliminate(a, packed, lower, pivot)
     whole = lower[...]
-    forward = pivot_times(pivot, nt(wide_row(v_ref, 0), whole, HIGHEST))
-    global_step = nn(forward, whole, HIGHEST)
-    regional_step = nn(q_ref[...] - nt(global_step, scaled_ref[...], HIGHEST), flower_ref[...], HIGHEST)
-    regional_ref[...] = regional_step[0:1, :]
-    global_ref[...] = global_step[0:1, :]
+    forward = by_row(whole, wide_row(v_ref, 0))
+    forward = jnp.concatenate(
+        [
+            turn(by_column(pivot[i * NB : (i + 1) * NB, :], forward[i * NB : (i + 1) * NB]))[:, 0:1]
+            for i in range(NBLK)
+        ],
+        axis=0,
+    )
+    global_step = by_column(whole, forward)
+    rest = q_ref[:, 0:1] - by_row(scaled_ref[...], global_step)
+    regional_step = by_column(flower_ref[...], rest)
+    regional_ref[...] = regional_step
+    global_ref[...] = global_step
 
     aux = aux_ref[...]
     at = 0
@@ -443,7 +452,7 @@
     return pl.BlockSpec(dims, lambda i: (0,) * len(dims))
 
 
-def call(kernel, out_shape, scratch, specs, flops, grid=()):
+def call(kernel, out_shape, scratch, specs, flops, grid=(), limit=16):
     return pl.pallas_call(
         kernel,
         grid=grid,
@@ -452,7 +461,7 @@
         out_specs=[VMEM] * len(out_shape),
         scratch_shapes=scratch,
         name=kernel.__name__,
-        compiler_params=pltpu.CompilerParams(vmem_limit_bytes=40 * 1024 * 1024),
+        compiler_params=pltpu.CompilerParams(vmem_limit_bytes=limit * 1024 * 1024),
         cost_estimate=pl.CostEstimate(flops=flops, bytes_accessed=4_000_000, transcendentals=0),
     )
 
@@ -506,6 +515,7 @@
         ],
         2_000_000_000,
         grid=(1,),
+        limit=60,
     )(
         local_jac, global_jac, coeff_index, coeff_weight, residual[None], obs_weight[None],
         obs_count, local_prior, regional_prior, global_prior[None],
@@ -528,8 +538,12 @@
     )(main, prior)
     outer, scaled, q = call(
         coupling_kernel,
-        [shape(REG_PARTS * PART_ROWS, NB), shape(width, width), shape(8, width)],
-        [pltpu.VMEM((width, width), f32), pltpu.VMEM((width, width), f32)],
+        [shape(REG_PARTS * PART_ROWS, NB), shape(width, width), shape(width, NB)],
+        [
+            pltpu.VMEM((width, width + NB), f32),
+            pltpu.VMEM((width, width), f32),
+            pltpu.VMEM((width, width + NB), f32),
+        ],
         [VMEM] * 4,
         4_000_000_000,
     )(main, rg, lower, pivot)

time: 236 us -> 228 us (0.966)
  local copies, waits for them, and re-layouts: 8.64 us -> 2.86 us
    unnamed x24 -> x12, local copies, waits for them, and re-layouts: 7.46 us -> 1.68 us
where the time goes in v4:
time: 228 us; the launch traced here: 227 us
  blocking collectives  135 us (59%)
  Pallas kernels  47.6 us (21%)
  starting transfers between devices  14.2 us (6%)
  between operations  14.1 us (6%)
  waiting for transfers between devices  11.2 us (5%)
  local copies, waits for them, and re-layouts  2.86 us (1%)
  other arithmetic  2.6 us (1%)
    all_to_all x3, blocking collectives, part_sums(): moved = lax.all_to_all(value, axis, 0, 0, tiled=True)  77.1 us
    all_to_all x1, blocking collectives, copies_back(): return lax.all_to_all(copies, axis, 0, 0, tiled=True)  32.3 us
    pallas_call x1, Pallas kernels, body(): call(finish_kernel, [shape(nparams, 8), shape(1, width), shape(1, width)]...  19 us
    pallas_call x1, Pallas kernels, body(): call(regional_kernel, [shape(width, width), shape(width, NB)], [pltpu.VME...  16.7 us
    all_gather x1, blocking collectives, body(): matrix = lax.all_gather(mine, GROUPS, axis=0, tiled=True)  14.3 us
    all_to_all x1, waiting for transfers between devices, part_sums(): moved = lax.all_to_all(value, axis, 0, 0, tiled=True)  11.2 us
    all_gather x1, blocking collectives, body(): main = lax.all_gather(both[:MAIN_ROWS // nx], 'x', axis=0, tiled=True)  10.7 us
    all_to_all x1, starting transfers between devices, part_sums(): moved = lax.all_to_all(value, axis, 0, 0, tiled=True)  10.3 us
  transfers between devices with their start and end apart: 3, of which 1 were waited for; matrix products, arithmetic and copies ran while one was open for 0% of the time, Pallas kernels for 7%

profile of v4, /device:TPU:1, one launch (start us, length us, event | category | flops | bytes accessed | tf_op | source)
XLA Modules:
  0.0 227.1 jit_solution(8295291188119878219)
XLA Ops:
  7.2 0.0 reduce-scatter.2.cloned.1.call-start
  7.2 6.5 %assemble_kernel.1 = (f32[1344,128]{1,0:T(8,128)}, f32[1288,128]{1,0:T(8,128)}, f32[2048,128]{1,0:T(8,128)}, f32[64,1024]{1,0:T(8,128)}, f32[8,128]{1,0:T(8,128)}, /*index=5*/f32[8,1024]{1,0:T(8,128)}) custom-call(bf16[7,480]{1,0:T(8,128)(2,1)} %lj_ref.1, bf16[480,512]{1,0:T(8,128)(2,1)} %gj_ref.1, s32[4,480]{1,0:T(4,128)} %ci_ref.1, bf16[4,480]{1,0:T(4,128)(2,1)} %cw_ref.1, ...), custom_call_target="tpu_custom_call" | custom-call | flops 2000000000 | bytes 4000000 | tf_op jit(solution)/shard_map/assemble_kernel/pallas_call | solution.py:496
  13.7 0.0 reduce-scatter.2.cloned.1.call-update
  13.7 10.3 %all-to-all-start = ((f32[8,168,128]{2,1,0:T(8,128)}), f32[8,168,128]{2,1,0:T(8,128)S(1)}, u32[]{:S(2)}, u32[]{:S(2)}) async-start(f32[8,168,128]{2,1,0:T(8,128)} %bitcast.3), calls=%async_computation | async-start | bytes 1376256 | tf_op jit(solution)/shard_map/all_to_all | solution.py:470
  24.1 0.0 copy-start.5
  24.1 0.1 pad.4.clone
  24.2 11.2 %all-to-all-done = f32[8,168,128]{2,1,0:T(8,128)S(1)} async-done(((f32[8,168,128]{2,1,0:T(8,128)}), f32[8,168,128]{2,1,0:T(8,128)S(1)}, u32[]{:S(2)}, u32[]{:S(2)}) %all-to-all-start) | async-done | bytes 688160 | tf_op jit(solution)/shard_map/all_to_all | solution.py:470
  35.4 0.0 copy-done.5
  35.4 0.3 maximum_maximum_fusion
  35.7 19.7 %all_to_all.53 = f32[4,384,128]{2,1,0:T(8,128)S(1)} all-to-all(f32[4,384,128]{2,1,0:T(8,128)S(1)} %bitcast.12), channel_id=1, replica_groups=mesh['y'=4,'core'=2,'x'=4,'z'=16] {'x'}, dimensions={0} | all-to-all | bytes 1572864 | tf_op jit(solution)/shard_map/all_to_all | solution.py:470
  55.4 0.0 reduce-scatter.2.cloned.1.call-done
  55.4 1.0 pad_maximum_fusion
  56.4 32.6 %all_to_all.54 = f32[16,56,128]{2,1,0:T(8,128)S(1)} all-to-all(f32[16,56,128]{2,1,0:T(8,128)S(1)} %bitcast.13), channel_id=1, replica_groups=mesh['y'=4,'core'=2,'x'=4,'z'=16] {'z'}, dimensions={0} | all-to-all | bytes 917504 | tf_op jit(solution)/shard_map/all_to_all | solution.py:470
  89.0 32.3 %all_to_all.55 = f32[16,56,128]{2,1,0:T(8,128)S(1)} all-to-all(f32[16,56,128]{2,1,0:T(8,128)S(1)} %broadcast_in_dim.28), channel_id=1, replica_groups=mesh['y'=4,'core'=2,'x'=4,'z'=16] {'z'}, dimensions={0} | all-to-all | bytes 917504 | tf_op jit(solution)/shard_map/all_to_all | solution.py:476
  121.4 10.7 %all_gather.6.main_ref = f32[1536,128]{1,0:T(8,128)S(1)} all-gather(f32[384,128]{1,0:T(8,128)S(1)} %slice.20), channel_id=1, replica_groups=mesh['y'=4,'core'=2,'x'=4,'z'=16] {'x'}, dimensions={0}, use_global_device_ids=true | all-gather | bytes 983040 | tf_op jit(solution)/shard_map/all_gather | solution.py:529
  132.1 1.0 broadcast_in_dim.29
  133.2 0.0 copy-start.3
  133.2 3.8 %all-to-all-start.4 = ((f32[4,512,128]{2,1,0:T(8,128)}), f32[4,512,128]{2,1,0:T(8,128)S(1)}, u32[]{:S(2)}, u32[]{:S(2)}) async-start(f32[4,512,128]{2,1,0:T(8,128)} %broadcast_in_dim.29), calls=%async_computation.5 | async-start | bytes 2097152 | tf_op jit(solution)/shard_map/all_to_all | solution.py:476
  137.0 0.0 copy-done.3
  137.0 16.7 %regional_kernel.1 = (f32[512,512]{1,0:T(8,128)S(1)}, f32[512,128]{1,0:T(8,128)S(1)}) custom-call(f32[1536,128]{1,0:T(8,128)S(1)} %all_gather.6.main_ref, f32[8,1024]{1,0:T(8,128)S(1)} %copy-done.3), custom_call_target="tpu_custom_call" | custom-call | flops 20000000000 | bytes 4000000 | tf_op jit(solution)/shard_map/regional_kernel/pallas_call | solution.py:532
  153.7 0.0 all-to-all-done.4
  153.7 5.4 %coupling_kernel.1 = (f32[1344,128]{1,0:T(8,128)S(1)}, f32[512,512]{1,0:T(8,128)S(1)}, f32[512,128]{1,0:T(8,128)S(1)}) custom-call(f32[1536,128]{1,0:T(8,128)S(1)} %all_gather.6.main_ref, f32[2048,128]{1,0:T(8,128)S(1)} %bitcast.10, f32[512,512]{1,0:T(8,128)S(1)} %get-tuple-element.25.lower_ref.flower_ref, f32[512,128]{1,0:T(8,128)S(1)} %get-tuple-element.26.pivot_ref), custom_call_target="tpu_custom_call" | custom-call | flops 4000000000 | bytes 4000000 | tf_op jit(solution)/shard_map/coupling_kernel/pallas_call | solution.py:539
  159.1 0.0 copy-start
  159.1 1.0 copy-done
  160.1 24.9 %all_to_all.56 = f32[8,168,128]{2,1,0:T(8,128)} all-to-all(f32[8,168,128]{2,1,0:T(8,128)S(1)} %bitcast.11), channel_id=1, replica_groups=mesh['y'=4,'core'=2,'x'=4,'z'=16] {'y','core'}, dimensions={0} | all-to-all | bytes 1376256 | tf_op jit(solution)/shard_map/all_to_all | solution.py:470
  184.9 0.0 copy-start.1
  184.9 1.2 reduce_sum.39
  186.2 0.0 copy-start.2
  186.2 14.3 %all_gather.7.g_ref = f32[1280,128]{1,0:T(8,128)S(1)} all-gather(f32[160,128]{1,0:T(8,128)S(1)} %slice_subtract_fusion), channel_id=1, replica_groups=mesh['y'=4,'core'=2,'x'=4,'z'=16] {'y','core'}, dimensions={0}, use_global_device_ids=true | all-gather | bytes 737280 | tf_op jit(solution)/shard_map/all_gather | solution.py:552
  200.6 0.0 copy-start.4
  200.6 0.0 copy-done.1
  200.6 0.0 copy-done.2
  200.6 0.7 copy-done.4
  201.2 19.0 %finish_kernel.1 = (f32[7,8]{1,0:T(8,128)}, f32[1,512]{1,0:T(1,128)}, f32[1,512]{1,0:T(1,128)}) custom-call(f32[1280,128]{1,0:T(8,128)S(1)} %all_gather.7.g_ref, f32[8,128]{1,0:T(8,128)S(1)} %slice.23.v_ref, f32[1536,128]{1,0:T(8,128)S(1)} %all_gather.6.main_ref, f32[8,1024]{1,0:T(8,128)S(1)} %copy-done.3, ...), custom_call_target="tpu_custom_call" | custom-call | flops 20000000000 | bytes 4000000 | tf_op jit(solution)/shard_map/finish_kernel/pallas_call | solution.py:553
  (9 shorter events, 0.2 us)
Async XLA Ops:
  7.2 48.2 %reduce-scatter.2.cloned.1.call-start = ((), (), s32[]{:S(2)}) async-start(), calls=%async_computation.7 | async-start | bytes 1310720 | tf_op jit(solution)/shard_map/reduce_scatter | solution.py:524
  13.7 21.6 %all-to-all-start = ((f32[8,168,128]{2,1,0:T(8,128)}), f32[8,168,128]{2,1,0:T(8,128)S(1)}, u32[]{:S(2)}, u32[]{:S(2)}) async-start(f32[8,168,128]{2,1,0:T(8,128)} %bitcast.3), calls=%async_computation | async-start | bytes 1376256 | tf_op jit(solution)/shard_map/all_to_all | solution.py:470
  24.1 11.3 %copy-start.5 = (f32[1288,128]{1,0:T(8,128)S(1)}, f32[1288,128]{1,0:T(8,128)}, u32[]{:S(2)}) copy-start(f32[1288,128]{1,0:T(8,128)} %get-tuple-element.19) | copy-start | bytes 1978372
  133.2 3.8 %copy-start.3 = (f32[8,1024]{1,0:T(8,128)S(1)}, f32[8,1024]{1,0:T(8,128)}, u32[]{:S(2)}) copy-start(f32[8,1024]{1,0:T(8,128)} %get-tuple-element.24.prior_ref) | copy-start | bytes 98308
  133.2 20.5 %all-to-all-start.4 = ((f32[4,512,128]{2,1,0:T(8,128)}), f32[4,512,128]{2,1,0:T(8,128)S(1)}, u32[]{:S(2)}, u32[]{:S(2)}) async-start(f32[4,512,128]{2,1,0:T(8,128)} %broadcast_in_dim.29), calls=%async_computation.5 | async-start | bytes 2097152 | tf_op jit(solution)/shard_map/all_to_all | solution.py:476
  159.1 1.0 copy-start
  184.9 15.6 %copy-start.1 = (f32[512,512]{1,0:T(8,128)S(1)}, f32[512,512]{1,0:T(8,128)}, u32[]{:S(2)}) copy-start(f32[512,512]{1,0:T(8,128)} %copy-done) | copy-start | bytes 3145732
  186.2 14.4 %copy-start.2 = (f32[64,1024]{1,0:T(8,128)S(1)}, f32[64,1024]{1,0:T(8,128)}, u32[]{:S(2)}) copy-start(f32[64,1024]{1,0:T(8,128)} %get-tuple-element.30.red_ref) | copy-start | bytes 786436
  200.6 0.7 copy-start.4
Sparse Core Ops, SparseCore 0:
  13.9 40.3 reduce-scatter.1

commit v5 on v4

--- a/solution.py
+++ b/solution.py
@@ -250,7 +250,7 @@
         for k in range(0, 8, 2):
             c0, c1 = columns[k], columns[k + 1]
             a, b, c = spread(c0, k), spread(c1, k), spread(c1, k + 1)
-            q = 1.0 / (a * c - b * b)
+            q = pltpu.reciprocal(a * c - b * b, approx=True)
             pa, pb, pc = c * q, b * q, a * q
             s0, s1 = sub == k, sub == k + 1
             m0, m1 = col == base + k, col == base + k + 1
@@ -281,12 +281,19 @@
     lax.fori_loop(0, PB // 8, group, 0)
 
 
+def halves(value):
+    first = value.astype(bf16)
+    return first, (value - first.astype(f32)).astype(bf16)
+
+
 def split_product(a, b):
-    a0, a1, a2 = pieces(a)
-    b0, b1, b2 = pieces(b)
-    left = jnp.concatenate([a0, a0, a1, a1, a0, a2], axis=0)
-    right = jnp.concatenate([b0, b1, b0, b1, b2, b0], axis=0)
-    return tn(left, right)
+    a0, a1 = halves(a)
+    b0, b1 = halves(b)
+    return tn(jnp.concatenate([a0, a0, a1], axis=0), jnp.concatenate([b0, b1, b0], axis=0))
+
+
+def three(dot, a, b):
+    return dot(a[0], b[0]) + (dot(a[0], b[1]) + dot(a[1], b[0]))
 
 
 def eliminate(a, packed, lower_ref, pivot_ref):
@@ -368,24 +375,29 @@
     eliminate(a, packed, lower_ref, pivot_ref)
 
 
-def coupling_kernel(main_ref, rg_ref, lower_ref, pivot_ref, out_ref, scaled_ref, q_ref, b, u, w):
+def coupling_kernel(main_ref, rg_ref, lower_ref, pivot_ref, out_ref, scaled_ref, q_ref, b0, b1, u0, u1, w0, w1):
     width = NBLK * NB
     for c in range(NBLK):
-        b[:, c * NB : (c + 1) * NB] = rg_ref[c * width : (c + 1) * width, :]
-    b[:, width:] = jnp.zeros((width, NB), f32)
-    for i in range(NBLK):
-        b[i * NB : (i + 1) * NB, width : width + 8] = turn(main_ref[TRI + i : TRI + i + 1, :])
+        lanes = slice(c * NB, (c + 1) * NB)
+        b0[:, lanes], b1[:, lanes] = halves(rg_ref[c * width : (c + 1) * width, :])
+        column = turn(main_ref[TRI + c : TRI + c + 1, :])
+        column = jnp.concatenate([column, jnp.zeros((NB, NB - 8), f32)], axis=1)
+        b0[lanes, width:], b1[lanes, width:] = halves(column)
     for i in range(NBLK):
         rows = slice(i * NB, (i + 1) * NB)
-        value = nn(lower_ref[rows, : (i + 1) * NB], b[: (i + 1) * NB, :], HIGHEST)
-        u[rows, :] = value[:, :width]
-        w[rows, :] = nn(pivot_ref[rows, :], value, HIGHEST)
-    scaled_ref[...] = w[:, :width]
-    q_ref[...] = w[:, width:]
+        depth = slice(0, (i + 1) * NB)
+        value = three(nn, halves(lower_ref[rows, depth]), (b0[depth, :], b1[depth, :]))
+        parts = halves(value)
+        u0[rows, :], u1[rows, :] = parts[0][:, :width], parts[1][:, :width]
+        value = three(nn, halves(pivot_ref[rows, :]), parts)
+        scaled_ref[rows, :] = value[:, :width]
+        q_ref[rows, :] = value[:, width:]
+        w0[rows, :], w1[rows, :] = halves(value)
     sub = lax.broadcasted_iota(jnp.int32, (8, NB), 0)
     tail = jnp.zeros((8, NB), f32)
     for i in range(NBLK):
-        value = tn(u[:, i * NB : (i + 1) * NB], w[:, i * NB :], HIGHEST)
+        lanes = slice(i * NB, (i + 1) * NB)
+        value = three(tn, (u0[:, lanes], u1[:, lanes]), (w0[:, i * NB :], w1[:, i * NB :]))
         for j in range(i, NBLK):
             store_split(out_ref, SLOT[i, j], value[:, (j - i) * NB : (j - i + 1) * NB])
         line = TRI + NBLK + i
@@ -440,25 +452,44 @@
         local_ref[i : i + 1, :] = jnp.sum(jnp.where(sub == lane, found[i], 0.0), axis=0, keepdims=True)
 
 
+def join_kernel(parts_ref, rest_ref, out_ref, total, sems):
+    parts = total.shape[0]
+    aside = pltpu.make_async_copy(rest_ref, out_ref.at[pl.ds(parts, rest_ref.shape[0])], sems.at[0])
+    aside.start()
+    total[...] = jnp.sum(parts_ref[...], axis=0)
+    copy = pltpu.make_async_copy(total, out_ref.at[pl.ds(0, parts)], sems.at[1])
+    copy.start()
+    copy.wait()
+    aside.wait()
+
+
+def sum_kernel(parts_ref, out_ref, total, sem):
+    total[...] = jnp.sum(parts_ref[...], axis=0)
+    copy = pltpu.make_async_copy(total, out_ref, sem)
+    copy.start()
+    copy.wait()
+
+
 def shape(*dims, dtype=f32):
     return jax.ShapeDtypeStruct(dims, dtype)
 
 
 VMEM = pl.BlockSpec(memory_space=pltpu.VMEM)
 SMEM = pl.BlockSpec(memory_space=pltpu.SMEM)
+HBM = pl.BlockSpec(memory_space=pltpu.HBM)
 
 
 def whole_block(dims):
     return pl.BlockSpec(dims, lambda i: (0,) * len(dims))
 
 
-def call(kernel, out_shape, scratch, specs, flops, grid=(), limit=16):
+def call(kernel, out_shape, scratch, specs, flops, grid=(), limit=16, out=VMEM):
     return pl.pallas_call(
         kernel,
         grid=grid,
         out_shape=out_shape,
         in_specs=specs,
-        out_specs=[VMEM] * len(out_shape),
+        out_specs=[out] * len(out_shape),
         scratch_shapes=scratch,
         name=kernel.__name__,
         compiler_params=pltpu.CompilerParams(vmem_limit_bytes=limit * 1024 * 1024),
@@ -523,9 +554,30 @@
     share = part_sums(gg, GROUPS, REG_PARTS)
     rg = lax.psum_scatter(rg, "x", scatter_dimension=0, tiled=True)
     main = jnp.concatenate([main, share, jnp.zeros((MAIN_ROWS - SUM_AT - PART_ROWS, NB), f32)], axis=0)
-    main = part_sums(main, "x", nx)
-    both = part_sums(jnp.concatenate([main, rg], axis=0), "z", nz)
-    both = copies_back(both, "z", nz)
+    main = lax.all_to_all(main, "x", 0, 0, tiled=True).reshape(nx, -1, NB)
+    count = main.shape[1] + rg.shape[0]
+    both = call(
+        join_kernel,
+        [shape(count, NB)],
+        [pltpu.VMEM(main.shape[1:], f32), pltpu.SemaphoreType.DMA((2,))],
+        [whole_block(main.shape), HBM],
+        1_000_000,
+        grid=(1,),
+        limit=60,
+        out=HBM,
+    )(main, rg)[0]
+    both = lax.all_to_all(both, "z", 0, 0, tiled=True).reshape(nz, -1, NB)
+    both = call(
+        sum_kernel,
+        [shape(*both.shape[1:])],
+        [pltpu.VMEM(both.shape[1:], f32), pltpu.SemaphoreType.DMA],
+        [whole_block(both.shape)],
+        1_000_000,
+        grid=(1,),
+        limit=60,
+        out=HBM,
+    )(both)[0]
+    both = lax.all_gather(both, "z", axis=0, tiled=True)
     main = lax.all_gather(both[: MAIN_ROWS // nx], "x", axis=0, tiled=True)
     main, rg = lax.optimization_barrier((main, both[MAIN_ROWS // nx :]))
     rg = copies_back(rg, "x", nx)
@@ -540,9 +592,12 @@
         coupling_kernel,
         [shape(REG_PARTS * PART_ROWS, NB), shape(width, width), shape(width, NB)],
         [
-            pltpu.VMEM((width, width + NB), f32),
-            pltpu.VMEM((width, width), f32),
-            pltpu.VMEM((width, width + NB), f32),
+            pltpu.VMEM((width, width + NB), bf16),
+            pltpu.VMEM((width, width + NB), bf16),
+            pltpu.VMEM((width, width), bf16),
+            pltpu.VMEM((width, width), bf16),
+            pltpu.VMEM((width, width + NB), bf16),
+            pltpu.VMEM((width, width + NB), bf16),
         ],
         [VMEM] * 4,
         4_000_000_000,

time: 228 us -> 239 us (1.048)
  Pallas kernels: 47.6 us -> 55.7 us
  blocking collectives: 135 us -> 139 us
    all_to_all x3 -> x1, blocking collectives: 77.1 us -> 33.4 us  [part_sums(): moved = lax.all_to_all(value, axis, 0, 0, tiled=True)]
    all_gather x0 -> x1, blocking collectives: none -> 27.9 us  [body(): both = lax.all_gather(both, 'z', axis=0, tiled=True)]
    all_to_all x1 -> x2, blocking collectives: 32.3 us -> 52.7 us  [the longest x1 32.6 us: body(): both = lax.all_to_all(both, 'z', 0, 0, tiled=True).reshape(nz, -1, NB)]
    pallas_call x0 -> x2, Pallas kernels: none -> 11.8 us  [the longest x1 10.2 us: body(): call(join_kernel, [shape(count, NB)], [pltpu.VMEM(main.shape[1:], f32), p...]
where the time goes in v5:
time: 239 us; the launch traced here: 238 us
  blocking collectives  139 us (58%)
  Pallas kernels  55.7 us (23%)
  between operations  14.1 us (6%)
  starting transfers between devices  14 us (6%)
  waiting for transfers between devices  11.2 us (5%)
  local copies, waits for them, and re-layouts  2.82 us (1%)
    all_to_all x1, blocking collectives, part_sums(): moved = lax.all_to_all(value, axis, 0, 0, tiled=True)  33.4 us
    all_to_all x1, blocking collectives, body(): both = lax.all_to_all(both, 'z', 0, 0, tiled=True).reshape(nz, -1, NB)  32.6 us
    all_gather x1, blocking collectives, body(): both = lax.all_gather(both, 'z', axis=0, tiled=True)  27.9 us
    all_to_all x1, blocking collectives, body(): main = lax.all_to_all(main, 'x', 0, 0, tiled=True).reshape(nx, -1, NB)  20 us
    pallas_call x1, Pallas kernels, body(): call(finish_kernel, [shape(nparams, 8), shape(1, width), shape(1, width)]...  18.2 us
    pallas_call x1, Pallas kernels, body(): call(regional_kernel, [shape(width, width), shape(width, NB)], [pltpu.VME...  15.8 us
    all_gather x1, blocking collectives, body(): matrix = lax.all_gather(mine, GROUPS, axis=0, tiled=True)  14.3 us
    all_to_all x1, waiting for transfers between devices, part_sums(): moved = lax.all_to_all(value, axis, 0, 0, tiled=True)  11.2 us
  transfers between devices with their start and end apart: 3, of which 1 were waited for; matrix products, arithmetic and copies ran while one was open for 0% of the time, Pallas kernels for 7%

profile of v5, /device:TPU:1, one launch (start us, length us, event | category | flops | bytes accessed | tf_op | source)
XLA Modules:
  0.0 238.1 jit_solution(11422912870933755953)
XLA Ops:
  7.2 0.0 reduce-scatter.2.cloned.1.call-start
  7.2 6.5 %assemble_kernel.1 = (f32[1344,128]{1,0:T(8,128)}, f32[1288,128]{1,0:T(8,128)}, f32[2048,128]{1,0:T(8,128)}, f32[64,1024]{1,0:T(8,128)}, f32[8,128]{1,0:T(8,128)}, /*index=5*/f32[8,1024]{1,0:T(8,128)}) custom-call(bf16[7,480]{1,0:T(8,128)(2,1)} %lj_ref.1, bf16[480,512]{1,0:T(8,128)(2,1)} %gj_ref.1, s32[4,480]{1,0:T(4,128)} %ci_ref.1, bf16[4,480]{1,0:T(4,128)(2,1)} %cw_ref.1, ...), custom_call_target="tpu_custom_call" | custom-call | flops 2000000000 | bytes 4000000 | tf_op jit(solution)/shard_map/assemble_kernel/pallas_call | solution.py:527
  13.7 0.0 reduce-scatter.2.cloned.1.call-update
  13.7 10.3 %all-to-all-start = ((f32[8,168,128]{2,1,0:T(8,128)}), f32[8,168,128]{2,1,0:T(8,128)S(1)}, u32[]{:S(2)}, u32[]{:S(2)}) async-start(f32[8,168,128]{2,1,0:T(8,128)} %bitcast.3), calls=%async_computation | async-start | bytes 1376256 | tf_op jit(solution)/shard_map/all_to_all | solution.py:501
  24.1 0.0 copy-start.5
  24.1 0.1 pad.2.clone
  24.2 11.2 %all-to-all-done = f32[8,168,128]{2,1,0:T(8,128)S(1)} async-done(((f32[8,168,128]{2,1,0:T(8,128)}), f32[8,168,128]{2,1,0:T(8,128)S(1)}, u32[]{:S(2)}, u32[]{:S(2)}) %all-to-all-start) | async-done | bytes 688160 | tf_op jit(solution)/shard_map/all_to_all | solution.py:501
  35.4 0.0 copy-done.5
  35.4 0.3 maximum_maximum_fusion
  35.6 20.0 %all_to_all.44.parts_ref = f32[4,384,128]{2,1,0:T(8,128)} all-to-all(f32[4,384,128]{2,1,0:T(8,128)S(1)} %bitcast.11), channel_id=1, replica_groups=mesh['y'=4,'core'=2,'x'=4,'z'=16] {'x'}, dimensions={0} | all-to-all | bytes 1572864 | tf_op jit(solution)/shard_map/all_to_all | solution.py:557
  55.7 0.0 reduce-scatter.2.cloned.1.call-done.rest_ref
  55.7 10.2 %join_kernel.1 = f32[896,128]{1,0:T(8,128)} custom-call(f32[4,384,128]{2,1,0:T(8,128)} %all_to_all.44.parts_ref, f32[512,128]{1,0:T(8,128)} %reduce-scatter.2.cloned.1.call-done.rest_ref), custom_call_target="tpu_custom_call" | custom-call | flops 1000000 | bytes 4000000 | tf_op jit(solution)/shard_map/join_kernel/pallas_call | solution.py:559
  65.9 32.6 %all_to_all.45.parts_ref = f32[16,56,128]{2,1,0:T(8,128)} all-to-all(f32[16,56,128]{2,1,0:T(8,128)} %bitcast.12), channel_id=1, replica_groups=mesh['y'=4,'core'=2,'x'=4,'z'=16] {'z'}, dimensions={0} | all-to-all | bytes 917504 | tf_op jit(solution)/shard_map/all_to_all | solution.py:569
  98.5 1.7 sum_kernel.1
  100.2 27.9 %all_gather.9 = f32[896,128]{1,0:T(8,128)S(1)} all-gather(f32[56,128]{1,0:T(8,128)} %sum_kernel.1), channel_id=1, replica_groups=mesh['y'=4,'core'=2,'x'=4,'z'=16] {'z'}, dimensions={0}, use_global_device_ids=true | all-gather | bytes 487424 | tf_op jit(solution)/shard_map/all_gather | solution.py:580
  128.1 10.4 %all_gather.10.main_ref = f32[1536,128]{1,0:T(8,128)S(1)} all-gather(f32[384,128]{1,0:T(8,128)S(1)} %slice.20), channel_id=1, replica_groups=mesh['y'=4,'core'=2,'x'=4,'z'=16] {'x'}, dimensions={0}, use_global_device_ids=true | all-gather | bytes 983040 | tf_op jit(solution)/shard_map/all_gather | solution.py:581
  138.6 1.0 broadcast_in_dim.22
  139.6 0.0 copy-start.3
  139.6 3.6 %all-to-all-start.3 = ((f32[4,512,128]{2,1,0:T(8,128)}), f32[4,512,128]{2,1,0:T(8,128)S(1)}, u32[]{:S(2)}, u32[]{:S(2)}) async-start(f32[4,512,128]{2,1,0:T(8,128)} %broadcast_in_dim.22), calls=%async_computation.4 | async-start | bytes 2097152 | tf_op jit(solution)/shard_map/all_to_all | solution.py:507
  143.3 0.0 copy-done.3
  143.3 15.8 %regional_kernel.1 = (f32[512,512]{1,0:T(8,128)S(1)}, f32[512,128]{1,0:T(8,128)S(1)}) custom-call(f32[1536,128]{1,0:T(8,128)S(1)} %all_gather.10.main_ref, f32[8,1024]{1,0:T(8,128)S(1)} %copy-done.3), custom_call_target="tpu_custom_call" | custom-call | flops 20000000000 | bytes 4000000 | tf_op jit(solution)/shard_map/regional_kernel/pallas_call | solution.py:584
  159.1 0.0 all-to-all-done.3
  159.1 3.3 %coupling_kernel.1 = (f32[1344,128]{1,0:T(8,128)S(1)}, f32[512,512]{1,0:T(8,128)S(1)}, f32[512,128]{1,0:T(8,128)S(1)}) custom-call(f32[1536,128]{1,0:T(8,128)S(1)} %all_gather.10.main_ref, f32[2048,128]{1,0:T(8,128)S(1)} %bitcast.9, f32[512,512]{1,0:T(8,128)S(1)} %get-tuple-element.25.lower_ref.flower_ref, f32[512,128]{1,0:T(8,128)S(1)} %get-tuple-element.26.pivot_ref), custom_call_target="tpu_custom_call" | custom-call | flops 4000000000 | bytes 4000000 | tf_op jit(solution)/shard_map/coupling_kernel/pallas_call | solution.py:591
  162.4 0.0 copy-start
  162.4 1.0 copy-done
  163.4 33.4 %all_to_all.46 = f32[8,168,128]{2,1,0:T(8,128)} all-to-all(f32[8,168,128]{2,1,0:T(8,128)S(1)} %bitcast.10), channel_id=1, replica_groups=mesh['y'=4,'core'=2,'x'=4,'z'=16] {'y','core'}, dimensions={0} | all-to-all | bytes 1376256 | tf_op jit(solution)/shard_map/all_to_all | solution.py:501
  196.8 0.0 copy-start.1
  196.8 1.2 reduce_sum.19
  198.0 0.0 copy-start.2
  198.1 14.3 %all_gather.11.g_ref = f32[1280,128]{1,0:T(8,128)S(1)} all-gather(f32[160,128]{1,0:T(8,128)S(1)} %slice_subtract_fusion), channel_id=1, replica_groups=mesh['y'=4,'core'=2,'x'=4,'z'=16] {'y','core'}, dimensions={0}, use_global_device_ids=true | all-gather | bytes 737280 | tf_op jit(solution)/shard_map/all_gather | solution.py:607
  212.4 0.0 copy-start.4
  212.4 0.0 copy-done.1
  212.4 0.0 copy-done.2
  212.4 0.7 copy-done.4
  213.0 18.2 %finish_kernel.1 = (f32[7,8]{1,0:T(8,128)}, f32[1,512]{1,0:T(1,128)}, f32[1,512]{1,0:T(1,128)}) custom-call(f32[1280,128]{1,0:T(8,128)S(1)} %all_gather.11.g_ref, f32[8,128]{1,0:T(8,128)S(1)} %slice.23.v_ref, f32[1536,128]{1,0:T(8,128)S(1)} %all_gather.10.main_ref, f32[8,1024]{1,0:T(8,128)S(1)} %copy-done.3, ...), custom_call_target="tpu_custom_call" | custom-call | flops 20000000000 | bytes 4000000 | tf_op jit(solution)/shard_map/finish_kernel/pallas_call | solution.py:608
  (6 shorter events, 0.1 us)
Async XLA Ops:
  7.2 48.5 %reduce-scatter.2.cloned.1.call-start = ((), (), s32[]{:S(2)}) async-start(), calls=%async_computation.6 | async-start | bytes 1310720 | tf_op jit(solution)/shard_map/reduce_scatter | solution.py:555
  13.7 21.6 %all-to-all-start = ((f32[8,168,128]{2,1,0:T(8,128)}), f32[8,168,128]{2,1,0:T(8,128)S(1)}, u32[]{:S(2)}, u32[]{:S(2)}) async-start(f32[8,168,128]{2,1,0:T(8,128)} %bitcast.3), calls=%async_computation | async-start | bytes 1376256 | tf_op jit(solution)/shard_map/all_to_all | solution.py:501
  24.1 11.3 %copy-start.5 = (f32[1288,128]{1,0:T(8,128)S(1)}, f32[1288,128]{1,0:T(8,128)}, u32[]{:S(2)}) copy-start(f32[1288,128]{1,0:T(8,128)} %get-tuple-element.19) | copy-start | bytes 1978372
  139.6 3.7 %copy-start.3 = (f32[8,1024]{1,0:T(8,128)S(1)}, f32[8,1024]{1,0:T(8,128)}, u32[]{:S(2)}) copy-start(f32[8,1024]{1,0:T(8,128)} %get-tuple-element.24.prior_ref) | copy-start | bytes 98308
  139.6 19.5 %all-to-all-start.3 = ((f32[4,512,128]{2,1,0:T(8,128)}), f32[4,512,128]{2,1,0:T(8,128)S(1)}, u32[]{:S(2)}, u32[]{:S(2)}) async-start(f32[4,512,128]{2,1,0:T(8,128)} %broadcast_in_dim.22), calls=%async_computation.4 | async-start | bytes 2097152 | tf_op jit(solution)/shard_map/all_to_all | solution.py:507
  162.4 1.0 copy-start
  196.8 15.6 %copy-start.1 = (f32[512,512]{1,0:T(8,128)S(1)}, f32[512,512]{1,0:T(8,128)}, u32[]{:S(2)}) copy-start(f32[512,512]{1,0:T(8,128)} %copy-done) | copy-start | bytes 3145732
  198.0 14.3 %copy-start.2 = (f32[64,1024]{1,0:T(8,128)S(1)}, f32[64,1024]{1,0:T(8,128)}, u32[]{:S(2)}) copy-start(f32[64,1024]{1,0:T(8,128)} %get-tuple-element.30.red_ref) | copy-start | bytes 786436
  212.4 0.7 copy-start.4
Sparse Core Ops, SparseCore 0:
  13.9 40.2 reduce-scatter.1

commit v6 on v4

--- a/solution.py
+++ b/solution.py
@@ -289,6 +289,15 @@
     return tn(left, right)
 
 
+def halves(value):
+    first = value.astype(bf16)
+    return first, (value - first.astype(f32)).astype(bf16)
+
+
+def three(dot, a, b):
+    return dot(a[0], b[0]) + (dot(a[0], b[1]) + dot(a[1], b[0]))
+
+
 def eliminate(a, packed, lower_ref, pivot_ref):
     size = NBLK * NB
     lane = lax.broadcasted_iota(jnp.int32, (PB, size), 1)
@@ -368,24 +377,29 @@
     eliminate(a, packed, lower_ref, pivot_ref)
 
 
-def coupling_kernel(main_ref, rg_ref, lower_ref, pivot_ref, out_ref, scaled_ref, q_ref, b, u, w):
+def coupling_kernel(main_ref, rg_ref, lower_ref, pivot_ref, out_ref, scaled_ref, q_ref, b0, b1, u0, u1, w0, w1):
     width = NBLK * NB
     for c in range(NBLK):
-        b[:, c * NB : (c + 1) * NB] = rg_ref[c * width : (c + 1) * width, :]
-    b[:, width:] = jnp.zeros((width, NB), f32)
-    for i in range(NBLK):
-        b[i * NB : (i + 1) * NB, width : width + 8] = turn(main_ref[TRI + i : TRI + i + 1, :])
+        lanes = slice(c * NB, (c + 1) * NB)
+        b0[:, lanes], b1[:, lanes] = halves(rg_ref[c * width : (c + 1) * width, :])
+        column = turn(main_ref[TRI + c : TRI + c + 1, :])
+        column = jnp.concatenate([column, jnp.zeros((NB, NB - 8), f32)], axis=1)
+        b0[lanes, width:], b1[lanes, width:] = halves(column)
     for i in range(NBLK):
         rows = slice(i * NB, (i + 1) * NB)
-        value = nn(lower_ref[rows, : (i + 1) * NB], b[: (i + 1) * NB, :], HIGHEST)
-        u[rows, :] = value[:, :width]
-        w[rows, :] = nn(pivot_ref[rows, :], value, HIGHEST)
-    scaled_ref[...] = w[:, :width]
-    q_ref[...] = w[:, width:]
+        depth = slice(0, (i + 1) * NB)
+        value = three(nn, halves(lower_ref[rows, depth]), (b0[depth, :], b1[depth, :]))
+        parts = halves(value)
+        u0[rows, :], u1[rows, :] = parts[0][:, :width], parts[1][:, :width]
+        value = three(nn, halves(pivot_ref[rows, :]), parts)
+        scaled_ref[rows, :] = value[:, :width]
+        q_ref[rows, :] = value[:, width:]
+        w0[rows, :], w1[rows, :] = halves(value)
     sub = lax.broadcasted_iota(jnp.int32, (8, NB), 0)
     tail = jnp.zeros((8, NB), f32)
     for i in range(NBLK):
-        value = tn(u[:, i * NB : (i + 1) * NB], w[:, i * NB :], HIGHEST)
+        lanes = slice(i * NB, (i + 1) * NB)
+        value = three(tn, (u0[:, lanes], u1[:, lanes]), (w0[:, i * NB :], w1[:, i * NB :]))
         for j in range(i, NBLK):
             store_split(out_ref, SLOT[i, j], value[:, (j - i) * NB : (j - i + 1) * NB])
         line = TRI + NBLK + i
@@ -540,9 +554,12 @@
         coupling_kernel,
         [shape(REG_PARTS * PART_ROWS, NB), shape(width, width), shape(width, NB)],
         [
-            pltpu.VMEM((width, width + NB), f32),
-            pltpu.VMEM((width, width), f32),
-            pltpu.VMEM((width, width + NB), f32),
+            pltpu.VMEM((width, width + NB), bf16),
+            pltpu.VMEM((width, width + NB), bf16),
+            pltpu.VMEM((width, width), bf16),
+            pltpu.VMEM((width, width), bf16),
+            pltpu.VMEM((width, width + NB), bf16),
+            pltpu.VMEM((width, width + NB), bf16),
         ],
         [VMEM] * 4,
         4_000_000_000,

time: 228 us -> 225 us (0.987)
  no operation moved by 1% of the time
where the time goes in v6:
time: 225 us
  blocking collectives  134 us (60%)
  Pallas kernels  45.5 us (20%)
  starting transfers between devices  14.2 us (6%)
  between operations  14.1 us (6%)
  waiting for transfers between devices  11.2 us (5%)
  local copies, waits for them, and re-layouts  2.86 us (1%)
  other arithmetic  2.6 us (1%)
    all_to_all x3, blocking collectives, part_sums(): moved = lax.all_to_all(value, axis, 0, 0, tiled=True)  77.1 us
    all_to_all x1, blocking collectives, copies_back(): return lax.all_to_all(copies, axis, 0, 0, tiled=True)  32.3 us
    pallas_call x1, Pallas kernels, body(): call(finish_kernel, [shape(nparams, 8), shape(1, width), shape(1, width)]...  19 us
    pallas_call x1, Pallas kernels, body(): call(regional_kernel, [shape(width, width), shape(width, NB)], [pltpu.VME...  16.7 us
    all_gather x1, blocking collectives, body(): matrix = lax.all_gather(mine, GROUPS, axis=0, tiled=True)  14.1 us
    all_to_all x1, waiting for transfers between devices, part_sums(): moved = lax.all_to_all(value, axis, 0, 0, tiled=True)  11.2 us
    all_gather x1, blocking collectives, body(): main = lax.all_gather(both[:MAIN_ROWS // nx], 'x', axis=0, tiled=True)  10.7 us
    all_to_all x1, starting transfers between devices, part_sums(): moved = lax.all_to_all(value, axis, 0, 0, tiled=True)  10.3 us
  transfers between devices with their start and end apart: 3, of which 1 were waited for; matrix products, arithmetic and copies ran while one was open for 0% of the time, Pallas kernels for 7%

profile of v6, /device:TPU:1, one launch (start us, length us, event | category | flops | bytes accessed | tf_op | source)
XLA Modules:
  0.0 224.8 jit_solution(17224959179694547733)
XLA Ops:
  7.2 0.0 reduce-scatter.2.cloned.1.call-start
  7.2 6.5 %assemble_kernel.1 = (f32[1344,128]{1,0:T(8,128)}, f32[1288,128]{1,0:T(8,128)}, f32[2048,128]{1,0:T(8,128)}, f32[64,1024]{1,0:T(8,128)}, f32[8,128]{1,0:T(8,128)}, /*index=5*/f32[8,1024]{1,0:T(8,128)}) custom-call(bf16[7,480]{1,0:T(8,128)(2,1)} %lj_ref.1, bf16[480,512]{1,0:T(8,128)(2,1)} %gj_ref.1, s32[4,480]{1,0:T(4,128)} %ci_ref.1, bf16[4,480]{1,0:T(4,128)(2,1)} %cw_ref.1, ...), custom_call_target="tpu_custom_call" | custom-call | flops 2000000000 | bytes 4000000 | tf_op jit(solution)/shard_map/assemble_kernel/pallas_call | solution.py:510
  13.7 0.0 reduce-scatter.2.cloned.1.call-update
  13.7 10.3 %all-to-all-start = ((f32[8,168,128]{2,1,0:T(8,128)}), f32[8,168,128]{2,1,0:T(8,128)S(1)}, u32[]{:S(2)}, u32[]{:S(2)}) async-start(f32[8,168,128]{2,1,0:T(8,128)} %bitcast.3), calls=%async_computation | async-start | bytes 1376256 | tf_op jit(solution)/shard_map/all_to_all | solution.py:484
  24.1 0.0 copy-start.5
  24.1 0.1 pad.4.clone
  24.2 11.2 %all-to-all-done = f32[8,168,128]{2,1,0:T(8,128)S(1)} async-done(((f32[8,168,128]{2,1,0:T(8,128)}), f32[8,168,128]{2,1,0:T(8,128)S(1)}, u32[]{:S(2)}, u32[]{:S(2)}) %all-to-all-start) | async-done | bytes 688160 | tf_op jit(solution)/shard_map/all_to_all | solution.py:484
  35.4 0.0 copy-done.5
  35.4 0.3 maximum_maximum_fusion
  35.7 19.7 %all_to_all.53 = f32[4,384,128]{2,1,0:T(8,128)S(1)} all-to-all(f32[4,384,128]{2,1,0:T(8,128)S(1)} %bitcast.12), channel_id=1, replica_groups=mesh['y'=4,'core'=2,'x'=4,'z'=16] {'x'}, dimensions={0} | all-to-all | bytes 1572864 | tf_op jit(solution)/shard_map/all_to_all | solution.py:484
  55.4 0.0 reduce-scatter.2.cloned.1.call-done
  55.4 1.0 pad_maximum_fusion
  56.4 32.6 %all_to_all.54 = f32[16,56,128]{2,1,0:T(8,128)S(1)} all-to-all(f32[16,56,128]{2,1,0:T(8,128)S(1)} %bitcast.13), channel_id=1, replica_groups=mesh['y'=4,'core'=2,'x'=4,'z'=16] {'z'}, dimensions={0} | all-to-all | bytes 917504 | tf_op jit(solution)/shard_map/all_to_all | solution.py:484
  89.0 32.3 %all_to_all.55 = f32[16,56,128]{2,1,0:T(8,128)S(1)} all-to-all(f32[16,56,128]{2,1,0:T(8,128)S(1)} %broadcast_in_dim.28), channel_id=1, replica_groups=mesh['y'=4,'core'=2,'x'=4,'z'=16] {'z'}, dimensions={0} | all-to-all | bytes 917504 | tf_op jit(solution)/shard_map/all_to_all | solution.py:490
  121.4 10.7 %all_gather.6.main_ref = f32[1536,128]{1,0:T(8,128)S(1)} all-gather(f32[384,128]{1,0:T(8,128)S(1)} %slice.20), channel_id=1, replica_groups=mesh['y'=4,'core'=2,'x'=4,'z'=16] {'x'}, dimensions={0}, use_global_device_ids=true | all-gather | bytes 983040 | tf_op jit(solution)/shard_map/all_gather | solution.py:543
  132.1 1.0 broadcast_in_dim.29
  133.2 0.0 copy-start.3
  133.2 3.8 %all-to-all-start.4 = ((f32[4,512,128]{2,1,0:T(8,128)}), f32[4,512,128]{2,1,0:T(8,128)S(1)}, u32[]{:S(2)}, u32[]{:S(2)}) async-start(f32[4,512,128]{2,1,0:T(8,128)} %broadcast_in_dim.29), calls=%async_computation.5 | async-start | bytes 2097152 | tf_op jit(solution)/shard_map/all_to_all | solution.py:490
  137.0 0.0 copy-done.3
  137.0 16.7 %regional_kernel.1 = (f32[512,512]{1,0:T(8,128)S(1)}, f32[512,128]{1,0:T(8,128)S(1)}) custom-call(f32[1536,128]{1,0:T(8,128)S(1)} %all_gather.6.main_ref, f32[8,1024]{1,0:T(8,128)S(1)} %copy-done.3), custom_call_target="tpu_custom_call" | custom-call | flops 20000000000 | bytes 4000000 | tf_op jit(solution)/shard_map/regional_kernel/pallas_call | solution.py:546
  153.7 0.0 all-to-all-done.4
  153.7 3.3 %coupling_kernel.1 = (f32[1344,128]{1,0:T(8,128)S(1)}, f32[512,512]{1,0:T(8,128)S(1)}, f32[512,128]{1,0:T(8,128)S(1)}) custom-call(f32[1536,128]{1,0:T(8,128)S(1)} %all_gather.6.main_ref, f32[2048,128]{1,0:T(8,128)S(1)} %bitcast.10, f32[512,512]{1,0:T(8,128)S(1)} %get-tuple-element.25.lower_ref.flower_ref, f32[512,128]{1,0:T(8,128)S(1)} %get-tuple-element.26.pivot_ref), custom_call_target="tpu_custom_call" | custom-call | flops 4000000000 | bytes 4000000 | tf_op jit(solution)/shard_map/coupling_kernel/pallas_call | solution.py:553
  157.0 0.0 copy-start
  157.0 1.0 copy-done
  158.0 24.9 %all_to_all.56 = f32[8,168,128]{2,1,0:T(8,128)} all-to-all(f32[8,168,128]{2,1,0:T(8,128)S(1)} %bitcast.11), channel_id=1, replica_groups=mesh['y'=4,'core'=2,'x'=4,'z'=16] {'y','core'}, dimensions={0} | all-to-all | bytes 1376256 | tf_op jit(solution)/shard_map/all_to_all | solution.py:484
  182.8 0.0 copy-start.1
  182.8 1.2 reduce_sum.39
  184.1 0.0 copy-start.2
  184.1 14.1 %all_gather.7.g_ref = f32[1280,128]{1,0:T(8,128)S(1)} all-gather(f32[160,128]{1,0:T(8,128)S(1)} %slice_subtract_fusion), channel_id=1, replica_groups=mesh['y'=4,'core'=2,'x'=4,'z'=16] {'y','core'}, dimensions={0}, use_global_device_ids=true | all-gather | bytes 737280 | tf_op jit(solution)/shard_map/all_gather | solution.py:569
  198.2 0.0 copy-start.4
  198.2 0.0 copy-done.1
  198.2 0.0 copy-done.2
  198.2 0.7 copy-done.4
  198.9 19.0 %finish_kernel.1 = (f32[7,8]{1,0:T(8,128)}, f32[1,512]{1,0:T(1,128)}, f32[1,512]{1,0:T(1,128)}) custom-call(f32[1280,128]{1,0:T(8,128)S(1)} %all_gather.7.g_ref, f32[8,128]{1,0:T(8,128)S(1)} %slice.23.v_ref, f32[1536,128]{1,0:T(8,128)S(1)} %all_gather.6.main_ref, f32[8,1024]{1,0:T(8,128)S(1)} %copy-done.3, ...), custom_call_target="tpu_custom_call" | custom-call | flops 20000000000 | bytes 4000000 | tf_op jit(solution)/shard_map/finish_kernel/pallas_call | solution.py:570
  (9 shorter events, 0.2 us)
Async XLA Ops:
  7.2 48.2 %reduce-scatter.2.cloned.1.call-start = ((), (), s32[]{:S(2)}) async-start(), calls=%async_computation.7 | async-start | bytes 1310720 | tf_op jit(solution)/shard_map/reduce_scatter | solution.py:538
  13.7 21.6 %all-to-all-start = ((f32[8,168,128]{2,1,0:T(8,128)}), f32[8,168,128]{2,1,0:T(8,128)S(1)}, u32[]{:S(2)}, u32[]{:S(2)}) async-start(f32[8,168,128]{2,1,0:T(8,128)} %bitcast.3), calls=%async_computation | async-start | bytes 1376256 | tf_op jit(solution)/shard_map/all_to_all | solution.py:484
  24.1 11.3 %copy-start.5 = (f32[1288,128]{1,0:T(8,128)S(1)}, f32[1288,128]{1,0:T(8,128)}, u32[]{:S(2)}) copy-start(f32[1288,128]{1,0:T(8,128)} %get-tuple-element.19) | copy-start | bytes 1978372
  133.2 3.8 %copy-start.3 = (f32[8,1024]{1,0:T(8,128)S(1)}, f32[8,1024]{1,0:T(8,128)}, u32[]{:S(2)}) copy-start(f32[8,1024]{1,0:T(8,128)} %get-tuple-element.24.prior_ref) | copy-start | bytes 98308
  133.2 20.5 %all-to-all-start.4 = ((f32[4,512,128]{2,1,0:T(8,128)}), f32[4,512,128]{2,1,0:T(8,128)S(1)}, u32[]{:S(2)}, u32[]{:S(2)}) async-start(f32[4,512,128]{2,1,0:T(8,128)} %broadcast_in_dim.29), calls=%async_computation.5 | async-start | bytes 2097152 | tf_op jit(solution)/shard_map/all_to_all | solution.py:490
  157.0 1.0 copy-start
  182.8 15.4 %copy-start.1 = (f32[512,512]{1,0:T(8,128)S(1)}, f32[512,512]{1,0:T(8,128)}, u32[]{:S(2)}) copy-start(f32[512,512]{1,0:T(8,128)} %copy-done) | copy-start | bytes 3145732
  184.1 14.1 %copy-start.2 = (f32[64,1024]{1,0:T(8,128)S(1)}, f32[64,1024]{1,0:T(8,128)}, u32[]{:S(2)}) copy-start(f32[64,1024]{1,0:T(8,128)} %get-tuple-element.30.red_ref) | copy-start | bytes 786436
  198.2 0.7 copy-start.4
Sparse Core Ops, SparseCore 0:
  13.9 40.3 reduce-scatter.1

commit v7 on v6

--- a/solution.py
+++ b/solution.py
@@ -281,17 +281,15 @@
     lax.fori_loop(0, PB // 8, group, 0)
 
 
-def split_product(a, b):
-    a0, a1, a2 = pieces(a)
-    b0, b1, b2 = pieces(b)
-    left = jnp.concatenate([a0, a0, a1, a1, a0, a2], axis=0)
-    right = jnp.concatenate([b0, b1, b0, b1, b2, b0], axis=0)
-    return tn(left, right)
-
-
 def halves(value):
     first = value.astype(bf16)
     return first, (value - first.astype(f32)).astype(bf16)
+
+
+def split_product(a, b):
+    a0, a1 = halves(a)
+    b0, b1 = halves(b)
+    return tn(jnp.concatenate([a0, a0, a1], axis=0), jnp.concatenate([b0, b1, b0], axis=0))
 
 
 def three(dot, a, b):

time: 225 us -> 224 us (level)
  no operation moved by 1% of the time
where the time goes in v7:
time: 224 us; the launch traced here: 223 us
  blocking collectives  134 us (60%)
  Pallas kernels  43.8 us (20%)
  between operations  14.1 us (6%)
  starting transfers between devices  14 us (6%)
  waiting for transfers between devices  11.2 us (5%)
  local copies, waits for them, and re-layouts  2.86 us (1%)
  other arithmetic  2.6 us (1%)
    all_to_all x3, blocking collectives, part_sums(): moved = lax.all_to_all(value, axis, 0, 0, tiled=True)  77.1 us
    all_to_all x1, blocking collectives, copies_back(): return lax.all_to_all(copies, axis, 0, 0, tiled=True)  32.3 us
    pallas_call x1, Pallas kernels, body(): call(finish_kernel, [shape(nparams, 8), shape(1, width), shape(1, width)]...  18.2 us
    pallas_call x1, Pallas kernels, body(): call(regional_kernel, [shape(width, width), shape(width, NB)], [pltpu.VME...  15.8 us
    all_gather x1, blocking collectives, body(): matrix = lax.all_gather(mine, GROUPS, axis=0, tiled=True)  14.3 us
    all_to_all x1, waiting for transfers between devices, part_sums(): moved = lax.all_to_all(value, axis, 0, 0, tiled=True)  11.2 us
    all_gather x1, blocking collectives, body(): main = lax.all_gather(both[:MAIN_ROWS // nx], 'x', axis=0, tiled=True)  10.7 us
    all_to_all x1, starting transfers between devices, part_sums(): moved = lax.all_to_all(value, axis, 0, 0, tiled=True)  10.3 us
  transfers between devices with their start and end apart: 3, of which 1 were waited for; matrix products, arithmetic and copies ran while one was open for 0% of the time, Pallas kernels for 7%

profile of v7, /device:TPU:1, one launch (start us, length us, event | category | flops | bytes accessed | tf_op | source)
XLA Modules:
  0.0 223.2 jit_solution(15361940880915136799)
XLA Ops:
  7.2 0.0 reduce-scatter.2.cloned.1.call-start
  7.2 6.5 %assemble_kernel.1 = (f32[1344,128]{1,0:T(8,128)}, f32[1288,128]{1,0:T(8,128)}, f32[2048,128]{1,0:T(8,128)}, f32[64,1024]{1,0:T(8,128)}, f32[8,128]{1,0:T(8,128)}, /*index=5*/f32[8,1024]{1,0:T(8,128)}) custom-call(bf16[7,480]{1,0:T(8,128)(2,1)} %lj_ref.1, bf16[480,512]{1,0:T(8,128)(2,1)} %gj_ref.1, s32[4,480]{1,0:T(4,128)} %ci_ref.1, bf16[4,480]{1,0:T(4,128)(2,1)} %cw_ref.1, ...), custom_call_target="tpu_custom_call" | custom-call | flops 2000000000 | bytes 4000000 | tf_op jit(solution)/shard_map/assemble_kernel/pallas_call | solution.py:508
  13.7 0.0 reduce-scatter.2.cloned.1.call-update
  13.7 10.3 %all-to-all-start = ((f32[8,168,128]{2,1,0:T(8,128)}), f32[8,168,128]{2,1,0:T(8,128)S(1)}, u32[]{:S(2)}, u32[]{:S(2)}) async-start(f32[8,168,128]{2,1,0:T(8,128)} %bitcast.3), calls=%async_computation | async-start | bytes 1376256 | tf_op jit(solution)/shard_map/all_to_all | solution.py:482
  24.1 0.0 copy-start.5
  24.1 0.1 pad.4.clone
  24.2 11.2 %all-to-all-done = f32[8,168,128]{2,1,0:T(8,128)S(1)} async-done(((f32[8,168,128]{2,1,0:T(8,128)}), f32[8,168,128]{2,1,0:T(8,128)S(1)}, u32[]{:S(2)}, u32[]{:S(2)}) %all-to-all-start) | async-done | bytes 688160 | tf_op jit(solution)/shard_map/all_to_all | solution.py:482
  35.4 0.0 copy-done.5
  35.4 0.3 maximum_maximum_fusion
  35.7 19.7 %all_to_all.53 = f32[4,384,128]{2,1,0:T(8,128)S(1)} all-to-all(f32[4,384,128]{2,1,0:T(8,128)S(1)} %bitcast.12), channel_id=1, replica_groups=mesh['y'=4,'core'=2,'x'=4,'z'=16] {'x'}, dimensions={0} | all-to-all | bytes 1572864 | tf_op jit(solution)/shard_map/all_to_all | solution.py:482
  55.4 0.0 reduce-scatter.2.cloned.1.call-done
  55.4 1.0 pad_maximum_fusion
  56.4 32.6 %all_to_all.54 = f32[16,56,128]{2,1,0:T(8,128)S(1)} all-to-all(f32[16,56,128]{2,1,0:T(8,128)S(1)} %bitcast.13), channel_id=1, replica_groups=mesh['y'=4,'core'=2,'x'=4,'z'=16] {'z'}, dimensions={0} | all-to-all | bytes 917504 | tf_op jit(solution)/shard_map/all_to_all | solution.py:482
  89.0 32.3 %all_to_all.55 = f32[16,56,128]{2,1,0:T(8,128)S(1)} all-to-all(f32[16,56,128]{2,1,0:T(8,128)S(1)} %broadcast_in_dim.28), channel_id=1, replica_groups=mesh['y'=4,'core'=2,'x'=4,'z'=16] {'z'}, dimensions={0} | all-to-all | bytes 917504 | tf_op jit(solution)/shard_map/all_to_all | solution.py:488
  121.4 10.7 %all_gather.6.main_ref = f32[1536,128]{1,0:T(8,128)S(1)} all-gather(f32[384,128]{1,0:T(8,128)S(1)} %slice.20), channel_id=1, replica_groups=mesh['y'=4,'core'=2,'x'=4,'z'=16] {'x'}, dimensions={0}, use_global_device_ids=true | all-gather | bytes 983040 | tf_op jit(solution)/shard_map/all_gather | solution.py:541
  132.1 1.0 broadcast_in_dim.29
  133.2 0.0 copy-start.3
  133.2 3.6 %all-to-all-start.4 = ((f32[4,512,128]{2,1,0:T(8,128)}), f32[4,512,128]{2,1,0:T(8,128)S(1)}, u32[]{:S(2)}, u32[]{:S(2)}) async-start(f32[4,512,128]{2,1,0:T(8,128)} %broadcast_in_dim.29), calls=%async_computation.5 | async-start | bytes 2097152 | tf_op jit(solution)/shard_map/all_to_all | solution.py:488
  136.8 0.0 copy-done.3
  136.8 15.8 %regional_kernel.1 = (f32[512,512]{1,0:T(8,128)S(1)}, f32[512,128]{1,0:T(8,128)S(1)}) custom-call(f32[1536,128]{1,0:T(8,128)S(1)} %all_gather.6.main_ref, f32[8,1024]{1,0:T(8,128)S(1)} %copy-done.3), custom_call_target="tpu_custom_call" | custom-call | flops 20000000000 | bytes 4000000 | tf_op jit(solution)/shard_map/regional_kernel/pallas_call | solution.py:544
  152.7 0.0 all-to-all-done.4
  152.7 3.3 %coupling_kernel.1 = (f32[1344,128]{1,0:T(8,128)S(1)}, f32[512,512]{1,0:T(8,128)S(1)}, f32[512,128]{1,0:T(8,128)S(1)}) custom-call(f32[1536,128]{1,0:T(8,128)S(1)} %all_gather.6.main_ref, f32[2048,128]{1,0:T(8,128)S(1)} %bitcast.10, f32[512,512]{1,0:T(8,128)S(1)} %get-tuple-element.25.lower_ref.flower_ref, f32[512,128]{1,0:T(8,128)S(1)} %get-tuple-element.26.pivot_ref), custom_call_target="tpu_custom_call" | custom-call | flops 4000000000 | bytes 4000000 | tf_op jit(solution)/shard_map/coupling_kernel/pallas_call | solution.py:551
  156.0 0.0 copy-start
  156.0 1.0 copy-done
  157.0 24.9 %all_to_all.56 = f32[8,168,128]{2,1,0:T(8,128)} all-to-all(f32[8,168,128]{2,1,0:T(8,128)S(1)} %bitcast.11), channel_id=1, replica_groups=mesh['y'=4,'core'=2,'x'=4,'z'=16] {'y','core'}, dimensions={0} | all-to-all | bytes 1376256 | tf_op jit(solution)/shard_map/all_to_all | solution.py:482
  181.8 0.0 copy-start.1
  181.8 1.2 reduce_sum.39
  183.1 0.0 copy-start.2
  183.1 14.3 %all_gather.7.g_ref = f32[1280,128]{1,0:T(8,128)S(1)} all-gather(f32[160,128]{1,0:T(8,128)S(1)} %slice_subtract_fusion), channel_id=1, replica_groups=mesh['y'=4,'core'=2,'x'=4,'z'=16] {'y','core'}, dimensions={0}, use_global_device_ids=true | all-gather | bytes 737280 | tf_op jit(solution)/shard_map/all_gather | solution.py:567
  197.4 0.0 copy-start.4
  197.4 0.0 copy-done.1
  197.4 0.0 copy-done.2
  197.4 0.7 copy-done.4
  198.1 18.2 %finish_kernel.1 = (f32[7,8]{1,0:T(8,128)}, f32[1,512]{1,0:T(1,128)}, f32[1,512]{1,0:T(1,128)}) custom-call(f32[1280,128]{1,0:T(8,128)S(1)} %all_gather.7.g_ref, f32[8,128]{1,0:T(8,128)S(1)} %slice.23.v_ref, f32[1536,128]{1,0:T(8,128)S(1)} %all_gather.6.main_ref, f32[8,1024]{1,0:T(8,128)S(1)} %copy-done.3, ...), custom_call_target="tpu_custom_call" | custom-call | flops 20000000000 | bytes 4000000 | tf_op jit(solution)/shard_map/finish_kernel/pallas_call | solution.py:568
  (9 shorter events, 0.2 us)
Async XLA Ops:
  7.2 48.2 %reduce-scatter.2.cloned.1.call-start = ((), (), s32[]{:S(2)}) async-start(), calls=%async_computation.7 | async-start | bytes 1310720 | tf_op jit(solution)/shard_map/reduce_scatter | solution.py:536
  13.7 21.6 %all-to-all-start = ((f32[8,168,128]{2,1,0:T(8,128)}), f32[8,168,128]{2,1,0:T(8,128)S(1)}, u32[]{:S(2)}, u32[]{:S(2)}) async-start(f32[8,168,128]{2,1,0:T(8,128)} %bitcast.3), calls=%async_computation | async-start | bytes 1376256 | tf_op jit(solution)/shard_map/all_to_all | solution.py:482
  24.1 11.3 %copy-start.5 = (f32[1288,128]{1,0:T(8,128)S(1)}, f32[1288,128]{1,0:T(8,128)}, u32[]{:S(2)}) copy-start(f32[1288,128]{1,0:T(8,128)} %get-tuple-element.19) | copy-start | bytes 1978372
  133.2 3.7 %copy-start.3 = (f32[8,1024]{1,0:T(8,128)S(1)}, f32[8,1024]{1,0:T(8,128)}, u32[]{:S(2)}) copy-start(f32[8,1024]{1,0:T(8,128)} %get-tuple-element.24.prior_ref) | copy-start | bytes 98308
  133.2 19.5 %all-to-all-start.4 = ((f32[4,512,128]{2,1,0:T(8,128)}), f32[4,512,128]{2,1,0:T(8,128)S(1)}, u32[]{:S(2)}, u32[]{:S(2)}) async-start(f32[4,512,128]{2,1,0:T(8,128)} %broadcast_in_dim.29), calls=%async_computation.5 | async-start | bytes 2097152 | tf_op jit(solution)/shard_map/all_to_all | solution.py:488
  156.0 1.0 copy-start
  181.8 15.6 %copy-start.1 = (f32[512,512]{1,0:T(8,128)S(1)}, f32[512,512]{1,0:T(8,128)}, u32[]{:S(2)}) copy-start(f32[512,512]{1,0:T(8,128)} %copy-done) | copy-start | bytes 3145732
  183.1 14.3 %copy-start.2 = (f32[64,1024]{1,0:T(8,128)S(1)}, f32[64,1024]{1,0:T(8,128)}, u32[]{:S(2)}) copy-start(f32[64,1024]{1,0:T(8,128)} %get-tuple-element.30.red_ref) | copy-start | bytes 786436
  197.4 0.7 copy-start.4
Sparse Core Ops, SparseCore 0:
  13.9 40.3 reduce-scatter.1

commit v8 on v7

--- a/solution.py
+++ b/solution.py
@@ -176,9 +176,9 @@
     reduced = forward_small(factor, [coupling[8 * a : 8 * a + 8] for a in range(nparams)])
     joint = jnp.concatenate(reduced + [jnp.zeros((8, 2 * width), f32)], axis=0)
     red_ref[...] = joint
-    r0, r1, r2 = pieces(joint)
+    r0, r1 = halves(joint)
     base = 2 * rows
-    for at, (one, two) in enumerate(((r0, r0), (r0, r1), (r1, r0), (r1, r1), (r0, r2), (r2, r0))):
+    for at, (one, two) in enumerate(((r0, r0), (r0, r1), (r1, r0))):
         left[base + at * RPAD : base + (at + 1) * RPAD, :] = -one
         right[base + at * RPAD : base + (at + 1) * RPAD, :] = two
 
@@ -504,7 +504,7 @@
     rows = residual.shape[0]
     nparams = local_jac.shape[0]
     width = global_jac.shape[1]
-    stack = 2 * rows + 6 * RPAD
+    stack = 2 * rows + 3 * RPAD
     gg, main, rg, red, aux, prior = call(
         assemble_kernel,
         [

time: 224 us -> 223 us (level)
  no operation moved by 1% of the time
where the time goes in v8:
time: 223 us
  blocking collectives  135 us (61%)
  Pallas kernels  43.3 us (19%)
  between operations  14.1 us (6%)
  starting transfers between devices  14 us (6%)
  waiting for transfers between devices  11.2 us (5%)
  local copies, waits for them, and re-layouts  2.86 us (1%)
  other arithmetic  2.6 us (1%)
    all_to_all x3, blocking collectives, part_sums(): moved = lax.all_to_all(value, axis, 0, 0, tiled=True)  77.3 us
    all_to_all x1, blocking collectives, copies_back(): return lax.all_to_all(copies, axis, 0, 0, tiled=True)  32.3 us
    pallas_call x1, Pallas kernels, body(): call(finish_kernel, [shape(nparams, 8), shape(1, width), shape(1, width)]...  18.2 us
    pallas_call x1, Pallas kernels, body(): call(regional_kernel, [shape(width, width), shape(width, NB)], [pltpu.VME...  15.8 us
    all_gather x1, blocking collectives, body(): matrix = lax.all_gather(mine, GROUPS, axis=0, tiled=True)  14.3 us
    all_to_all x1, waiting for transfers between devices, part_sums(): moved = lax.all_to_all(value, axis, 0, 0, tiled=True)  11.2 us
    all_gather x1, blocking collectives, body(): main = lax.all_gather(both[:MAIN_ROWS // nx], 'x', axis=0, tiled=True)  10.7 us
    all_to_all x1, starting transfers between devices, part_sums(): moved = lax.all_to_all(value, axis, 0, 0, tiled=True)  10.3 us
  transfers between devices with their start and end apart: 3, of which 1 were waited for; matrix products, arithmetic and copies ran while one was open for 0% of the time, Pallas kernels for 7%

profile of v8, /device:TPU:1, one launch (start us, length us, event | category | flops | bytes accessed | tf_op | source)
XLA Modules:
  0.0 222.8 jit_solution(1998676295406036494)
XLA Ops:
  7.2 0.0 reduce-scatter.2.cloned.1.call-start
  7.2 5.9 %assemble_kernel.1 = (f32[1344,128]{1,0:T(8,128)}, f32[1288,128]{1,0:T(8,128)}, f32[2048,128]{1,0:T(8,128)}, f32[64,1024]{1,0:T(8,128)}, f32[8,128]{1,0:T(8,128)}, /*index=5*/f32[8,1024]{1,0:T(8,128)}) custom-call(bf16[7,480]{1,0:T(8,128)(2,1)} %lj_ref.1, bf16[480,512]{1,0:T(8,128)(2,1)} %gj_ref.1, s32[4,480]{1,0:T(4,128)} %ci_ref.1, bf16[4,480]{1,0:T(4,128)(2,1)} %cw_ref.1, ...), custom_call_target="tpu_custom_call" | custom-call | flops 2000000000 | bytes 4000000 | tf_op jit(solution)/shard_map/assemble_kernel/pallas_call | solution.py:508
  13.1 0.0 reduce-scatter.2.cloned.1.call-update
  13.1 10.3 %all-to-all-start = ((f32[8,168,128]{2,1,0:T(8,128)}), f32[8,168,128]{2,1,0:T(8,128)S(1)}, u32[]{:S(2)}, u32[]{:S(2)}) async-start(f32[8,168,128]{2,1,0:T(8,128)} %bitcast.3), calls=%async_computation | async-start | bytes 1376256 | tf_op jit(solution)/shard_map/all_to_all | solution.py:482
  23.5 0.0 copy-start.5
  23.5 0.1 pad.4.clone
  23.6 11.2 %all-to-all-done = f32[8,168,128]{2,1,0:T(8,128)S(1)} async-done(((f32[8,168,128]{2,1,0:T(8,128)}), f32[8,168,128]{2,1,0:T(8,128)S(1)}, u32[]{:S(2)}, u32[]{:S(2)}) %all-to-all-start) | async-done | bytes 688160 | tf_op jit(solution)/shard_map/all_to_all | solution.py:482
  34.8 0.0 copy-done.5
  34.8 0.3 maximum_maximum_fusion
  35.1 19.7 %all_to_all.53 = f32[4,384,128]{2,1,0:T(8,128)S(1)} all-to-all(f32[4,384,128]{2,1,0:T(8,128)S(1)} %bitcast.12), channel_id=1, replica_groups=mesh['y'=4,'core'=2,'x'=4,'z'=16] {'x'}, dimensions={0} | all-to-all | bytes 1572864 | tf_op jit(solution)/shard_map/all_to_all | solution.py:482
  54.8 0.0 reduce-scatter.2.cloned.1.call-done
  54.8 1.0 pad_maximum_fusion
  55.8 32.6 %all_to_all.54 = f32[16,56,128]{2,1,0:T(8,128)S(1)} all-to-all(f32[16,56,128]{2,1,0:T(8,128)S(1)} %bitcast.13), channel_id=1, replica_groups=mesh['y'=4,'core'=2,'x'=4,'z'=16] {'z'}, dimensions={0} | all-to-all | bytes 917504 | tf_op jit(solution)/shard_map/all_to_all | solution.py:482
  88.4 32.3 %all_to_all.55 = f32[16,56,128]{2,1,0:T(8,128)S(1)} all-to-all(f32[16,56,128]{2,1,0:T(8,128)S(1)} %broadcast_in_dim.28), channel_id=1, replica_groups=mesh['y'=4,'core'=2,'x'=4,'z'=16] {'z'}, dimensions={0} | all-to-all | bytes 917504 | tf_op jit(solution)/shard_map/all_to_all | solution.py:488
  120.8 10.7 %all_gather.6.main_ref = f32[1536,128]{1,0:T(8,128)S(1)} all-gather(f32[384,128]{1,0:T(8,128)S(1)} %slice.20), channel_id=1, replica_groups=mesh['y'=4,'core'=2,'x'=4,'z'=16] {'x'}, dimensions={0}, use_global_device_ids=true | all-gather | bytes 983040 | tf_op jit(solution)/shard_map/all_gather | solution.py:541
  131.5 1.0 broadcast_in_dim.29
  132.6 0.0 copy-start.3
  132.6 3.6 %all-to-all-start.4 = ((f32[4,512,128]{2,1,0:T(8,128)}), f32[4,512,128]{2,1,0:T(8,128)S(1)}, u32[]{:S(2)}, u32[]{:S(2)}) async-start(f32[4,512,128]{2,1,0:T(8,128)} %broadcast_in_dim.29), calls=%async_computation.5 | async-start | bytes 2097152 | tf_op jit(solution)/shard_map/all_to_all | solution.py:488
  136.2 0.0 copy-done.3
  136.2 15.8 %regional_kernel.1 = (f32[512,512]{1,0:T(8,128)S(1)}, f32[512,128]{1,0:T(8,128)S(1)}) custom-call(f32[1536,128]{1,0:T(8,128)S(1)} %all_gather.6.main_ref, f32[8,1024]{1,0:T(8,128)S(1)} %copy-done.3), custom_call_target="tpu_custom_call" | custom-call | flops 20000000000 | bytes 4000000 | tf_op jit(solution)/shard_map/regional_kernel/pallas_call | solution.py:544
  152.1 0.0 all-to-all-done.4
  152.1 3.3 %coupling_kernel.1 = (f32[1344,128]{1,0:T(8,128)S(1)}, f32[512,512]{1,0:T(8,128)S(1)}, f32[512,128]{1,0:T(8,128)S(1)}) custom-call(f32[1536,128]{1,0:T(8,128)S(1)} %all_gather.6.main_ref, f32[2048,128]{1,0:T(8,128)S(1)} %bitcast.10, f32[512,512]{1,0:T(8,128)S(1)} %get-tuple-element.25.lower_ref.flower_ref, f32[512,128]{1,0:T(8,128)S(1)} %get-tuple-element.26.pivot_ref), custom_call_target="tpu_custom_call" | custom-call | flops 4000000000 | bytes 4000000 | tf_op jit(solution)/shard_map/coupling_kernel/pallas_call | solution.py:551
  155.4 0.0 copy-start
  155.4 1.0 copy-done
  156.4 25.1 %all_to_all.56 = f32[8,168,128]{2,1,0:T(8,128)} all-to-all(f32[8,168,128]{2,1,0:T(8,128)S(1)} %bitcast.11), channel_id=1, replica_groups=mesh['y'=4,'core'=2,'x'=4,'z'=16] {'y','core'}, dimensions={0} | all-to-all | bytes 1376256 | tf_op jit(solution)/shard_map/all_to_all | solution.py:482
  181.4 0.0 copy-start.1
  181.4 1.2 reduce_sum.39
  182.7 0.0 copy-start.2
  182.7 14.3 %all_gather.7.g_ref = f32[1280,128]{1,0:T(8,128)S(1)} all-gather(f32[160,128]{1,0:T(8,128)S(1)} %slice_subtract_fusion), channel_id=1, replica_groups=mesh['y'=4,'core'=2,'x'=4,'z'=16] {'y','core'}, dimensions={0}, use_global_device_ids=true | all-gather | bytes 737280 | tf_op jit(solution)/shard_map/all_gather | solution.py:567
  197.0 0.0 copy-start.4
  197.0 0.0 copy-done.1
  197.0 0.0 copy-done.2
  197.0 0.7 copy-done.4
  197.7 18.2 %finish_kernel.1 = (f32[7,8]{1,0:T(8,128)}, f32[1,512]{1,0:T(1,128)}, f32[1,512]{1,0:T(1,128)}) custom-call(f32[1280,128]{1,0:T(8,128)S(1)} %all_gather.7.g_ref, f32[8,128]{1,0:T(8,128)S(1)} %slice.23.v_ref, f32[1536,128]{1,0:T(8,128)S(1)} %all_gather.6.main_ref, f32[8,1024]{1,0:T(8,128)S(1)} %copy-done.3, ...), custom_call_target="tpu_custom_call" | custom-call | flops 20000000000 | bytes 4000000 | tf_op jit(solution)/shard_map/finish_kernel/pallas_call | solution.py:568
  (9 shorter events, 0.2 us)
Async XLA Ops:
  7.2 47.6 %reduce-scatter.2.cloned.1.call-start = ((), (), s32[]{:S(2)}) async-start(), calls=%async_computation.7 | async-start | bytes 1310720 | tf_op jit(solution)/shard_map/reduce_scatter | solution.py:536
  13.1 21.6 %all-to-all-start = ((f32[8,168,128]{2,1,0:T(8,128)}), f32[8,168,128]{2,1,0:T(8,128)S(1)}, u32[]{:S(2)}, u32[]{:S(2)}) async-start(f32[8,168,128]{2,1,0:T(8,128)} %bitcast.3), calls=%async_computation | async-start | bytes 1376256 | tf_op jit(solution)/shard_map/all_to_all | solution.py:482
  23.5 11.3 %copy-start.5 = (f32[1288,128]{1,0:T(8,128)S(1)}, f32[1288,128]{1,0:T(8,128)}, u32[]{:S(2)}) copy-start(f32[1288,128]{1,0:T(8,128)} %get-tuple-element.19) | copy-start | bytes 1978372
  132.6 3.7 %copy-start.3 = (f32[8,1024]{1,0:T(8,128)S(1)}, f32[8,1024]{1,0:T(8,128)}, u32[]{:S(2)}) copy-start(f32[8,1024]{1,0:T(8,128)} %get-tuple-element.24.prior_ref) | copy-start | bytes 98308
  132.6 19.5 %all-to-all-start.4 = ((f32[4,512,128]{2,1,0:T(8,128)}), f32[4,512,128]{2,1,0:T(8,128)S(1)}, u32[]{:S(2)}, u32[]{:S(2)}) async-start(f32[4,512,128]{2,1,0:T(8,128)} %broadcast_in_dim.29), calls=%async_computation.5 | async-start | bytes 2097152 | tf_op jit(solution)/shard_map/all_to_all | solution.py:488
  155.4 1.0 copy-start
  181.4 15.6 %copy-start.1 = (f32[512,512]{1,0:T(8,128)S(1)}, f32[512,512]{1,0:T(8,128)}, u32[]{:S(2)}) copy-start(f32[512,512]{1,0:T(8,128)} %copy-done) | copy-start | bytes 3145732
  182.7 14.3 %copy-start.2 = (f32[64,1024]{1,0:T(8,128)S(1)}, f32[64,1024]{1,0:T(8,128)}, u32[]{:S(2)}) copy-start(f32[64,1024]{1,0:T(8,128)} %get-tuple-element.30.red_ref) | copy-start | bytes 786436
  197.0 0.7 copy-start.4
Sparse Core Ops, SparseCore 0:
  13.3 40.3 reduce-scatter.1
